TPU v7x, 32 devices: a whole 2x2x4 slice. The times are simulated.
32 devices in a mesh: blk: 8 (over z, y), rep: 4 (over x, core).
Axes of the slice: x: 2, y: 2, z: 4, core: 2. Of those that a mesh axis runs over, the one named last changes fastest.
Arguments:
- tile_vals: bfloat16 [8, 8, 20, 128, 128], P('blk', 'rep'), may hold values from -4 to 4
- tile_coords: int32 [8, 8, 20, 2], P('blk', 'rep'), may hold values from 0 to 3
- tile_live: int32 [8, 8, 20], P('blk', 'rep'), may hold values from 0 to 1, as said below
- features: bfloat16 [4096, 256], P('blk'), may hold values from -6 to 6
- degree: int32 [4096], P(('blk', 'rep')), may hold values from 512 to 8192
- w_self: bfloat16 [256, 256], replicated, may hold values from -0.375 to 0.375
- w_neigh: bfloat16 [256, 256], replicated, may hold values from -0.375 to 0.375
- cotangent: bfloat16 [4096, 256], P(('blk', 'rep')), may hold values from -6 to 6
Outputs:
- hidden: bfloat16 [4096, 256], P(('blk', 'rep'))
- grad_features: bfloat16 [4096, 256], P(('blk', 'rep'))
- grad_self: float32 [256, 256], replicated
- grad_neigh: float32 [256, 256], replicated
Inputs may be any that keep to these rules, and one draw needn't show every extreme that they name: `tile_coords`: entry 0 names a tile row block of the row partition, entry 1 a tile column block of the column partition; tiles with equal coordinates add. `tile_live`: 1 marks a present tile, 0 a padding tile; the share of present tiles differs between row partitions.
All inputs are finite; a program needn't handle non-finite values.
Results may differ from a plain program's by a relative error of at most 0.012.
Values may be sent and summed in bfloat16 or wider, within the bound.
No kernel may reach another device: no remote copies, remote signals or barrier semaphores. Data moves between devices by JAX's collectives and lax.ppermute only.
A program may use at most 64 MiB of HBM per device.

v0:
```python
import math

import jax
import jax.numpy as jnp
from jax import lax
from jax.sharding import PartitionSpec as P


def from_behind(value, axis, steps):
    count = lax.axis_size(axis)
    pairs = [(source, (source + steps) % count) for source in range(count)]
    return lax.ppermute(value, axis, pairs)


def on_device(tile_vals, tile_coords, tile_live, features, degree, w_self, w_neigh, cotangent):
    part_total = lax.axis_size("blk")
    rep_count = lax.axis_size("rep")
    rep_id = lax.axis_index("rep")
    step_count = tile_vals.shape[1]
    offset_count = step_count * rep_count
    half_span = offset_count // 2
    tile_size = tile_vals.shape[3]
    row_count, feature_dim = features.shape
    block_count = row_count // tile_size
    share_rows = row_count // rep_count
    live_flags = tile_live[0].astype(jnp.bfloat16)
    masked = tile_vals[0] * live_flags[:, :, None, None]
    row_ids = tile_coords[0, :, :, 0]
    col_ids = tile_coords[0, :, :, 1]

    def forward_term(slot_idx, panel_now):
        blocked = panel_now.reshape(block_count, tile_size, feature_dim)
        sources = blocked[col_ids[slot_idx]]
        products = jnp.einsum(
            "krc,kcd->krd", masked[slot_idx], sources, preferred_element_type=jnp.float32
        )
        placed = (
            jnp.zeros((block_count, tile_size, feature_dim), jnp.float32)
            .at[row_ids[slot_idx]]
            .add(products)
        )
        return placed.reshape(row_count, feature_dim)

    panel_now = from_behind(features, "blk", half_span)
    slots = [features for slot_idx in range(step_count)]
    for offset_idx in range(offset_count):
        slot_idx = offset_idx % step_count
        slots[slot_idx] = jnp.where(rep_id == offset_idx // step_count, panel_now, slots[slot_idx])
        if offset_idx + 1 < offset_count:
            panel_now = from_behind(panel_now, "blk", -1)
    summed = forward_term(0, slots[0])
    slot_idx = 1
    summed = summed + forward_term(slot_idx, slots[slot_idx])
    shared = lax.psum_scatter(summed, "rep", scatter_dimension=0, tiled=True)
    root_deg = jnp.sqrt(degree.astype(jnp.float32))[:, None]
    aggregate = (shared / root_deg).astype(jnp.bfloat16)
    own_rows = lax.dynamic_slice_in_dim(features, rep_id * share_rows, share_rows, 0)
    preact = jnp.dot(own_rows, w_self, preferred_element_type=jnp.float32) + jnp.dot(
        aggregate, w_neigh, preferred_element_type=jnp.float32
    )
    sigmoid_pre = jax.nn.sigmoid(preact)
    hidden = (preact * sigmoid_pre).astype(jnp.bfloat16)
    silu_slope = sigmoid_pre * (1.0 + preact * (1.0 - sigmoid_pre))
    grad_pre = (cotangent.astype(jnp.float32) * silu_slope).astype(jnp.bfloat16)
    local_self = jnp.einsum("nd,ne->de", own_rows, grad_pre, preferred_element_type=jnp.float32)
    local_neigh = jnp.einsum("nd,ne->de", aggregate, grad_pre, preferred_element_type=jnp.float32)
    total_self, total_neigh = lax.psum((local_self, local_neigh), ("blk", "rep"))
    grad_scale = 1.0 / math.sqrt(row_count * part_total)
    back_proj = (
        jnp.einsum("ne,de->nd", grad_pre, w_neigh, preferred_element_type=jnp.float32) / root_deg
    ).astype(jnp.bfloat16)
    full_back = lax.all_gather(back_proj, "rep", axis=0, tiled=True)
    back_blocks = full_back.reshape(block_count, tile_size, feature_dim)

    def backward_term(slot_idx):
        sources = back_blocks[row_ids[slot_idx]]
        products = jnp.einsum(
            "krc,krd->kcd", masked[slot_idx], sources, preferred_element_type=jnp.float32
        )
        placed = (
            jnp.zeros((block_count, tile_size, feature_dim), jnp.float32)
            .at[col_ids[slot_idx]]
            .add(products)
        )
        return placed.reshape(row_count, feature_dim)

    terms = [backward_term(slot_idx) for slot_idx in range(step_count)]
    carried = jnp.zeros((row_count, feature_dim), jnp.float32)
    for offset_idx in range(offset_count):
        mine = rep_id == offset_idx // step_count
        carried = carried + jnp.where(mine, terms[offset_idx % step_count], 0.0)
        if offset_idx + 1 < offset_count:
            carried = from_behind(carried.astype(jnp.bfloat16), "blk", -1).astype(carried.dtype)
    carried = from_behind(carried.astype(jnp.bfloat16), "blk", offset_count - 1 - half_span).astype(
        carried.dtype
    )
    neighbour = lax.psum_scatter(
        carried.astype(jnp.bfloat16), "rep", scatter_dimension=0, tiled=True
    ).astype(jnp.float32)
    own_term = jnp.einsum("ne,de->nd", grad_pre, w_self, preferred_element_type=jnp.float32)
    grad_features = (own_term + neighbour).astype(jnp.bfloat16)
    return (hidden, grad_features, total_self * grad_scale, total_neigh * grad_scale)


def solution(mesh):
    return jax.shard_map(
        on_device,
        mesh=mesh,
        in_specs=(
            P("blk", "rep", None, None, None),
            P("blk", "rep", None, None),
            P("blk", "rep", None),
            P("blk", None),
            P(("blk", "rep")),
            P(),
            P(),
            P(("blk", "rep"), None),
        ),
        out_specs=(P(("blk", "rep"), None), P(("blk", "rep"), None), P(), P()),
        check_vma=False,
    )
```

profile of v0, /device:TPU:0, one launch (start us, length us, event | category | flops | bytes accessed | tf_op | source)
XLA Modules:
  0.0 379.4 jit_solution(11539721537776812333)
XLA Ops:
  7.2 4.1 %collective-permute-start = (bf16[512,256]{1,0:T(8,128)(2,1)}, bf16[512,256]{1,0:T(8,128)(2,1)S(1)}, u32[]{:S(2)}, u32[]{:S(2)}) collective-permute-start(bf16[512,256]{1,0:T(8,128)(2,1)} %param.11), channel_id=1, source_target_pairs={{0,16},{4,20},{8,24},{12,28},{16,0},{20,4},{24,8},{28,12},{1,17},{... | collective-permute-start | bytes 786440 | tf_op jit(solution)/shard_map/ppermute | solution.py:12
  11.3 12.1 %collective-permute-done = bf16[512,256]{1,0:T(8,128)(2,1)S(1)} collective-permute-done((bf16[512,256]{1,0:T(8,128)(2,1)}, bf16[512,256]{1,0:T(8,128)(2,1)S(1)}, u32[]{:S(2)}, u32[]{:S(2)}) %collective-permute-start) | collective-permute-done | bytes 262176 | tf_op jit(solution)/shard_map/ppermute | solution.py:12
  23.5 4.5 %collective-permute-start.1 = (bf16[512,256]{1,0:T(8,128)(2,1)S(1)}, bf16[512,256]{1,0:T(8,128)(2,1)S(1)}, u32[]{:S(2)}, u32[]{:S(2)}) collective-permute-start(bf16[512,256]{1,0:T(8,128)(2,1)S(1)} %collective-permute-done), channel_id=1, source_target_pairs={{0,28},{4,0},{8,4},{12,8},{16,12},{20,16},{24,20},{28,24},{1,29},{... | collective-permute-start | bytes 786440 | tf_op jit(solution)/shard_map/ppermute | solution.py:12
  28.0 5.7 %collective-permute-done.1 = bf16[512,256]{1,0:T(8,128)(2,1)S(1)} collective-permute-done((bf16[512,256]{1,0:T(8,128)(2,1)S(1)}, bf16[512,256]{1,0:T(8,128)(2,1)S(1)}, u32[]{:S(2)}, u32[]{:S(2)}) %collective-permute-start.1) | collective-permute-done | bytes 262176 | tf_op jit(solution)/shard_map/ppermute | solution.py:12
  33.7 5.2 %collective-permute-start.2 = (bf16[512,256]{1,0:T(8,128)(2,1)S(1)}, bf16[512,256]{1,0:T(8,128)(2,1)S(1)}, u32[]{:S(2)}, u32[]{:S(2)}) collective-permute-start(bf16[512,256]{1,0:T(8,128)(2,1)S(1)} %collective-permute-done.1), channel_id=1, source_target_pairs={{0,28},{4,0},{8,4},{12,8},{16,12},{20,16},{24,20},{28,24},{1,29},{... | collective-permute-start | bytes 786440 | tf_op jit(solution)/shard_map/ppermute | solution.py:12
  38.9 4.9 %collective-permute-done.2 = bf16[512,256]{1,0:T(8,128)(2,1)S(1)} collective-permute-done((bf16[512,256]{1,0:T(8,128)(2,1)S(1)}, bf16[512,256]{1,0:T(8,128)(2,1)S(1)}, u32[]{:S(2)}, u32[]{:S(2)}) %collective-permute-start.2) | collective-permute-done | bytes 262176 | tf_op jit(solution)/shard_map/ppermute | solution.py:12
  43.8 5.2 %collective-permute-start.3 = (bf16[512,256]{1,0:T(8,128)(2,1)S(1)}, bf16[512,256]{1,0:T(8,128)(2,1)S(1)}, u32[]{:S(2)}, u32[]{:S(2)}) collective-permute-start(bf16[512,256]{1,0:T(8,128)(2,1)S(1)} %collective-permute-done.2), channel_id=1, source_target_pairs={{0,28},{4,0},{8,4},{12,8},{16,12},{20,16},{24,20},{28,24},{1,29},{... | collective-permute-start | bytes 786440 | tf_op jit(solution)/shard_map/ppermute | solution.py:12
  49.0 4.0 %collective-permute-done.3 = bf16[512,256]{1,0:T(8,128)(2,1)S(1)} collective-permute-done((bf16[512,256]{1,0:T(8,128)(2,1)S(1)}, bf16[512,256]{1,0:T(8,128)(2,1)S(1)}, u32[]{:S(2)}, u32[]{:S(2)}) %collective-permute-start.3) | collective-permute-done | bytes 262176 | tf_op jit(solution)/shard_map/ppermute | solution.py:12
  52.9 5.2 %collective-permute-start.4 = (bf16[512,256]{1,0:T(8,128)(2,1)S(1)}, bf16[512,256]{1,0:T(8,128)(2,1)S(1)}, u32[]{:S(2)}, u32[]{:S(2)}) collective-permute-start(bf16[512,256]{1,0:T(8,128)(2,1)S(1)} %collective-permute-done.3), channel_id=1, source_target_pairs={{0,28},{4,0},{8,4},{12,8},{16,12},{20,16},{24,20},{28,24},{1,29},{... | collective-permute-start | bytes 786440 | tf_op jit(solution)/shard_map/ppermute | solution.py:12
  58.1 3.9 %collective-permute-done.4 = bf16[512,256]{1,0:T(8,128)(2,1)S(1)} collective-permute-done((bf16[512,256]{1,0:T(8,128)(2,1)S(1)}, bf16[512,256]{1,0:T(8,128)(2,1)S(1)}, u32[]{:S(2)}, u32[]{:S(2)}) %collective-permute-start.4) | collective-permute-done | bytes 262176 | tf_op jit(solution)/shard_map/ppermute | solution.py:12
  62.0 5.2 %collective-permute-start.5 = (bf16[512,256]{1,0:T(8,128)(2,1)S(1)}, bf16[512,256]{1,0:T(8,128)(2,1)S(1)}, u32[]{:S(2)}, u32[]{:S(2)}) collective-permute-start(bf16[512,256]{1,0:T(8,128)(2,1)S(1)} %collective-permute-done.4), channel_id=1, source_target_pairs={{0,28},{4,0},{8,4},{12,8},{16,12},{20,16},{24,20},{28,24},{1,29},{... | collective-permute-start | bytes 786440 | tf_op jit(solution)/shard_map/ppermute | solution.py:12
  67.2 1.3 fusion.19
  68.5 2.6 collective-permute-done.5
  71.1 5.2 %collective-permute-start.6 = (bf16[512,256]{1,0:T(8,128)(2,1)S(1)}, bf16[512,256]{1,0:T(8,128)(2,1)S(1)}, u32[]{:S(2)}, u32[]{:S(2)}) collective-permute-start(bf16[512,256]{1,0:T(8,128)(2,1)S(1)} %collective-permute-done.5), channel_id=1, source_target_pairs={{0,28},{4,0},{8,4},{12,8},{16,12},{20,16},{24,20},{28,24},{1,29},{... | collective-permute-start | bytes 786440 | tf_op jit(solution)/shard_map/ppermute | solution.py:12
  76.3 0.7 convert_bitcast_fusion
  77.0 4.0 %collective-permute-done.6 = bf16[512,256]{1,0:T(8,128)(2,1)S(1)} collective-permute-done((bf16[512,256]{1,0:T(8,128)(2,1)S(1)}, bf16[512,256]{1,0:T(8,128)(2,1)S(1)}, u32[]{:S(2)}, u32[]{:S(2)}) %collective-permute-start.6) | collective-permute-done | bytes 262176 | tf_op jit(solution)/shard_map/ppermute | solution.py:12
  80.9 5.2 %collective-permute-start.7 = (bf16[512,256]{1,0:T(8,128)(2,1)S(1)}, bf16[512,256]{1,0:T(8,128)(2,1)S(1)}, u32[]{:S(2)}, u32[]{:S(2)}) collective-permute-start(bf16[512,256]{1,0:T(8,128)(2,1)S(1)} %collective-permute-done.6), channel_id=1, source_target_pairs={{0,28},{4,0},{8,4},{12,8},{16,12},{20,16},{24,20},{28,24},{1,29},{... | collective-permute-start | bytes 786440 | tf_op jit(solution)/shard_map/ppermute | solution.py:12
  86.1 1.5 bitcast_multiply_fusion
  87.6 2.4 collective-permute-done.7
  90.0 0.1 select_select_fusion
  90.1 0.6 gather_fusion.1
  90.8 2.0 fusion.4
  92.8 0.6 gather_fusion
  93.5 2.0 fusion.2
  95.5 5.9 %scatter_fusion.1 = f32[4,128,256]{2,1,0:T(8,128)S(1)} fusion(f32[4,128,256]{2,1,0:T(8,128)S(1)} %broadcast.93.clone.1, s32[20]{0:T(128)S(1)} %copy-done.8, f32[20,128,256]{2,1,0:T(8,128)} %fusion.4), kind=kCustom, calls=%fused_computation.5 | custom fusion | flops 655360 | bytes 7864400 | tf_op jit(solution)/shard_map/scatter-add | solution.py:40
  101.5 5.9 %scatter_fusion = f32[4,128,256]{2,1,0:T(8,128)S(1)} fusion(f32[4,128,256]{2,1,0:T(8,128)S(1)} %broadcast.93.clone, s32[20]{0:T(128)S(1)} %copy-done.7, f32[20,128,256]{2,1,0:T(8,128)} %fusion.2), kind=kCustom, calls=%fused_computation.4 | custom fusion | flops 655360 | bytes 7864400 | tf_op jit(solution)/shard_map/scatter-add | solution.py:40
  107.4 0.9 add.107
  108.4 0.2 fusion.14
  108.6 23.4 %reduce-scatter.3.cloned.1.call-done = f32[128,256]{1,0:T(8,128)} async-done(((f32[512,256]{1,0:T(8,128)}), f32[128,256]{1,0:T(8,128)}) %reduce-scatter.3.cloned.1.call-update) | async-done | bytes 131088 | tf_op jit(solution)/shard_map/reduce_scatter | solution.py:54
  132.0 1.8 multiply_convert_fusion
  133.8 0.2 fusion
  134.0 5.8 %all_gather.3 = bf16[512,256]{1,0:T(8,128)(2,1)S(1)} all-gather(bf16[128,256]{1,0:T(8,128)(2,1)S(1)} %fusion), channel_id=1, replica_groups=mesh['blk'=8,'rep'=4] {'rep'}, dimensions={0}, use_global_device_ids=true | all-gather | bytes 327680 | tf_op jit(solution)/shard_map/all_gather | solution.py:72
  139.8 0.6 gather_fusion.3
  140.4 2.1 fusion.3
  142.5 0.6 gather_fusion.2
  143.1 2.1 fusion.1
  145.3 5.9 %scatter_fusion.2 = f32[4,128,256]{2,1,0:T(8,128)S(1)} fusion(f32[4,128,256]{2,1,0:T(8,128)S(1)} %broadcast.93.clone.3, s32[20]{0:T(128)S(1)} %get-tuple-element.18, f32[20,128,256]{2,1,0:T(8,128)} %fusion.1), kind=kCustom, calls=%fused_computation.6 | custom fusion | flops 655360 | bytes 7864400 | tf_op jit(solution)/shard_map/scatter-add | solution.py:83
  151.2 4.3 %collective-permute-start.8 = (bf16[512,256]{1,0:T(8,128)(2,1)S(1)}, bf16[512,256]{1,0:T(8,128)(2,1)S(1)}, u32[]{:S(2)}, u32[]{:S(2)}) collective-permute-start(bf16[512,256]{1,0:T(8,128)(2,1)S(1)} %bitcast.78), channel_id=1, source_target_pairs={{0,28},{4,0},{8,4},{12,8},{16,12},{20,16},{24,20},{28,24},{1,29},{... | collective-permute-start | bytes 786440 | tf_op jit(solution)/shard_map/ppermute | solution.py:12
  155.5 5.9 %scatter_fusion.3 = f32[4,128,256]{2,1,0:T(8,128)S(1)} fusion(f32[4,128,256]{2,1,0:T(8,128)S(1)} %broadcast.93.clone.2, s32[20]{0:T(128)S(1)} %get-tuple-element.17, f32[20,128,256]{2,1,0:T(8,128)} %fusion.3), kind=kCustom, calls=%fused_computation.7 | custom fusion | flops 655360 | bytes 7864400 | tf_op jit(solution)/shard_map/scatter-add | solution.py:83
  161.4 0.2 broadcast_select_fusion.6
  161.7 5.2 %collective-permute-start.9 = (bf16[512,256]{1,0:T(8,128)(2,1)S(1)}, bf16[512,256]{1,0:T(8,128)(2,1)S(1)}, u32[]{:S(2)}, u32[]{:S(2)}) collective-permute-start(bf16[512,256]{1,0:T(8,128)(2,1)S(1)} %fusion.11), channel_id=1, source_target_pairs={{0,28},{4,0},{8,4},{12,8},{16,12},{20,16},{24,20},{28,24},{1,29},{... | collective-permute-start | bytes 786440 | tf_op jit(solution)/shard_map/ppermute | solution.py:12
  166.8 0.1 broadcast_select_fusion.5
  167.0 5.1 %collective-permute-done.9 = bf16[512,256]{1,0:T(8,128)(2,1)S(1)} collective-permute-done((bf16[512,256]{1,0:T(8,128)(2,1)S(1)}, bf16[512,256]{1,0:T(8,128)(2,1)S(1)}, u32[]{:S(2)}, u32[]{:S(2)}) %collective-permute-start.9) | collective-permute-done | bytes 262176 | tf_op jit(solution)/shard_map/ppermute | solution.py:12
  172.2 5.2 %collective-permute-start.10 = (bf16[512,256]{1,0:T(8,128)(2,1)S(1)}, bf16[512,256]{1,0:T(8,128)(2,1)S(1)}, u32[]{:S(2)}, u32[]{:S(2)}) collective-permute-start(bf16[512,256]{1,0:T(8,128)(2,1)S(1)} %fusion.10), channel_id=1, source_target_pairs={{0,28},{4,0},{8,4},{12,8},{16,12},{20,16},{24,20},{28,24},{1,29},{... | collective-permute-start | bytes 786440 | tf_op jit(solution)/shard_map/ppermute | solution.py:12
  177.4 4.4 %collective-permute-done.10 = bf16[512,256]{1,0:T(8,128)(2,1)S(1)} collective-permute-done((bf16[512,256]{1,0:T(8,128)(2,1)S(1)}, bf16[512,256]{1,0:T(8,128)(2,1)S(1)}, u32[]{:S(2)}, u32[]{:S(2)}) %collective-permute-start.10) | collective-permute-done | bytes 262176 | tf_op jit(solution)/shard_map/ppermute | solution.py:12
  181.8 5.2 %collective-permute-start.11 = (bf16[512,256]{1,0:T(8,128)(2,1)S(1)}, bf16[512,256]{1,0:T(8,128)(2,1)S(1)}, u32[]{:S(2)}, u32[]{:S(2)}) collective-permute-start(bf16[512,256]{1,0:T(8,128)(2,1)S(1)} %fusion.9), channel_id=1, source_target_pairs={{0,28},{4,0},{8,4},{12,8},{16,12},{20,16},{24,20},{28,24},{1,29},{... | collective-permute-start | bytes 786440 | tf_op jit(solution)/shard_map/ppermute | solution.py:12
  187.1 3.9 %collective-permute-done.11 = bf16[512,256]{1,0:T(8,128)(2,1)S(1)} collective-permute-done((bf16[512,256]{1,0:T(8,128)(2,1)S(1)}, bf16[512,256]{1,0:T(8,128)(2,1)S(1)}, u32[]{:S(2)}, u32[]{:S(2)}) %collective-permute-start.11) | collective-permute-done | bytes 262176 | tf_op jit(solution)/shard_map/ppermute | solution.py:12
  191.0 5.2 %collective-permute-start.12 = (bf16[512,256]{1,0:T(8,128)(2,1)S(1)}, bf16[512,256]{1,0:T(8,128)(2,1)S(1)}, u32[]{:S(2)}, u32[]{:S(2)}) collective-permute-start(bf16[512,256]{1,0:T(8,128)(2,1)S(1)} %fusion.8), channel_id=1, source_target_pairs={{0,28},{4,0},{8,4},{12,8},{16,12},{20,16},{24,20},{28,24},{1,29},{... | collective-permute-start | bytes 786440 | tf_op jit(solution)/shard_map/ppermute | solution.py:12
  196.3 3.9 %collective-permute-done.12 = bf16[512,256]{1,0:T(8,128)(2,1)S(1)} collective-permute-done((bf16[512,256]{1,0:T(8,128)(2,1)S(1)}, bf16[512,256]{1,0:T(8,128)(2,1)S(1)}, u32[]{:S(2)}, u32[]{:S(2)}) %collective-permute-start.12) | collective-permute-done | bytes 262176 | tf_op jit(solution)/shard_map/ppermute | solution.py:12
  200.2 5.2 %collective-permute-start.13 = (bf16[512,256]{1,0:T(8,128)(2,1)S(1)}, bf16[512,256]{1,0:T(8,128)(2,1)S(1)}, u32[]{:S(2)}, u32[]{:S(2)}) collective-permute-start(bf16[512,256]{1,0:T(8,128)(2,1)S(1)} %fusion.7), channel_id=1, source_target_pairs={{0,28},{4,0},{8,4},{12,8},{16,12},{20,16},{24,20},{28,24},{1,29},{... | collective-permute-start | bytes 786440 | tf_op jit(solution)/shard_map/ppermute | solution.py:12
  205.4 4.2 %collective-permute-done.13 = bf16[512,256]{1,0:T(8,128)(2,1)S(1)} collective-permute-done((bf16[512,256]{1,0:T(8,128)(2,1)S(1)}, bf16[512,256]{1,0:T(8,128)(2,1)S(1)}, u32[]{:S(2)}, u32[]{:S(2)}) %collective-permute-start.13) | collective-permute-done | bytes 262176 | tf_op jit(solution)/shard_map/ppermute | solution.py:12
  209.7 5.3 %collective-permute-start.14 = (bf16[512,256]{1,0:T(8,128)(2,1)S(1)}, bf16[512,256]{1,0:T(8,128)(2,1)S(1)}, u32[]{:S(2)}, u32[]{:S(2)}) collective-permute-start(bf16[512,256]{1,0:T(8,128)(2,1)S(1)} %fusion.6), channel_id=1, source_target_pairs={{0,28},{4,0},{8,4},{12,8},{16,12},{20,16},{24,20},{28,24},{1,29},{... | collective-permute-start | bytes 786440 | tf_op jit(solution)/shard_map/ppermute | solution.py:12
  214.9 1.0 fusion.22
  215.9 2.9 collective-permute-done.14
  218.9 0.1 collective-permute-start.15
  218.9 0.9 fusion.12
  219.9 10.1 %collective-permute-done.15 = bf16[512,256]{1,0:T(8,128)(2,1)S(1)} collective-permute-done((bf16[512,256]{1,0:T(8,128)(2,1)S(1)}, bf16[512,256]{1,0:T(8,128)(2,1)S(1)}, u32[]{:S(2)}, u32[]{:S(2)}) %collective-permute-start.15) | collective-permute-done | bytes 262176 | tf_op jit(solution)/shard_map/ppermute | solution.py:12
  230.0 0.7 copy-done.6
  230.7 0.2 fusion.23
  230.9 118.9 %all-reduce.3.cloned.1.call-done = (f32[256,256]{1,0:T(8,128)}, f32[256,256]{1,0:T(8,128)}) async-done(((f32[256,256]{1,0:T(8,128)}, f32[256,256]{1,0:T(8,128)}), (f32[256,256]{1,0:T(8,128)}, f32[256,256]{1,0:T(8,128)})) %all-reduce.3.cloned.1.call-update) | async-done | bytes 524304 | tf_op jit(solution)/shard_map/psum | solution.py:67
  349.8 1.7 broadcast_multiply_fusion
  351.5 1.7 broadcast_multiply_fusion.1
  353.2 18.2 %reduce-scatter.5.cloned.1.call-done = bf16[128,256]{1,0:T(8,128)(2,1)} async-done(((bf16[512,256]{1,0:T(8,128)(2,1)}), bf16[128,256]{1,0:T(8,128)(2,1)}) %reduce-scatter.5.cloned.1.call-update) | async-done | bytes 65552 | tf_op jit(solution)/shard_map/reduce_scatter | solution.py:97
  371.4 1.5 add_convert_fusion
  (49 shorter events, 0.8 us)
Async XLA Ops:
  7.2 124.8 %copy-start = (bf16[256,256]{1,0:T(8,128)(2,1)S(1)}, bf16[256,256]{1,0:T(8,128)(2,1)}, u32[]{:S(2)}) copy-start(bf16[256,256]{1,0:T(8,128)(2,1)} %param.14) | copy-start | bytes 393220
  7.2 124.8 %reduce-scatter.3.cloned.1.call-start = ((), (), s32[]{:S(2)}) async-start(), calls=%async_computation.2 | async-start | bytes 655360 | tf_op jit(solution)/shard_map/reduce_scatter | solution.py:54
  7.2 16.2 %collective-permute-start = (bf16[512,256]{1,0:T(8,128)(2,1)}, bf16[512,256]{1,0:T(8,128)(2,1)S(1)}, u32[]{:S(2)}, u32[]{:S(2)}) collective-permute-start(bf16[512,256]{1,0:T(8,128)(2,1)} %param.11), channel_id=1, source_target_pairs={{0,16},{4,20},{8,24},{12,28},{16,0},{20,4},{24,8},{28,12},{1,17},{... | collective-permute-start | bytes 786440 | tf_op jit(solution)/shard_map/ppermute | solution.py:12
  23.5 10.2 %collective-permute-start.1 = (bf16[512,256]{1,0:T(8,128)(2,1)S(1)}, bf16[512,256]{1,0:T(8,128)(2,1)S(1)}, u32[]{:S(2)}, u32[]{:S(2)}) collective-permute-start(bf16[512,256]{1,0:T(8,128)(2,1)S(1)} %collective-permute-done), channel_id=1, source_target_pairs={{0,28},{4,0},{8,4},{12,8},{16,12},{20,16},{24,20},{28,24},{1,29},{... | collective-permute-start | bytes 786440 | tf_op jit(solution)/shard_map/ppermute | solution.py:12
  33.7 10.1 %collective-permute-start.2 = (bf16[512,256]{1,0:T(8,128)(2,1)S(1)}, bf16[512,256]{1,0:T(8,128)(2,1)S(1)}, u32[]{:S(2)}, u32[]{:S(2)}) collective-permute-start(bf16[512,256]{1,0:T(8,128)(2,1)S(1)} %collective-permute-done.1), channel_id=1, source_target_pairs={{0,28},{4,0},{8,4},{12,8},{16,12},{20,16},{24,20},{28,24},{1,29},{... | collective-permute-start | bytes 786440 | tf_op jit(solution)/shard_map/ppermute | solution.py:12
  43.8 9.2 %collective-permute-start.3 = (bf16[512,256]{1,0:T(8,128)(2,1)S(1)}, bf16[512,256]{1,0:T(8,128)(2,1)S(1)}, u32[]{:S(2)}, u32[]{:S(2)}) collective-permute-start(bf16[512,256]{1,0:T(8,128)(2,1)S(1)} %collective-permute-done.2), channel_id=1, source_target_pairs={{0,28},{4,0},{8,4},{12,8},{16,12},{20,16},{24,20},{28,24},{1,29},{... | collective-permute-start | bytes 786440 | tf_op jit(solution)/shard_map/ppermute | solution.py:12
  52.9 9.1 %collective-permute-start.4 = (bf16[512,256]{1,0:T(8,128)(2,1)S(1)}, bf16[512,256]{1,0:T(8,128)(2,1)S(1)}, u32[]{:S(2)}, u32[]{:S(2)}) collective-permute-start(bf16[512,256]{1,0:T(8,128)(2,1)S(1)} %collective-permute-done.3), channel_id=1, source_target_pairs={{0,28},{4,0},{8,4},{12,8},{16,12},{20,16},{24,20},{28,24},{1,29},{... | collective-permute-start | bytes 786440 | tf_op jit(solution)/shard_map/ppermute | solution.py:12
  62.0 9.1 %collective-permute-start.5 = (bf16[512,256]{1,0:T(8,128)(2,1)S(1)}, bf16[512,256]{1,0:T(8,128)(2,1)S(1)}, u32[]{:S(2)}, u32[]{:S(2)}) collective-permute-start(bf16[512,256]{1,0:T(8,128)(2,1)S(1)} %collective-permute-done.4), channel_id=1, source_target_pairs={{0,28},{4,0},{8,4},{12,8},{16,12},{20,16},{24,20},{28,24},{1,29},{... | collective-permute-start | bytes 786440 | tf_op jit(solution)/shard_map/ppermute | solution.py:12
  71.1 9.8 %copy-start.3 = (bf16[512,256]{1,0:T(8,128)(2,1)}, bf16[512,256]{1,0:T(8,128)(2,1)S(1)}, u32[]{:S(2)}) copy-start(bf16[512,256]{1,0:T(8,128)(2,1)S(1)} %collective-permute-done.5) | copy-start | bytes 786436
  71.1 9.8 %collective-permute-start.6 = (bf16[512,256]{1,0:T(8,128)(2,1)S(1)}, bf16[512,256]{1,0:T(8,128)(2,1)S(1)}, u32[]{:S(2)}, u32[]{:S(2)}) collective-permute-start(bf16[512,256]{1,0:T(8,128)(2,1)S(1)} %collective-permute-done.5), channel_id=1, source_target_pairs={{0,28},{4,0},{8,4},{12,8},{16,12},{20,16},{24,20},{28,24},{1,29},{... | collective-permute-start | bytes 786440 | tf_op jit(solution)/shard_map/ppermute | solution.py:12
  76.9 13.0 %copy-start.1 = (bf16[512,256]{1,0:T(8,128)(2,1)S(1)}, bf16[512,256]{1,0:T(8,128)(2,1)}, u32[]{:S(2)}) copy-start(bf16[512,256]{1,0:T(8,128)(2,1)} %param.11) | copy-start | bytes 786436
  80.9 6.7 %copy-start.5 = (bf16[512,256]{1,0:T(8,128)(2,1)}, bf16[512,256]{1,0:T(8,128)(2,1)S(1)}, u32[]{:S(2)}) copy-start(bf16[512,256]{1,0:T(8,128)(2,1)S(1)} %collective-permute-done.6) | copy-start | bytes 786436
  80.9 9.1 %collective-permute-start.7 = (bf16[512,256]{1,0:T(8,128)(2,1)S(1)}, bf16[512,256]{1,0:T(8,128)(2,1)S(1)}, u32[]{:S(2)}, u32[]{:S(2)}) collective-permute-start(bf16[512,256]{1,0:T(8,128)(2,1)S(1)} %collective-permute-done.6), channel_id=1, source_target_pairs={{0,28},{4,0},{8,4},{12,8},{16,12},{20,16},{24,20},{28,24},{1,29},{... | collective-permute-start | bytes 786440 | tf_op jit(solution)/shard_map/ppermute | solution.py:12
  86.1 3.9 %copy-start.4 = (bf16[512,256]{1,0:T(8,128)(2,1)S(1)}, bf16[512,256]{1,0:T(8,128)(2,1)}, u32[]{:S(2)}) copy-start(bf16[512,256]{1,0:T(8,128)(2,1)} %copy-done.3) | copy-start | bytes 786436
  93.5 2.1 copy-start.8
  95.5 5.9 %copy-start.7 = (s32[20]{0:T(128)S(1)}, s32[20]{0:T(128)}, u32[]{:S(2)}) copy-start(s32[20]{0:T(128)} %get-tuple-element.19) | copy-start | bytes 244
  107.3 1.0 copy-start.11
  107.4 1.0 copy-start.2
  107.4 24.6 %copy-start.10 = (bf16[128,256]{1,0:T(8,128)(2,1)S(1)}, bf16[128,256]{1,0:T(8,128)(2,1)}, u32[]{:S(2)}) copy-start(bf16[128,256]{1,0:T(8,128)(2,1)} %param.15) | copy-start | bytes 196612
  108.3 241.6 %all-reduce.3.cloned.1.call-start = ((), (), s32[]{:S(2)}) async-start(), calls=%async_computation.4 | async-start | bytes 1048576 | tf_op jit(solution)/shard_map/psum | solution.py:67
  108.4 25.4 %copy-start.12 = (f32[128]{0:T(128)}, f32[128]{0:T(128)S(1)}, u32[]{:S(2)}) copy-start(f32[128]{0:T(128)S(1)} %convert_sqrt_fusion) | copy-start | bytes 1540
  151.2 10.4 %collective-permute-start.8 = (bf16[512,256]{1,0:T(8,128)(2,1)S(1)}, bf16[512,256]{1,0:T(8,128)(2,1)S(1)}, u32[]{:S(2)}, u32[]{:S(2)}) collective-permute-start(bf16[512,256]{1,0:T(8,128)(2,1)S(1)} %bitcast.78), channel_id=1, source_target_pairs={{0,28},{4,0},{8,4},{12,8},{16,12},{20,16},{24,20},{28,24},{1,29},{... | collective-permute-start | bytes 786440 | tf_op jit(solution)/shard_map/ppermute | solution.py:12
  161.7 10.4 %collective-permute-start.9 = (bf16[512,256]{1,0:T(8,128)(2,1)S(1)}, bf16[512,256]{1,0:T(8,128)(2,1)S(1)}, u32[]{:S(2)}, u32[]{:S(2)}) collective-permute-start(bf16[512,256]{1,0:T(8,128)(2,1)S(1)} %fusion.11), channel_id=1, source_target_pairs={{0,28},{4,0},{8,4},{12,8},{16,12},{20,16},{24,20},{28,24},{1,29},{... | collective-permute-start | bytes 786440 | tf_op jit(solution)/shard_map/ppermute | solution.py:12
  172.2 9.6 %collective-permute-start.10 = (bf16[512,256]{1,0:T(8,128)(2,1)S(1)}, bf16[512,256]{1,0:T(8,128)(2,1)S(1)}, u32[]{:S(2)}, u32[]{:S(2)}) collective-permute-start(bf16[512,256]{1,0:T(8,128)(2,1)S(1)} %fusion.10), channel_id=1, source_target_pairs={{0,28},{4,0},{8,4},{12,8},{16,12},{20,16},{24,20},{28,24},{1,29},{... | collective-permute-start | bytes 786440 | tf_op jit(solution)/shard_map/ppermute | solution.py:12
  181.8 9.1 %collective-permute-start.11 = (bf16[512,256]{1,0:T(8,128)(2,1)S(1)}, bf16[512,256]{1,0:T(8,128)(2,1)S(1)}, u32[]{:S(2)}, u32[]{:S(2)}) collective-permute-start(bf16[512,256]{1,0:T(8,128)(2,1)S(1)} %fusion.9), channel_id=1, source_target_pairs={{0,28},{4,0},{8,4},{12,8},{16,12},{20,16},{24,20},{28,24},{1,29},{... | collective-permute-start | bytes 786440 | tf_op jit(solution)/shard_map/ppermute | solution.py:12
  191.0 23.9 %copy-start.9 = (f32[128,256]{1,0:T(8,128)S(1)}, f32[128,256]{1,0:T(8,128)}, u32[]{:S(2)}) copy-start(f32[128,256]{1,0:T(8,128)} %reduce-scatter.3.cloned.1.call-done) | copy-start | bytes 393220
  191.0 23.9 %copy-start.13 = (f32[128]{0:T(128)S(1)}, f32[128]{0:T(128)}, u32[]{:S(2)}) copy-start(f32[128]{0:T(128)} %copy-done.12) | copy-start | bytes 1540
  191.0 9.1 %collective-permute-start.12 = (bf16[512,256]{1,0:T(8,128)(2,1)S(1)}, bf16[512,256]{1,0:T(8,128)(2,1)S(1)}, u32[]{:S(2)}, u32[]{:S(2)}) collective-permute-start(bf16[512,256]{1,0:T(8,128)(2,1)S(1)} %fusion.8), channel_id=1, source_target_pairs={{0,28},{4,0},{8,4},{12,8},{16,12},{20,16},{24,20},{28,24},{1,29},{... | collective-permute-start | bytes 786440 | tf_op jit(solution)/shard_map/ppermute | solution.py:12
  200.2 9.4 %collective-permute-start.13 = (bf16[512,256]{1,0:T(8,128)(2,1)S(1)}, bf16[512,256]{1,0:T(8,128)(2,1)S(1)}, u32[]{:S(2)}, u32[]{:S(2)}) collective-permute-start(bf16[512,256]{1,0:T(8,128)(2,1)S(1)} %fusion.7), channel_id=1, source_target_pairs={{0,28},{4,0},{8,4},{12,8},{16,12},{20,16},{24,20},{28,24},{1,29},{... | collective-permute-start | bytes 786440 | tf_op jit(solution)/shard_map/ppermute | solution.py:12
  209.7 9.2 %collective-permute-start.14 = (bf16[512,256]{1,0:T(8,128)(2,1)S(1)}, bf16[512,256]{1,0:T(8,128)(2,1)S(1)}, u32[]{:S(2)}, u32[]{:S(2)}) collective-permute-start(bf16[512,256]{1,0:T(8,128)(2,1)S(1)} %fusion.6), channel_id=1, source_target_pairs={{0,28},{4,0},{8,4},{12,8},{16,12},{20,16},{24,20},{28,24},{1,29},{... | collective-permute-start | bytes 786440 | tf_op jit(solution)/shard_map/ppermute | solution.py:12
  218.9 11.1 %collective-permute-start.15 = (bf16[512,256]{1,0:T(8,128)(2,1)S(1)}, bf16[512,256]{1,0:T(8,128)(2,1)S(1)}, u32[]{:S(2)}, u32[]{:S(2)}) collective-permute-start(bf16[512,256]{1,0:T(8,128)(2,1)S(1)} %fusion.5), channel_id=1, source_target_pairs={{0,12},{4,16},{8,20},{12,24},{16,28},{20,0},{24,4},{28,8},{1,13},{... | collective-permute-start | bytes 786440 | tf_op jit(solution)/shard_map/ppermute | solution.py:12
  219.9 151.5 %reduce-scatter.5.cloned.1.call-start = ((), (), s32[]{:S(2)}) async-start(), calls=%async_computation.3 | async-start | bytes 327680 | tf_op jit(solution)/shard_map/reduce_scatter | solution.py:97
  230.0 0.7 copy-start.6
Sparse Core Ops, SparseCore 0:
  108.4 23.5 reduce-scatter.2
  220.0 129.7 all-reduce.2
  352.3 19.0 reduce-scatter.4
where the time goes:
time: 380 us; the launch traced here: 379 us
  waiting for transfers between devices  235 us (62%)
  starting transfers between devices  75.5 us (20%)
  other arithmetic  33.6 us (9%)
  between operations  14.1 us (4%)
  matrix products  12.5 us (3%)
  blocking collectives  5.78 us (2%)
    psum x1, waiting for transfers between devices, on_device(): lax.psum((local_self, local_neigh), ('blk', 'rep'))  119 us
    ppermute x16, starting transfers between devices, from_behind(): return lax.ppermute(value, axis, pairs)  75.4 us
    ppermute x16, waiting for transfers between devices, from_behind(): return lax.ppermute(value, axis, pairs)  74 us
    reduce_scatter x1, waiting for transfers between devices, on_device(): shared = lax.psum_scatter(summed, 'rep', scatter_dimension=0, tiled=True)  23.4 us
    reduce_scatter x1, waiting for transfers between devices, on_device(): lax.psum_scatter(carried.astype(jnp.bfloat16), 'rep', scatter_dimension=0...  18.2 us
    scatter-add x2, other arithmetic, backward_term(): placed = jnp.zeros((block_count, tile_size, feature_dim), jnp.float32).at...  11.7 us
    scatter-add x2, other arithmetic, forward_term(): placed = jnp.zeros((block_count, tile_size, feature_dim), jnp.float32).at...  11.7 us
  transfers between devices with their start and end apart: 19, of which 18 were waited for; matrix products, arithmetic and copies ran while one was open for 4% of the time, Pallas kernels for 0%

commit v1 on v0

v1 whole, which is shorter than its diff:
```python
import math

import jax
import jax.numpy as jnp
from jax import lax
from jax.experimental import pallas as pl
from jax.experimental.pallas import tpu as pltpu
from jax.sharding import PartitionSpec as P

BOTH = ("blk", "rep")
BF16 = jnp.bfloat16
F32 = jnp.float32
VMEM = pl.BlockSpec(memory_space=pltpu.VMEM)
SMEM = pl.BlockSpec(memory_space=pltpu.SMEM)


def exchange(value, target):
    part_total, rep_count = lax.axis_size("blk"), lax.axis_size("rep")
    pairs = []
    for part in range(part_total):
        for rep in range(rep_count):
            to_part, to_rep = target(part, rep)
            pairs.append((part * rep_count + rep, (to_part % part_total) * rep_count + to_rep))
    return lax.ppermute(value, BOTH, pairs)


def dot(lhs, rhs, contract):
    return lax.dot_general(lhs, rhs, (contract, ((), ())), preferred_element_type=F32)


def place_tiles(slot, out_axis, coords, live, tiles, source, total):
    tile_count, size = tiles.shape[-3], tiles.shape[-1]
    spare = total.shape[0] // size - 1
    for k in range(tile_count):
        to = jnp.where(live[0, slot, k] != 0, coords[0, slot, k, out_axis], spare)
        take = coords[0, slot, k, 1 - out_axis]
        tile = tiles[0, slot, k]
        block = source[pl.ds(pl.multiple_of(take * size, size), size), :]
        rows = pl.ds(pl.multiple_of(to * size, size), size)
        total[rows, :] += dot(tile, block, ((1 - out_axis,), (0,)))


def forward_first(coords, live, tiles, low, high, out, source, total):
    half = low.shape[0]
    source[:half, :] = low[...]
    source[half:, :] = high[...]
    total[...] = jnp.zeros_like(total)
    place_tiles(0, 0, coords, live, tiles, source, total)
    out[...] = total[: out.shape[0], :]


def forward_second(coords, live, tiles, low, high, before, keep, send, source, total):
    half = low.shape[0]
    rows = before.shape[0]
    source[:half, :] = low[...]
    source[half:, :] = high[...]
    total[:rows, :] = before[...]
    total[rows:, :] = jnp.zeros((total.shape[0] - rows, total.shape[1]), F32)
    place_tiles(1, 0, coords, live, tiles, source, total)
    core = lax.rem(lax.axis_index("rep"), 2)
    share = rows // 4
    for h in range(2):
        mine = pl.ds(pl.multiple_of((2 * h + core) * share, share), share)
        other = pl.ds(pl.multiple_of((2 * h + 1 - core) * share, share), share)
        keep[h] = total[mine, :]
        send[h] = total[other, :].astype(BF16)


def middle(chip_sum, far_sum, inv_root, self_term, cotangent, w_neigh, agg, hidden, grad_pre, back):
    summed = chip_sum[...] + far_sum[...].astype(F32)
    inv = inv_root[...]
    aggregate = (summed * inv).astype(BF16)
    agg[...] = aggregate
    preact = self_term[...] + dot(aggregate, w_neigh[...], ((1,), (0,)))
    sig = jax.nn.sigmoid(preact)
    hidden[...] = (preact * sig).astype(BF16)
    slope = sig * (1.0 + preact * (1.0 - sig))
    grad = (cotangent[...].astype(F32) * slope).astype(BF16)
    grad_pre[...] = grad
    back[...] = (dot(grad, w_neigh[...], ((1,), (1,))) * inv).astype(BF16)


def backward(coords, live, tiles, own, other, same0, cross0, same1, cross1, source, total):
    rep = lax.axis_index("rep")
    core, plane = lax.rem(rep, 2), lax.div(rep, 2)
    share = own.shape[1]
    for h in range(2):
        source[pl.ds(pl.multiple_of((2 * h + core) * share, share), share), :] = own[h]
        source[pl.ds(pl.multiple_of((2 * h + 1 - core) * share, share), share), :] = other[h]
    half = 2 * share
    for slot, (same, cross) in enumerate(((same0, cross0), (same1, cross1))):
        total[...] = jnp.zeros_like(total)
        place_tiles(slot, 1, coords, live, tiles, source, total)
        same[...] = total[pl.ds(pl.multiple_of(plane * half, half), half), :].astype(BF16)
        cross[...] = total[pl.ds(pl.multiple_of((1 - plane) * half, half), half), :].astype(BF16)


def on_device(tile_vals, tile_coords, tile_live, features, degree, w_self, w_neigh, cotangent):
    part_total = lax.axis_size("blk")
    rep_count = lax.axis_size("rep")
    rep = lax.axis_index("rep")
    core, plane = rep % 2, rep // 2
    slots = tile_vals.shape[1]
    half_span = slots * rep_count // 2
    tile_size = tile_vals.shape[3]
    rows, dim = features.shape
    half, share = rows // 2, rows // rep_count

    def shift(r, j):
        return slots * r + j - half_span

    def flip_core(value):
        return exchange(value, lambda b, r: (b, r ^ 1))

    def flip_plane(value):
        return exchange(value, lambda b, r: (b, r ^ 2))

    low, high = features[:half], features[half:]
    panels = []
    for j in range(slots):
        panels.append(
            (
                exchange(low, lambda b, r: (b - shift(r, j), r)),
                exchange(high, lambda b, r: (b - shift(r ^ 2, j), r ^ 2)),
            )
        )

    cot_far = flip_plane(cotangent)
    deg = degree.astype(F32)
    quarters = features.reshape(2, 2, share, dim)
    own_rows = lax.dynamic_index_in_dim(quarters, core, 1, keepdims=False)
    own_rows = own_rows.reshape(half, dim)
    cot = jnp.where(plane == 0, jnp.stack([cotangent, cot_far]), jnp.stack([cot_far, cotangent])).reshape(half, dim)
    deg_far = flip_plane(degree)
    deg = jnp.where(plane == 0, jnp.stack([degree, deg_far]), jnp.stack([deg_far, degree])).astype(F32)
    inv_root = jnp.broadcast_to((1.0 / jnp.sqrt(deg)).reshape(half, 1), (half, dim))
    self_term = jnp.dot(own_rows, w_self, preferred_element_type=F32)

    scratch = [pltpu.VMEM((rows, dim), BF16), pltpu.VMEM((rows + tile_size, dim), F32)]
    spec_in = [SMEM, SMEM, VMEM]
    first = pl.pallas_call(
        forward_first,
        out_shape=jax.ShapeDtypeStruct((rows, dim), F32),
        in_specs=spec_in + [VMEM] * 2,
        out_specs=VMEM,
        scratch_shapes=scratch,
        name="forward_first",
    )(tile_coords, tile_live, tile_vals, *panels[0])
    keep, send = pl.pallas_call(
        forward_second,
        out_shape=[jax.ShapeDtypeStruct((2, share, dim), F32), jax.ShapeDtypeStruct((2, share, dim), BF16)],
        in_specs=spec_in + [VMEM] * 3,
        out_specs=[VMEM] * 2,
        scratch_shapes=scratch,
        name="forward_second",
    )(tile_coords, tile_live, tile_vals, *panels[1], first)

    chip_sum = (keep + flip_core(send).astype(F32)).reshape(half, dim)
    far_sum = flip_plane(chip_sum.astype(BF16))
    wide = jax.ShapeDtypeStruct((half, dim), BF16)
    agg, hidden_both, grad_pre, back = pl.pallas_call(
        middle,
        out_shape=[wide] * 4,
        in_specs=[VMEM] * 6,
        out_specs=[VMEM] * 4,
        name="middle",
    )(chip_sum, far_sum, inv_root, self_term, cot, w_neigh)

    back = back.reshape(2, share, dim)
    other_back = flip_core(back)
    piece = jax.ShapeDtypeStruct((half, dim), BF16)
    sends = pl.pallas_call(
        backward,
        out_shape=[piece] * 4,
        in_specs=spec_in + [VMEM] * 2,
        out_specs=[VMEM] * 4,
        scratch_shapes=scratch,
        name="backward",
    )(tile_coords, tile_live, tile_vals, back, other_back)

    arrived = []
    for j in range(slots):
        arrived.append(exchange(sends[2 * j], lambda b, r: (b + shift(r, j), r)))
        arrived.append(exchange(sends[2 * j + 1], lambda b, r: (b + shift(r, j), r ^ 2)))

    left = jnp.where(plane == 0, own_rows, agg)
    local = jnp.einsum("nd,ne->de", left, grad_pre, preferred_element_type=F32).reshape(2, dim // 2, dim)
    mine = lax.dynamic_index_in_dim(local, core, 0, keepdims=False)
    theirs = lax.dynamic_index_in_dim(local, 1 - core, 0, keepdims=False)
    grad = mine + flip_core(theirs.astype(BF16)).astype(F32)
    bit = 1
    while bit < part_total:
        rounded = grad.astype(BF16)
        grad = rounded.astype(F32) + exchange(rounded, lambda b, r: (b ^ bit, r)).astype(F32)
        bit *= 2
    rounded = grad.astype(BF16)
    far = flip_plane(rounded)
    by_plane = jnp.where(plane == 0, jnp.stack([rounded, far]), jnp.stack([far, rounded]))
    near = flip_core(by_plane)
    by_core = jnp.where(core == 0, jnp.stack([by_plane, near], 1), jnp.stack([near, by_plane], 1))
    grad_scale = 1.0 / math.sqrt(rows * part_total)
    totals = by_core.reshape(2, dim, dim).astype(F32) * grad_scale

    grad_pre_own = lax.dynamic_index_in_dim(grad_pre.reshape(2, share, dim), plane, 0, keepdims=False)
    own_term = jnp.einsum("ne,de->nd", grad_pre_own, w_self, preferred_element_type=F32)
    neighbour = sum(a.astype(F32) for a in arrived).reshape(2, share, dim)
    near = flip_core(lax.dynamic_index_in_dim(neighbour, 1 - core, 0, keepdims=False).astype(BF16))
    neighbour = lax.dynamic_index_in_dim(neighbour, core, 0, keepdims=False) + near.astype(F32)
    grad_features = (own_term + neighbour).astype(BF16)
    hidden = lax.dynamic_index_in_dim(hidden_both.reshape(2, share, dim), plane, 0, keepdims=False)
    return (hidden, grad_features, totals[0], totals[1])


def solution(mesh):
    return jax.shard_map(
        on_device,
        mesh=mesh,
        in_specs=(
            P("blk", "rep", None, None, None),
            P("blk", "rep", None, None),
            P("blk", "rep", None),
            P("blk", None),
            P(("blk", "rep")),
            P(),
            P(),
            P(("blk", "rep"), None),
        ),
        out_specs=(P(("blk", "rep"), None), P(("blk", "rep"), None), P(), P()),
        check_vma=False,
    )
```

time: 380 us -> 79.5 us (0.21)
  waiting for transfers between devices: 235 us -> 26.4 us
  starting transfers between devices: 75.5 us -> 28.5 us
  other arithmetic: 33.6 us -> 1.89 us
  between operations: 14.1 us -> 0.88 us
  Pallas kernels: 0 us -> 11 us
  matrix products: 12.5 us -> 2.88 us
  blocking collectives: 5.78 us -> 0 us
  local copies, waits for them, and re-layouts: 3.43 us -> 7.62 us
    psum x1 -> x0, waiting for transfers between devices: 119 us -> none  [on_device(): lax.psum((local_self, local_neigh), ('blk', 'rep'))]
    ppermute x16 -> x20, waiting for transfers between devices: 74 us -> 26.4 us  [exchange(): return lax.ppermute(value, BOTH, pairs)]
    ppermute x16 -> x20, starting transfers between devices: 75.4 us -> 28.5 us  [exchange(): return lax.ppermute(value, BOTH, pairs)]
    reduce_scatter x2 -> x0, waiting for transfers between devices: 41.6 us -> none  [the longest x1 23.4 us: on_device(): shared = lax.psum_scatter(summed, 'rep', scatter_dimension=0, tiled=True)]
    scatter-add x4 -> x0, other arithmetic: 23.5 us -> none  [the longest x2 11.7 us: backward_term(): placed = jnp.zeros((block_count, tile_size, feature_dim), jnp.float32).at...]
    pallas_call x0 -> x4, Pallas kernels: none -> 11 us  [the longest x1 3.09 us: on_device(): pl.pallas_call(backward, out_shape=[piece] * 4, in_specs=spec_in + [VMEM]...]
    dot_general x10 -> x3, matrix products: 12.5 us -> 2.88 us  [the longest x1 1.16 us: on_device(): jnp.einsum('nd,ne->de', left, grad_pre, preferred_element_type=F32)]
    all_gather x1 -> x0, blocking collectives: 5.78 us -> none  [on_device(): full_back = lax.all_gather(back_proj, 'rep', axis=0, tiled=True)]
  transfers between devices with their start and end apart: 19 -> 20, of which waited for: 18 -> 11; matrix products, arithmetic and copies ran while one was open for 4% -> 8% of each run, Pallas kernels for 0% -> 11%
where the time goes in v1:
time: 79.5 us; the launch traced here: 79.1 us
  starting transfers between devices  28.5 us (36%)
  waiting for transfers between devices  26.4 us (33%)
  Pallas kernels  11 us (14%)
  local copies, waits for them, and re-layouts  7.62 us (10%)
  matrix products  2.88 us (4%)
  other arithmetic  1.89 us (2%)
  between operations  0.88 us (1%)
    ppermute x20, starting transfers between devices, exchange(): return lax.ppermute(value, BOTH, pairs)  28.5 us
    ppermute x20, waiting for transfers between devices, exchange(): return lax.ppermute(value, BOTH, pairs)  26.4 us
    unnamed x25, local copies, waits for them, and re-layouts  3.38 us
    pallas_call x1, Pallas kernels, on_device(): pl.pallas_call(backward, out_shape=[piece] * 4, in_specs=spec_in + [VMEM]...  3.09 us
    pallas_call x1, Pallas kernels, on_device(): pl.pallas_call(forward_second, out_shape=[jax.ShapeDtypeStruct((2, share,...  2.83 us
    pallas_call x1, Pallas kernels, on_device(): pl.pallas_call(forward_first, out_shape=jax.ShapeDtypeStruct((rows, dim),...  2.76 us
    pallas_call x1, Pallas kernels, on_device(): pl.pallas_call(middle, out_shape=[wide] * 4, in_specs=[VMEM] * 6, out_spe...  2.29 us
  transfers between devices with their start and end apart: 20, of which 11 were waited for; matrix products, arithmetic and copies ran while one was open for 8% of the time, Pallas kernels for 11%

profile of v1, /device:TPU:0, one launch (start us, length us, event | category | flops | bytes accessed | tf_op | source)
XLA Modules:
  0.0 79.1 jit_solution(13785878976965777157)
XLA Ops:
  0.6 0.0 copy-start
  0.6 1.0 %fusion.18 = (bf16[256,256]{1,0:T(8,128)(2,1)S(1)}, bf16[256,256]{1,0:T(8,128)(2,1)S(1)}) fusion(bf16[512,256]{1,0:T(8,128)(2,1)} %param.11), kind=kLoop, calls=%fused_computation.34 | loop fusion | bytes 524288 | tf_op jit(solution)/shard_map/slice | solution.py:118
  1.7 5.9 %collective-permute-start.2 = (bf16[256,256]{1,0:T(8,128)(2,1)S(1)}, bf16[256,256]{1,0:T(8,128)(2,1)S(1)}, u32[]{:S(2)}, u32[]{:S(2)}) collective-permute-start(bf16[256,256]{1,0:T(8,128)(2,1)S(1)} %get-tuple-element.27), channel_id=1, source_target_pairs={{0,16},{1,9},{2,2},{3,27},{4,20},{5,13},{6,6},{7,31},{8,24},{9,17}... | collective-permute-start | bytes 393224 | tf_op jit(solution)/shard_map/ppermute | solution.py:24
  7.6 0.1 collective-permute-start.3
  7.7 2.6 %collective-permute-start = (bf16[256,256]{1,0:T(8,128)(2,1)S(1)}, bf16[256,256]{1,0:T(8,128)(2,1)S(1)}, u32[]{:S(2)}, u32[]{:S(2)}) collective-permute-start(bf16[256,256]{1,0:T(8,128)(2,1)S(1)} %get-tuple-element.27), channel_id=1, source_target_pairs={{0,12},{1,5},{2,30},{3,23},{4,16},{5,9},{6,2},{7,27},{8,20},{9,13}... | collective-permute-start | bytes 393224 | tf_op jit(solution)/shard_map/ppermute | solution.py:24
  10.3 3.7 %collective-permute-start.1 = (bf16[256,256]{1,0:T(8,128)(2,1)S(1)}, bf16[256,256]{1,0:T(8,128)(2,1)S(1)}, u32[]{:S(2)}, u32[]{:S(2)}) collective-permute-start(bf16[256,256]{1,0:T(8,128)(2,1)S(1)} %get-tuple-element.26), channel_id=1, source_target_pairs={{0,30},{1,23},{2,12},{3,5},{4,2},{5,27},{6,16},{7,9},{8,6},{9,31},... | collective-permute-start | bytes 393224 | tf_op jit(solution)/shard_map/ppermute | solution.py:24
  14.0 0.1 collective-permute-start.6
  14.0 1.4 %copy.13.coords = s32[1,2,20,2]{3,2,1,0:T(8,128)} copy(s32[1,2,20,2]{2,3,1,0:T(2,128)} %param.9) | data formatting | bytes 640 | tf_op args[1]
  15.4 0.9 %constant_dynamic-slice_fusion = bf16[2,1,128,256]{3,2,1,0:T(8,128)(2,1)S(1)} fusion(bf16[2,2,128,256]{3,2,1,0:T(8,128)(2,1)} %bitcast.57, s32[]{:T(128)S(6)} %select_n.89), kind=kLoop, calls=%fused_computation.27 | loop fusion | bytes 262148 | tf_op jit(solution)/shard_map/jit(dynamic_index_in_dim)/dynamic_slice | solution.py:131
  16.3 0.7 collective-permute-done.2.low
  17.0 1.4 %collective-permute-start.7 = (bf16[128,256]{1,0:T(8,128)(2,1)}, bf16[128,256]{1,0:T(8,128)(2,1)S(1)}, u32[]{:S(2)}, u32[]{:S(2)}) collective-permute-start(bf16[128,256]{1,0:T(8,128)(2,1)} %param.15), channel_id=1, source_target_pairs={{0,2},{1,3},{2,0},{3,1},{4,6},{5,7},{6,4},{7,5},{8,10},{9,11},{10,... | collective-permute-start | bytes 196616 | tf_op jit(solution)/shard_map/ppermute | solution.py:24
  18.4 0.0 collective-permute-done.3.high
  18.4 0.7 copy-done.8
  19.1 2.8 %forward_first.1.before = f32[512,256]{1,0:T(8,128)} custom-call(s32[1,2,20,2]{3,2,1,0:T(8,128)} %copy.13.coords, s32[1,2,20]{2,1,0:T(2,128)} %live.5, bf16[1,2,20,128,128]{4,3,2,1,0:T(8,128)(2,1)} %tiles.5, bf16[256,256]{1,0:T(8,128)(2,1)} %copy-done.7, bf16[256,256]{1,0:T(8,128)(2,1)} %copy-done.8), custom_call_target="tpu_custom_call" | custom-call | tf_op jit(solution)/shard_map/forward_first/pallas_call | solution.py:141
  21.8 0.0 collective-permute-done.low
  21.8 0.9 %collective-permute-done.1.high = bf16[256,256]{1,0:T(8,128)(2,1)S(1)} collective-permute-done((bf16[256,256]{1,0:T(8,128)(2,1)S(1)}, bf16[256,256]{1,0:T(8,128)(2,1)S(1)}, u32[]{:S(2)}, u32[]{:S(2)}) %collective-permute-start.1) | collective-permute-done | bytes 131104 | tf_op jit(solution)/shard_map/ppermute | solution.py:24
  22.8 0.6 copy-done.6
  23.4 2.8 %forward_second.1 = (f32[2,128,256]{2,1,0:T(8,128)}, bf16[2,128,256]{2,1,0:T(8,128)(2,1)}) custom-call(s32[1,2,20,2]{3,2,1,0:T(8,128)} %copy.13.coords, s32[1,2,20]{2,1,0:T(2,128)} %live.5, bf16[1,2,20,128,128]{4,3,2,1,0:T(8,128)(2,1)} %tiles.5, bf16[256,256]{1,0:T(8,128)(2,1)} %copy-done.5, bf16[256,256]{1,0:T(8,128)(2,1)} %copy-done.6, ...), custom_call_target="tpu_custom_call" | custom-call | tf_op jit(solution)/shard_map/forward_second/pallas_call | solution.py:149
  26.3 0.1 collective-permute-start.4
  26.3 0.9 %fusion.19.self_term = f32[256,256]{1,0:T(8,128)} fusion(bf16[256,256]{1,0:T(8,128)(2,1)S(1)} %bitcast.51, bf16[256,256]{1,0:T(8,128)(2,1)S(1)} %copy-done), kind=kOutput, calls=%fused_computation.35 | convolution fusion | flops 33554432 | bytes 524288 | tf_op jit(solution)/shard_map/dot_general | solution.py:137
  27.2 0.7 collective-permute-done.4
  27.9 1.0 %convert_add_fusion.1 = f32[2,128,256]{2,1,0:T(8,128)S(1)} fusion(f32[2,128,256]{2,1,0:T(8,128)} %get-tuple-element.14, bf16[2,128,256]{2,1,0:T(8,128)(2,1)S(1)} %collective-permute-done.4), kind=kLoop, calls=%fused_computation.3 | loop fusion | flops 131072 | bytes 655360 | tf_op jit(solution)/shard_map/add | solution.py:158
  28.9 0.0 copy-start.1
  28.9 0.4 collective-permute-start.5
  29.3 0.0 collective-permute-done.6
  29.3 0.0 copy-done.11
  29.3 0.0 collective-permute-done.7
  29.3 0.7 maximum_select_fusion.1
  30.0 4.5 %collective-permute-done.5.far_sum = bf16[256,256]{1,0:T(8,128)(2,1)S(1)} collective-permute-done((bf16[256,256]{1,0:T(8,128)(2,1)S(1)}, bf16[256,256]{1,0:T(8,128)(2,1)S(1)}, u32[]{:S(2)}, u32[]{:S(2)}) %collective-permute-start.5) | collective-permute-done | bytes 131104 | tf_op jit(solution)/shard_map/ppermute | solution.py:24
  34.5 0.8 %broadcast_in_dim.2.inv_root = f32[256,256]{1,0:T(8,128)} broadcast(f32[256]{0:T(256)S(1)} %fusion.16), dimensions={0} | broadcast | bytes 263168 | tf_op jit(solution)/shard_map/broadcast_in_dim | solution.py:136
  35.3 0.0 copy-done.1
  35.3 2.3 %middle.1 = (bf16[256,256]{1,0:T(8,128)(2,1)}, bf16[256,256]{1,0:T(8,128)(2,1)}, bf16[256,256]{1,0:T(8,128)(2,1)}, bf16[256,256]{1,0:T(8,128)(2,1)}) custom-call(f32[256,256]{1,0:T(8,128)} %bitcast.50, bf16[256,256]{1,0:T(8,128)(2,1)} %copy-done.3, f32[256,256]{1,0:T(8,128)} %broadcast_in_dim.2.inv_root, f32[256,256]{1,0:T(8,128)} %fusion.19.self_term, ...), custom_call_target="tpu_custom_call" | custom-call | tf_op jit(solution)/shard_map/middle/pallas_call | solution.py:161
  37.6 1.2 %fusion.3 = f32[256,256]{1,0:T(8,128)S(1)} fusion(bf16[256,256]{1,0:T(8,128)(2,1)} %get-tuple-element.17, bf16[256,256]{1,0:T(8,128)(2,1)S(1)} %bitcast.52, bf16[256,256]{1,0:T(8,128)(2,1)} %get-tuple-element.23, pred[]{:T(512)S(6)} %eq.6), kind=kOutput, calls=%fused_computation.16 | convolution fusion | flops 33619968 | bytes 655361 | tf_op jit(solution)/shard_map/nd,ne->de/dot_general | solution.py:187
  38.8 0.1 collective-permute-start.14
  38.9 1.2 %collective-permute-done.14 = bf16[128,256]{1,0:T(8,128)(2,1)S(1)} collective-permute-done((bf16[128,256]{1,0:T(8,128)(2,1)S(1)}, bf16[128,256]{1,0:T(8,128)(2,1)S(1)}, u32[]{:S(2)}, u32[]{:S(2)}) %collective-permute-start.14) | collective-permute-done | bytes 65568 | tf_op jit(solution)/shard_map/ppermute | solution.py:24
  40.1 3.1 %collective-permute-start.15 = (bf16[128,256]{1,0:T(8,128)(2,1)S(1)}, bf16[128,256]{1,0:T(8,128)(2,1)S(1)}, u32[]{:S(2)}, u32[]{:S(2)}) collective-permute-start(bf16[128,256]{1,0:T(8,128)(2,1)S(1)} %fusion), channel_id=1, source_target_pairs={{0,4},{1,5},{2,6},{3,7},{4,0},{5,1},{6,2},{7,3},{8,12},{9,13},{10,... | collective-permute-start | bytes 196616 | tf_op jit(solution)/shard_map/ppermute | solution.py:24
  43.3 2.4 %collective-permute-done.15 = bf16[128,256]{1,0:T(8,128)(2,1)S(1)} collective-permute-done((bf16[128,256]{1,0:T(8,128)(2,1)S(1)}, bf16[128,256]{1,0:T(8,128)(2,1)S(1)}, u32[]{:S(2)}, u32[]{:S(2)}) %collective-permute-start.15) | collective-permute-done | bytes 65568 | tf_op jit(solution)/shard_map/ppermute | solution.py:24
  45.7 0.1 collective-permute-start.16
  45.8 0.1 collective-permute-start.8
  45.9 4.2 %collective-permute-done.16 = bf16[128,256]{1,0:T(8,128)(2,1)S(1)} collective-permute-done((bf16[128,256]{1,0:T(8,128)(2,1)S(1)}, bf16[128,256]{1,0:T(8,128)(2,1)S(1)}, u32[]{:S(2)}, u32[]{:S(2)}) %collective-permute-start.16) | collective-permute-done | bytes 65568 | tf_op jit(solution)/shard_map/ppermute | solution.py:24
  50.1 1.0 %collective-permute-start.17 = (bf16[128,256]{1,0:T(8,128)(2,1)S(1)}, bf16[128,256]{1,0:T(8,128)(2,1)S(1)}, u32[]{:S(2)}, u32[]{:S(2)}) collective-permute-start(bf16[128,256]{1,0:T(8,128)(2,1)S(1)} %add_convert_fusion.1), channel_id=1, source_target_pairs={{0,16},{1,17},{2,18},{3,19},{4,20},{5,21},{6,22},{7,23},{8,24},{9,... | collective-permute-start | bytes 196616 | tf_op jit(solution)/shard_map/ppermute | solution.py:24
  51.1 0.6 dynamic-slice_bitcast_fusion
  51.7 0.0 collective-permute-done.8.other
  51.7 0.7 copy-done.4
  52.4 3.1 %backward.1 = (bf16[256,256]{1,0:T(8,128)(2,1)}, bf16[256,256]{1,0:T(8,128)(2,1)}, bf16[256,256]{1,0:T(8,128)(2,1)}, bf16[256,256]{1,0:T(8,128)(2,1)}) custom-call(s32[1,2,20,2]{3,2,1,0:T(8,128)} %copy.13.coords, s32[1,2,20]{2,1,0:T(2,128)} %live.5, bf16[1,2,20,128,128]{4,3,2,1,0:T(8,128)(2,1)} %tiles.5, bf16[2,128,256]{2,1,0:T(8,128)(2,1)} %bitcast.68, ...), custom_call_target="tpu_custom_call" | custom-call | tf_op jit(solution)/shard_map/backward/pallas_call | solution.py:172
  55.5 3.0 %collective-permute-start.12 = (bf16[256,256]{1,0:T(8,128)(2,1)}, bf16[256,256]{1,0:T(8,128)(2,1)S(1)}, u32[]{:S(2)}, u32[]{:S(2)}) collective-permute-start(bf16[256,256]{1,0:T(8,128)(2,1)} %get-tuple-element.22), channel_id=1, source_target_pairs={{0,22},{1,31},{2,4},{3,13},{4,26},{5,3},{6,8},{7,17},{8,30},{9,7},... | collective-permute-start | bytes 393224 | tf_op jit(solution)/shard_map/ppermute | solution.py:24
  58.5 1.9 %collective-permute-start.11 = (bf16[256,256]{1,0:T(8,128)(2,1)}, bf16[256,256]{1,0:T(8,128)(2,1)S(1)}, u32[]{:S(2)}, u32[]{:S(2)}) collective-permute-start(bf16[256,256]{1,0:T(8,128)(2,1)} %get-tuple-element.21), channel_id=1, source_target_pairs={{0,20},{1,29},{2,6},{3,15},{4,24},{5,1},{6,10},{7,19},{8,28},{9,5}... | collective-permute-start | bytes 393224 | tf_op jit(solution)/shard_map/ppermute | solution.py:24
  60.5 0.0 collective-permute-start.10
  60.5 4.2 %collective-permute-start.9 = (bf16[256,256]{1,0:T(8,128)(2,1)}, bf16[256,256]{1,0:T(8,128)(2,1)S(1)}, u32[]{:S(2)}, u32[]{:S(2)}) collective-permute-start(bf16[256,256]{1,0:T(8,128)(2,1)} %get-tuple-element.19), channel_id=1, source_target_pairs={{0,16},{1,25},{2,2},{3,11},{4,20},{5,29},{6,6},{7,15},{8,24},{9,1}... | collective-permute-start | bytes 393224 | tf_op jit(solution)/shard_map/ppermute | solution.py:24
  64.7 0.0 collective-permute-done.17
  64.7 0.1 collective-permute-start.18
  64.8 1.2 %collective-permute-done.12 = bf16[256,256]{1,0:T(8,128)(2,1)S(1)} collective-permute-done((bf16[256,256]{1,0:T(8,128)(2,1)}, bf16[256,256]{1,0:T(8,128)(2,1)S(1)}, u32[]{:S(2)}, u32[]{:S(2)}) %collective-permute-start.12) | collective-permute-done | bytes 131104 | tf_op jit(solution)/shard_map/ppermute | solution.py:24
  66.0 0.0 collective-permute-done.11
  66.0 1.1 %collective-permute-done.10 = bf16[256,256]{1,0:T(8,128)(2,1)S(1)} collective-permute-done((bf16[256,256]{1,0:T(8,128)(2,1)}, bf16[256,256]{1,0:T(8,128)(2,1)S(1)}, u32[]{:S(2)}, u32[]{:S(2)}) %collective-permute-start.10) | collective-permute-done | bytes 131104 | tf_op jit(solution)/shard_map/ppermute | solution.py:24
  67.1 8.8 %collective-permute-done.9 = bf16[256,256]{1,0:T(8,128)(2,1)S(1)} collective-permute-done((bf16[256,256]{1,0:T(8,128)(2,1)}, bf16[256,256]{1,0:T(8,128)(2,1)S(1)}, u32[]{:S(2)}, u32[]{:S(2)}) %collective-permute-start.9) | collective-permute-done | bytes 131104 | tf_op jit(solution)/shard_map/ppermute | solution.py:24
  75.9 0.1 convert_add_fusion
  76.0 0.1 collective-permute-start.13
  76.1 0.0 collective-permute-done.18
  76.1 0.5 collective-permute-start.19
  76.7 0.6 collective-permute-done.13
  77.4 0.8 %fusion.2 = bf16[128,256]{1,0:T(8,128)(2,1)} fusion(bf16[128,256]{1,0:T(8,128)(2,1)S(1)} %collective-permute-done.13, f32[2,128,256]{2,1,0:T(8,128)S(1)} %bitcast.54, s32[]{:T(128)S(6)} %select_n.89, bf16[256,256]{1,0:T(8,128)(2,1)S(1)} %copy-done, bf16[2,128,256]{2,1,0:T(8,128)(2,1)S(1)} %bitcast.61, s32[]{:T(128)S(6)} %select_n.93), kind=kOutput, calls=%fused_computation.11 | convolution fusion | flops 16908288 | bytes 458760 | tf_op jit(solution)/shard_map/ne,de->nd/dot_general | solution.py:205
  78.2 0.0 collective-permute-done.19
  78.2 0.1 convert_multiply_fusion
  78.3 0.8 %fusion.17 = (f32[1,2,128,256]{3,2,0,1:T(8,128)}, f32[1,2,128,256]{3,2,0,1:T(8,128)}) fusion(f32[2,2,128,256]{3,2,0,1:T(8,128)S(1)} %convert_multiply_fusion), kind=kLoop, calls=%fused_computation.33 | loop fusion | bytes 1048576 | tf_op jit(solution)/shard_map/slice | solution.py:211
  (27 shorter events, 0.2 us)
Async XLA Ops:
  0.6 25.7 %copy-start = (bf16[256,256]{1,0:T(8,128)(2,1)S(1)}, bf16[256,256]{1,0:T(8,128)(2,1)}, u32[]{:S(2)}) copy-start(bf16[256,256]{1,0:T(8,128)(2,1)} %param.13) | copy-start | bytes 393220
  1.7 15.3 %collective-permute-start.2 = (bf16[256,256]{1,0:T(8,128)(2,1)S(1)}, bf16[256,256]{1,0:T(8,128)(2,1)S(1)}, u32[]{:S(2)}, u32[]{:S(2)}) collective-permute-start(bf16[256,256]{1,0:T(8,128)(2,1)S(1)} %get-tuple-element.27), channel_id=1, source_target_pairs={{0,16},{1,9},{2,2},{3,27},{4,20},{5,13},{6,6},{7,31},{8,24},{9,17}... | collective-permute-start | bytes 393224 | tf_op jit(solution)/shard_map/ppermute | solution.py:24
  7.6 10.8 %collective-permute-start.3 = (bf16[256,256]{1,0:T(8,128)(2,1)S(1)}, bf16[256,256]{1,0:T(8,128)(2,1)S(1)}, u32[]{:S(2)}, u32[]{:S(2)}) collective-permute-start(bf16[256,256]{1,0:T(8,128)(2,1)S(1)} %get-tuple-element.26), channel_id=1, source_target_pairs={{0,2},{1,27},{2,16},{3,9},{4,6},{5,31},{6,20},{7,13},{8,10},{9,3},... | collective-permute-start | bytes 393224 | tf_op jit(solution)/shard_map/ppermute | solution.py:24
  7.7 14.1 %collective-permute-start = (bf16[256,256]{1,0:T(8,128)(2,1)S(1)}, bf16[256,256]{1,0:T(8,128)(2,1)S(1)}, u32[]{:S(2)}, u32[]{:S(2)}) collective-permute-start(bf16[256,256]{1,0:T(8,128)(2,1)S(1)} %get-tuple-element.27), channel_id=1, source_target_pairs={{0,12},{1,5},{2,30},{3,23},{4,16},{5,9},{6,2},{7,27},{8,20},{9,13}... | collective-permute-start | bytes 393224 | tf_op jit(solution)/shard_map/ppermute | solution.py:24
  10.3 12.5 %collective-permute-start.1 = (bf16[256,256]{1,0:T(8,128)(2,1)S(1)}, bf16[256,256]{1,0:T(8,128)(2,1)S(1)}, u32[]{:S(2)}, u32[]{:S(2)}) collective-permute-start(bf16[256,256]{1,0:T(8,128)(2,1)S(1)} %get-tuple-element.26), channel_id=1, source_target_pairs={{0,30},{1,23},{2,12},{3,5},{4,2},{5,27},{6,16},{7,9},{8,6},{9,31},... | collective-permute-start | bytes 393224 | tf_op jit(solution)/shard_map/ppermute | solution.py:24
  14.0 15.3 %collective-permute-start.6 = (s32[128]{0:T(128)}, s32[128]{0:T(128)S(1)}, u32[]{:S(2)}, u32[]{:S(2)}) collective-permute-start(s32[128]{0:T(128)} %param.12), channel_id=1, source_target_pairs={{0,2},{1,3},{2,0},{3,1},{4,6},{5,7},{6,4},{7,5},{8,10},{9,11},{10,... | collective-permute-start | bytes 1544 | tf_op jit(solution)/shard_map/ppermute | solution.py:24
  17.0 1.4 %copy-start.7 = (bf16[256,256]{1,0:T(8,128)(2,1)}, bf16[256,256]{1,0:T(8,128)(2,1)S(1)}, u32[]{:S(2)}) copy-start(bf16[256,256]{1,0:T(8,128)(2,1)S(1)} %collective-permute-done.2.low) | copy-start | bytes 393220
  17.0 12.3 %collective-permute-start.7 = (bf16[128,256]{1,0:T(8,128)(2,1)}, bf16[128,256]{1,0:T(8,128)(2,1)S(1)}, u32[]{:S(2)}, u32[]{:S(2)}) collective-permute-start(bf16[128,256]{1,0:T(8,128)(2,1)} %param.15), channel_id=1, source_target_pairs={{0,2},{1,3},{2,0},{3,1},{4,6},{5,7},{6,4},{7,5},{8,10},{9,11},{10,... | collective-permute-start | bytes 196616 | tf_op jit(solution)/shard_map/ppermute | solution.py:24
  18.4 0.7 copy-start.8
  21.8 0.9 %copy-start.5 = (bf16[256,256]{1,0:T(8,128)(2,1)}, bf16[256,256]{1,0:T(8,128)(2,1)S(1)}, u32[]{:S(2)}) copy-start(bf16[256,256]{1,0:T(8,128)(2,1)S(1)} %collective-permute-done.low) | copy-start | bytes 393220
  22.8 0.6 copy-start.6
  26.3 3.1 %copy-start.11 = (s32[128]{0:T(128)S(1)}, s32[128]{0:T(128)}, u32[]{:S(2)}) copy-start(s32[128]{0:T(128)} %param.12) | copy-start | bytes 1540
  26.3 3.1 %copy-start.9 = (bf16[128,256]{1,0:T(8,128)(2,1)S(1)}, bf16[128,256]{1,0:T(8,128)(2,1)}, u32[]{:S(2)}) copy-start(bf16[128,256]{1,0:T(8,128)(2,1)} %param.15) | copy-start | bytes 196612
  26.3 1.6 %collective-permute-start.4 = (bf16[2,128,256]{2,1,0:T(8,128)(2,1)}, bf16[2,128,256]{2,1,0:T(8,128)(2,1)S(1)}, u32[]{:S(2)}, u32[]{:S(2)}) collective-permute-start(bf16[2,128,256]{2,1,0:T(8,128)(2,1)} %get-tuple-element.15), channel_id=1, source_target_pairs={{0,1},{1,0},{2,3},{3,2},{4,5},{5,4},{6,7},{7,6},{8,9},{9,8},{10,11... | collective-permute-start | bytes 393224 | tf_op jit(solution)/shard_map/ppermute | solution.py:24
  28.9 6.5 %copy-start.1 = (f32[2,128,256]{2,1,0:T(8,128)}, f32[2,128,256]{2,1,0:T(8,128)S(1)}, u32[]{:S(2)}) copy-start(f32[2,128,256]{2,1,0:T(8,128)S(1)} %convert_add_fusion.1) | copy-start | bytes 786436
  28.9 5.6 %collective-permute-start.5 = (bf16[256,256]{1,0:T(8,128)(2,1)S(1)}, bf16[256,256]{1,0:T(8,128)(2,1)S(1)}, u32[]{:S(2)}, u32[]{:S(2)}) collective-permute-start(bf16[256,256]{1,0:T(8,128)(2,1)S(1)} %bitcast_convert_fusion), channel_id=1, source_target_pairs={{0,2},{1,3},{2,0},{3,1},{4,6},{5,7},{6,4},{7,5},{8,10},{9,11},{10,... | collective-permute-start | bytes 393224 | tf_op jit(solution)/shard_map/ppermute | solution.py:24
  34.5 0.8 %copy-start.3 = (bf16[256,256]{1,0:T(8,128)(2,1)}, bf16[256,256]{1,0:T(8,128)(2,1)S(1)}, u32[]{:S(2)}) copy-start(bf16[256,256]{1,0:T(8,128)(2,1)S(1)} %collective-permute-done.5.far_sum) | copy-start | bytes 393220
  37.6 13.5 %copy-start.10 = (bf16[256,256]{1,0:T(8,128)(2,1)S(1)}, bf16[256,256]{1,0:T(8,128)(2,1)}, u32[]{:S(2)}) copy-start(bf16[256,256]{1,0:T(8,128)(2,1)} %get-tuple-element.16) | copy-start | bytes 393220
  38.8 1.3 %collective-permute-start.14 = (bf16[128,256]{1,0:T(8,128)(2,1)S(1)}, bf16[128,256]{1,0:T(8,128)(2,1)S(1)}, u32[]{:S(2)}, u32[]{:S(2)}) collective-permute-start(bf16[128,256]{1,0:T(8,128)(2,1)S(1)} %fusion.7), channel_id=1, source_target_pairs={{0,1},{1,0},{2,3},{3,2},{4,5},{5,4},{6,7},{7,6},{8,9},{9,8},{10,11... | collective-permute-start | bytes 196616 | tf_op jit(solution)/shard_map/ppermute | solution.py:24
  40.1 5.5 %collective-permute-start.15 = (bf16[128,256]{1,0:T(8,128)(2,1)S(1)}, bf16[128,256]{1,0:T(8,128)(2,1)S(1)}, u32[]{:S(2)}, u32[]{:S(2)}) collective-permute-start(bf16[128,256]{1,0:T(8,128)(2,1)S(1)} %fusion), channel_id=1, source_target_pairs={{0,4},{1,5},{2,6},{3,7},{4,0},{5,1},{6,2},{7,3},{8,12},{9,13},{10,... | collective-permute-start | bytes 196616 | tf_op jit(solution)/shard_map/ppermute | solution.py:24
  45.7 4.3 %collective-permute-start.16 = (bf16[128,256]{1,0:T(8,128)(2,1)S(1)}, bf16[128,256]{1,0:T(8,128)(2,1)S(1)}, u32[]{:S(2)}, u32[]{:S(2)}) collective-permute-start(bf16[128,256]{1,0:T(8,128)(2,1)S(1)} %add_convert_fusion.2), channel_id=1, source_target_pairs={{0,8},{1,9},{2,10},{3,11},{4,12},{5,13},{6,14},{7,15},{8,0},{9,1},... | collective-permute-start | bytes 196616 | tf_op jit(solution)/shard_map/ppermute | solution.py:24
  45.8 5.9 %collective-permute-start.8 = (bf16[2,128,256]{2,1,0:T(8,128)(2,1)}, bf16[2,128,256]{2,1,0:T(8,128)(2,1)S(1)}, u32[]{:S(2)}, u32[]{:S(2)}) collective-permute-start(bf16[2,128,256]{2,1,0:T(8,128)(2,1)} %bitcast.67), channel_id=1, source_target_pairs={{0,1},{1,0},{2,3},{3,2},{4,5},{5,4},{6,7},{7,6},{8,9},{9,8},{10,11... | collective-permute-start | bytes 393224 | tf_op jit(solution)/shard_map/ppermute | solution.py:24
  50.1 14.6 %collective-permute-start.17 = (bf16[128,256]{1,0:T(8,128)(2,1)S(1)}, bf16[128,256]{1,0:T(8,128)(2,1)S(1)}, u32[]{:S(2)}, u32[]{:S(2)}) collective-permute-start(bf16[128,256]{1,0:T(8,128)(2,1)S(1)} %add_convert_fusion.1), channel_id=1, source_target_pairs={{0,16},{1,17},{2,18},{3,19},{4,20},{5,21},{6,22},{7,23},{8,24},{9,... | collective-permute-start | bytes 196616 | tf_op jit(solution)/shard_map/ppermute | solution.py:24
  51.7 25.6 %copy-start.2 = (bf16[256,256]{1,0:T(8,128)(2,1)S(1)}, bf16[256,256]{1,0:T(8,128)(2,1)}, u32[]{:S(2)}) copy-start(bf16[256,256]{1,0:T(8,128)(2,1)} %get-tuple-element.17) | copy-start | bytes 393220
  51.7 0.7 copy-start.4
  55.5 10.6 %collective-permute-start.12 = (bf16[256,256]{1,0:T(8,128)(2,1)}, bf16[256,256]{1,0:T(8,128)(2,1)S(1)}, u32[]{:S(2)}, u32[]{:S(2)}) collective-permute-start(bf16[256,256]{1,0:T(8,128)(2,1)} %get-tuple-element.22), channel_id=1, source_target_pairs={{0,22},{1,31},{2,4},{3,13},{4,26},{5,3},{6,8},{7,17},{8,30},{9,7},... | collective-permute-start | bytes 393224 | tf_op jit(solution)/shard_map/ppermute | solution.py:24
  58.5 7.5 %collective-permute-start.11 = (bf16[256,256]{1,0:T(8,128)(2,1)}, bf16[256,256]{1,0:T(8,128)(2,1)S(1)}, u32[]{:S(2)}, u32[]{:S(2)}) collective-permute-start(bf16[256,256]{1,0:T(8,128)(2,1)} %get-tuple-element.21), channel_id=1, source_target_pairs={{0,20},{1,29},{2,6},{3,15},{4,24},{5,1},{6,10},{7,19},{8,28},{9,5}... | collective-permute-start | bytes 393224 | tf_op jit(solution)/shard_map/ppermute | solution.py:24
  60.5 6.7 %collective-permute-start.10 = (bf16[256,256]{1,0:T(8,128)(2,1)}, bf16[256,256]{1,0:T(8,128)(2,1)S(1)}, u32[]{:S(2)}, u32[]{:S(2)}) collective-permute-start(bf16[256,256]{1,0:T(8,128)(2,1)} %get-tuple-element.20), channel_id=1, source_target_pairs={{0,18},{1,27},{2,0},{3,9},{4,22},{5,31},{6,4},{7,13},{8,26},{9,3},... | collective-permute-start | bytes 393224 | tf_op jit(solution)/shard_map/ppermute | solution.py:24
  60.5 15.5 %collective-permute-start.9 = (bf16[256,256]{1,0:T(8,128)(2,1)}, bf16[256,256]{1,0:T(8,128)(2,1)S(1)}, u32[]{:S(2)}, u32[]{:S(2)}) collective-permute-start(bf16[256,256]{1,0:T(8,128)(2,1)} %get-tuple-element.19), channel_id=1, source_target_pairs={{0,16},{1,25},{2,2},{3,11},{4,20},{5,29},{6,6},{7,15},{8,24},{9,1}... | collective-permute-start | bytes 393224 | tf_op jit(solution)/shard_map/ppermute | solution.py:24
  64.7 11.4 %collective-permute-start.18 = (bf16[128,256]{1,0:T(8,128)(2,1)S(1)}, bf16[128,256]{1,0:T(8,128)(2,1)S(1)}, u32[]{:S(2)}, u32[]{:S(2)}) collective-permute-start(bf16[128,256]{1,0:T(8,128)(2,1)S(1)} %add_convert_fusion), channel_id=1, source_target_pairs={{0,2},{1,3},{2,0},{3,1},{4,6},{5,7},{6,4},{7,5},{8,10},{9,11},{10,... | collective-permute-start | bytes 196616 | tf_op jit(solution)/shard_map/ppermute | solution.py:24
  76.0 1.3 %collective-permute-start.13 = (bf16[128,256]{1,0:T(8,128)(2,1)S(1)}, bf16[128,256]{1,0:T(8,128)(2,1)S(1)}, u32[]{:S(2)}, u32[]{:S(2)}) collective-permute-start(bf16[128,256]{1,0:T(8,128)(2,1)S(1)} %fusion.6), channel_id=1, source_target_pairs={{0,1},{1,0},{2,3},{3,2},{4,5},{5,4},{6,7},{7,6},{8,9},{9,8},{10,11... | collective-permute-start | bytes 196616 | tf_op jit(solution)/shard_map/ppermute | solution.py:24
  76.1 2.0 %collective-permute-start.19 = (bf16[2,128,256]{2,1,0:T(8,128)(2,1)S(1)}, bf16[2,128,256]{2,1,0:T(8,128)(2,1)S(1)}, u32[]{:S(2)}, u32[]{:S(2)}) collective-permute-start(bf16[2,128,256]{2,1,0:T(8,128)(2,1)S(1)} %maximum_select_fusion.3), channel_id=1, source_target_pairs={{0,1},{1,0},{2,3},{3,2},{4,5},{5,4},{6,7},{7,6},{8,9},{9,8},{10,11... | collective-permute-start | bytes 393224 | tf_op jit(solution)/shard_map/ppermute | solution.py:24

commit v2 on v1

v2 whole, which is shorter than its diff:
```python
import math

import jax
import jax.numpy as jnp
from jax import lax
from jax.experimental import pallas as pl
from jax.experimental.pallas import tpu as pltpu
from jax.sharding import PartitionSpec as P

BOTH = ("blk", "rep")
BF16 = jnp.bfloat16
F32 = jnp.float32
VMEM = pl.BlockSpec(memory_space=pltpu.VMEM)
SMEM = pl.BlockSpec(memory_space=pltpu.SMEM)


def exchange(value, target):
    part_total, rep_count = lax.axis_size("blk"), lax.axis_size("rep")
    pairs = []
    for part in range(part_total):
        for rep in range(rep_count):
            to_part, to_rep = target(part, rep)
            pairs.append((part * rep_count + rep, (to_part % part_total) * rep_count + to_rep))
    return lax.ppermute(value, BOTH, pairs)


def dot(lhs, rhs, contract):
    return lax.dot_general(lhs, rhs, (contract, ((), ())), preferred_element_type=F32)


def place_tiles(slot, out_axis, meta, tiles, source, total):
    size = tiles.shape[-1]
    tile_count = tiles.shape[-3]
    for k in range(tile_count):
        to = meta[out_axis, slot * tile_count + k]
        take = meta[3 - out_axis, slot * tile_count + k]
        block = source[pl.ds(pl.multiple_of(take * size, size), size), :]
        rows = pl.ds(pl.multiple_of(to * size, size), size)
        total[rows, :] += dot(tiles[0, slot, k], block, ((1 - out_axis,), (0,)))


def forward_first(meta, tiles, local, arrived, out, source, total):
    is_local = lax.axis_index("rep") == local_rep(tiles.shape[1])

    @pl.when(is_local)
    def _():
        source[...] = local[...]

    @pl.when(jnp.logical_not(is_local))
    def _():
        source[...] = arrived[...]

    total[...] = jnp.zeros_like(total)
    place_tiles(0, 0, meta, tiles, source, total)
    out[...] = total[: out.shape[0], :]


def forward_second(meta, tiles, arrived, before, keep, send, total):
    rows = before.shape[0]
    total[:rows, :] = before[...]
    total[rows:, :] = jnp.zeros((total.shape[0] - rows, total.shape[1]), F32)
    place_tiles(1, 0, meta, tiles, arrived, total)
    core = lax.rem(lax.axis_index("rep"), 2)
    share = rows // 4
    for h in range(2):
        mine = pl.ds(pl.multiple_of((2 * h + core) * share, share), share)
        other = pl.ds(pl.multiple_of((2 * h + 1 - core) * share, share), share)
        keep[h * share : (h + 1) * share, :] = total[mine, :]
        send[h * share : (h + 1) * share, :] = total[other, :].astype(BF16)


def prepare(
    coords, live, tiles, features, cot_own, deg_own, w_self, cot_far, deg_far,
    meta, kept_tiles, own_rows, self_term, cot, inv_root, deg_near, weights, sems,
):
    rep = lax.axis_index("rep")
    core, plane = lax.rem(rep, 2), lax.div(rep, 2)
    share = cot_own.shape[0]
    near = pl.ds(pl.multiple_of(plane * share, share), share)
    away = pl.ds(pl.multiple_of((1 - plane) * share, share), share)
    pairs = [(tiles, kept_tiles), (cot_own, cot.at[near]), (deg_own, deg_near), (w_self, weights)]
    for h in range(2):
        rows = features.at[pl.ds(pl.multiple_of((2 * h + core) * share, share), share)]
        pairs.append((rows, own_rows.at[h * share : (h + 1) * share]))
    copies = [pltpu.make_async_copy(*pair, sems.at[i]) for i, pair in enumerate(pairs)]
    for copy in copies:
        copy.start()
    slots, tile_count = live.shape[1:]
    spare = features.shape[0] // kept_tiles.shape[-1]
    for slot in range(slots):
        for k in range(tile_count):
            at = slot * tile_count + k
            present = live[0, slot, k] != 0
            row, column = coords[0, slot, k, 0], coords[0, slot, k, 1]
            meta[0, at] = jnp.where(present, row, spare)
            meta[1, at] = jnp.where(present, column, spare)
            meta[2, at] = row
            meta[3, at] = column
    for copy in copies:
        copy.wait()
    cot[away, :] = cot_far[...]
    width = inv_root.shape[1]
    for where, deg in ((near, deg_near), (away, deg_far)):
        inv_root[where, :] = jnp.transpose(jnp.broadcast_to(1.0 / jnp.sqrt(deg[...].astype(F32)), (width, share)))
    self_term[...] = dot(own_rows[...], weights[...], ((1,), (0,)))


def middle(chip_sum, far_sum, inv_root, self_term, cot, own_rows, w_self, w_neigh, hidden, own_term, message, kept_grad, grads):
    rep = lax.axis_index("rep")
    core, plane = lax.rem(rep, 2), lax.div(rep, 2)
    half, share = chip_sum.shape[0], hidden.shape[0]
    inv = inv_root[...]
    aggregate = ((chip_sum[...] + far_sum[...].astype(F32)) * inv).astype(BF16)
    preact = self_term[...] + dot(aggregate, w_neigh[...], ((1,), (0,)))
    sig = jax.nn.sigmoid(preact)
    slope = sig * (1.0 + preact * (1.0 - sig))
    grad = (cot[...].astype(F32) * slope).astype(BF16)
    message[:half, :] = (dot(grad, w_neigh[...], ((1,), (1,))) * inv).astype(BF16)
    left = jnp.where(plane == 0, own_rows[...].astype(F32), aggregate.astype(F32)).astype(BF16)
    grads[...] = dot(left, grad, ((0,), (0,)))
    rows = kept_grad.shape[0]
    kept_grad[...] = grads[pl.ds(pl.multiple_of(core * rows, rows), rows), :]
    message[half:, :] = grads[pl.ds(pl.multiple_of((1 - core) * rows, rows), rows), :].astype(BF16)
    value = (preact * sig).astype(BF16)
    term = dot(grad, w_self[...], ((1,), (1,)))

    @pl.when(plane == 0)
    def _():
        hidden[...] = value[:share]
        own_term[...] = term[:share]

    @pl.when(plane != 0)
    def _():
        hidden[...] = value[share:]
        own_term[...] = term[share:]


def backward(meta, tiles, own, other, far_cross, far_same, near_cross, near_same, source, total):
    rep = lax.axis_index("rep")
    core, plane = lax.rem(rep, 2), lax.div(rep, 2)
    share = source.shape[0] // 4
    for h in range(2):
        part = slice(h * share, (h + 1) * share)
        source[pl.ds(pl.multiple_of((2 * h + core) * share, share), share), :] = own[part, :]
        source[pl.ds(pl.multiple_of((2 * h + 1 - core) * share, share), share), :] = other[part, :]
    half = 2 * share
    for slot, cross, same in ((plane, far_cross, far_same), (1 - plane, near_cross, near_same)):
        total[...] = jnp.zeros_like(total)
        place_tiles(slot, 1, meta, tiles, source, total)
        cross[...] = total[pl.ds(pl.multiple_of((1 - plane) * half, half), half), :].astype(BF16)
        same[...] = total[pl.ds(pl.multiple_of(plane * half, half), half), :].astype(BF16)


def local_rep(slots):
    return (slots * lax.axis_size("rep") // 2) // slots


def kernel_call(kernel, name, outs, args, scratch=(), in_specs=None, out_specs=None):
    return pl.pallas_call(
        kernel,
        out_shape=[jax.ShapeDtypeStruct(*out) for out in outs],
        in_specs=in_specs or [VMEM] * len(args),
        out_specs=out_specs or [VMEM] * len(outs),
        scratch_shapes=scratch,
        compiler_params=pltpu.CompilerParams(vmem_limit_bytes=8 * 2**20),
        name=name,
    )(*args)


def on_device(tile_vals, tile_coords, tile_live, features, degree, w_self, w_neigh, cotangent):
    part_total = lax.axis_size("blk")
    rep_count = lax.axis_size("rep")
    rep = lax.axis_index("rep")
    core, plane = rep % 2, rep // 2
    slots, tile_count, tile_size = tile_vals.shape[1:4]
    half_span = slots * rep_count // 2
    rows, dim = features.shape
    half, share = rows // 2, rows // rep_count

    def shift(r, j):
        return slots * r + j - half_span

    def flip_core(value):
        return exchange(value, lambda b, r: (b, r ^ 1))

    def flip_plane(value):
        return exchange(value, lambda b, r: (b, r ^ 2))

    home = local_rep(slots)
    pairs = []
    for part in range(part_total):
        for r in range(rep_count):
            if r == home:
                continue
            giver = home if r == home - 1 else r
            pairs.append((((part + shift(r, 0)) % part_total) * rep_count + giver, part * rep_count + r))
    panel_first = lax.ppermute(features, BOTH, pairs)
    panel_second = exchange(features, lambda b, r: (b - shift(r, 1), r))

    degree = degree.reshape(1, share)
    wide = (half, dim)
    cot_far, deg_far = flip_plane(cotangent), flip_plane(degree)
    raw = [tile_coords, tile_live, tile_vals, features, cotangent, degree, w_self]
    raw = [pltpu.with_memory_space_constraint(a, pltpu.HBM) for a in raw]
    meta, tiles, own_rows, self_term, cot, inv_root = kernel_call(
        prepare,
        "prepare",
        [((4, slots * tile_count), jnp.int32), (tile_vals.shape, BF16), (wide, BF16), (wide, F32), (wide, BF16), (wide, F32)],
        raw + [cot_far, deg_far],
        [pltpu.VMEM((1, share), jnp.int32), pltpu.VMEM(w_self.shape, BF16), pltpu.SemaphoreType.DMA((6,))],
        [SMEM] * 2 + [pl.BlockSpec(memory_space=pltpu.HBM)] * 5 + [VMEM] * 2,
        [SMEM] + [VMEM] * 5,
    )

    source, total = pltpu.VMEM((rows, dim), BF16), pltpu.VMEM((rows + tile_size, dim), F32)
    first = kernel_call(
        forward_first, "forward_first", [((rows, dim), F32)], [meta, tiles, features, panel_first], [source, total],
        [SMEM] + [VMEM] * 3,
    )[0]
    keep, send = kernel_call(
        forward_second, "forward_second", [(wide, F32), (wide, BF16)], [meta, tiles, panel_second, first], [total],
        [SMEM] + [VMEM] * 3,
    )
    chip_sum = keep + flip_core(send).astype(F32)
    far_sum = flip_plane(chip_sum.astype(BF16))

    grad_rows = dim // 2
    hidden, own_term, message, kept_grad = kernel_call(
        middle,
        "middle",
        [((share, dim), BF16), ((share, dim), F32), ((half + grad_rows, dim), BF16), ((grad_rows, dim), F32)],
        [chip_sum, far_sum, inv_root, self_term, cot, own_rows, w_self, w_neigh],
        [pltpu.VMEM((dim, dim), F32)],
    )
    other = flip_core(message)
    sends = kernel_call(
        backward, "backward", [(wide, BF16)] * 4, [meta, tiles, message, other], [source, total], [SMEM] + [VMEM] * 3
    )

    def far(r):
        return shift(r, r // 2)

    def near(r):
        return shift(r, 1 - r // 2)

    arrived = [
        exchange(sends[0], lambda b, r: (b + far(r), r ^ 2)),
        exchange(sends[1], lambda b, r: (b + far(r), r)),
        exchange(sends[2], lambda b, r: (b + near(r), r ^ 2)),
        exchange(sends[3], lambda b, r: (b + near(r), r)),
    ]

    rounded = (kept_grad + other[half:].astype(F32)).astype(BF16)

    def others(value, bit):
        return exchange(value, lambda b, r: (b ^ bit, r)).astype(F32)

    grad = rounded.astype(F32)
    bits = [1 << i for i in range(part_total.bit_length() - 2, -1, -1)]
    for i, bit in enumerate(bits):
        rounded = grad.astype(BF16)
        come = others(rounded, bit)
        if i == 0:
            come, _ = lax.optimization_barrier((come, sends[0]))
        if i == 1:
            come, _ = lax.optimization_barrier((come, arrived[0]))
        grad = rounded.astype(F32) + come
    rounded = grad.astype(BF16)
    twin = flip_plane(rounded)
    by_plane = jnp.where(plane == 0, jnp.stack([rounded, twin]), jnp.stack([twin, rounded]))
    twin = flip_core(by_plane)
    by_core = jnp.where(core == 0, jnp.stack([by_plane, twin], 1), jnp.stack([twin, by_plane], 1))
    grad_scale = 1.0 / math.sqrt(rows * part_total)
    totals = by_core.reshape(2, dim, dim).astype(F32) * grad_scale

    neighbour = sum(a.astype(F32) for a in arrived).reshape(2, share, dim)
    twin = flip_core(lax.dynamic_index_in_dim(neighbour, 1 - core, 0, keepdims=False).astype(BF16))
    neighbour = lax.dynamic_index_in_dim(neighbour, core, 0, keepdims=False) + twin.astype(F32)
    grad_features = (own_term + neighbour).astype(BF16)
    return (hidden, grad_features, totals[0], totals[1])


def solution(mesh):
    return jax.shard_map(
        on_device,
        mesh=mesh,
        in_specs=(
            P("blk", "rep", None, None, None),
            P("blk", "rep", None, None),
            P("blk", "rep", None),
            P("blk", None),
            P(("blk", "rep")),
            P(),
            P(),
            P(("blk", "rep"), None),
        ),
        out_specs=(P(("blk", "rep"), None), P(("blk", "rep"), None), P(), P()),
        check_vma=False,
    )
```

time: 79.5 us -> 63.5 us (0.80)
  starting transfers between devices: 28.5 us -> 19.4 us
  local copies, waits for them, and re-layouts: 7.62 us -> 2.25 us
  waiting for transfers between devices: 26.4 us -> 31.1 us
  Pallas kernels: 11 us -> 8.12 us
  matrix products: 2.88 us -> 0 us
  other arithmetic: 1.89 us -> 0.94 us
    ppermute x20 -> x16, starting transfers between devices: 28.5 us -> 13.3 us  [exchange(): return lax.ppermute(value, BOTH, pairs)]
    ppermute x0 -> x1, starting transfers between devices: none -> 6.08 us  [on_device(): panel_first = lax.ppermute(features, BOTH, pairs)]
    ppermute x20 -> x16, waiting for transfers between devices: 26.4 us -> 31.1 us  [exchange(): return lax.ppermute(value, BOTH, pairs)]
    dot_general x3 -> x0, matrix products: 2.88 us -> none  [the longest x1 1.16 us: on_device(): jnp.einsum('nd,ne->de', left, grad_pre, preferred_element_type=F32)]
    pallas_call x4 -> x5, Pallas kernels: 11 us -> 8.12 us  [kernel_call(): pl.pallas_call(kernel, out_shape=[jax.ShapeDtypeStruct(*out) for out in o...]
    unnamed x25 -> x7, local copies, waits for them, and re-layouts: 3.38 us -> 1.4 us
    slice x1 -> x0, local copies, waits for them, and re-layouts: 1.02 us -> none  [on_device(): low, high = (features[:half], features[half:])]
    add x1 -> x0, other arithmetic: 0.98 us -> none  [on_device(): chip_sum = (keep + flip_core(send).astype(F32)).reshape(half, dim)]
  transfers between devices with their start and end apart: 20 -> 17, of which waited for: 11 -> 12; matrix products, arithmetic and copies ran while one was open for 8% -> 4% of each run, Pallas kernels for 11% -> 9%
where the time goes in v2:
time: 63.5 us; the launch traced here: 62.7 us
  waiting for transfers between devices  31.1 us (49%)
  starting transfers between devices  19.4 us (31%)
  Pallas kernels  8.12 us (13%)
  local copies, waits for them, and re-layouts  2.25 us (4%)
  other arithmetic  0.94 us (1%)
  between operations  0.88 us (1%)
    ppermute x16, waiting for transfers between devices, exchange(): return lax.ppermute(value, BOTH, pairs)  31.1 us
    ppermute x16, starting transfers between devices, exchange(): return lax.ppermute(value, BOTH, pairs)  13.3 us
    pallas_call x5, Pallas kernels, kernel_call(): pl.pallas_call(kernel, out_shape=[jax.ShapeDtypeStruct(*out) for out in o...  8.12 us
    ppermute x1, starting transfers between devices, on_device(): panel_first = lax.ppermute(features, BOTH, pairs)  6.08 us
    unnamed x7, local copies, waits for them, and re-layouts  1.4 us
  transfers between devices with their start and end apart: 17, of which 12 were waited for; matrix products, arithmetic and copies ran while one was open for 4% of the time, Pallas kernels for 9%

profile of v2, /device:TPU:0, one launch (start us, length us, event | category | flops | bytes accessed | tf_op | source)
XLA Modules:
  0.0 62.7 jit_solution(18285829379877589370)
XLA Ops:
  0.6 0.0 copy-start
  0.6 6.1 %collective-permute-start.3 = (bf16[512,256]{1,0:T(8,128)(2,1)}, bf16[512,256]{1,0:T(8,128)(2,1)S(1)}, u32[]{:S(2)}, u32[]{:S(2)}) collective-permute-start(bf16[512,256]{1,0:T(8,128)(2,1)} %local.1), channel_id=1, source_target_pairs={{16,0},{26,1},{11,3},{20,4},{30,5},{15,7},{24,8},{2,9},{19,11},{28... | collective-permute-start | bytes 786440 | tf_op jit(solution)/shard_map/ppermute | solution.py:197
  6.7 2.6 %collective-permute-start.2 = (bf16[512,256]{1,0:T(8,128)(2,1)}, bf16[512,256]{1,0:T(8,128)(2,1)S(1)}, u32[]{:S(2)}, u32[]{:S(2)}) collective-permute-start(bf16[512,256]{1,0:T(8,128)(2,1)} %local.1), channel_id=1, source_target_pairs={{0,12},{1,5},{2,30},{3,23},{4,16},{5,9},{6,2},{7,27},{8,20},{9,13}... | collective-permute-start | bytes 786440 | tf_op jit(solution)/shard_map/ppermute | solution.py:24
  9.3 0.6 collective-permute-start
  9.9 1.5 %collective-permute-start.1 = (s32[1,128]{1,0:T(1,128)}, s32[1,128]{1,0:T(1,128)S(1)}, u32[]{:S(2)}, u32[]{:S(2)}) collective-permute-start(s32[1,128]{1,0:T(1,128)} %bitcast.26), channel_id=1, source_target_pairs={{0,2},{1,3},{2,0},{3,1},{4,6},{5,7},{6,4},{7,5},{8,10},{9,11},{10,... | collective-permute-start | bytes 1544 | tf_op jit(solution)/shard_map/ppermute | solution.py:24
  11.3 1.4 %copy.12.coords = s32[1,2,20,2]{3,2,1,0:T(8,128)} copy(s32[1,2,20,2]{2,3,1,0:T(2,128)} %param.9) | data formatting | bytes 640 | tf_op args[1]
  12.7 1.8 %collective-permute-done.1.deg_far = s32[1,128]{1,0:T(1,128)S(1)} collective-permute-done((s32[1,128]{1,0:T(1,128)}, s32[1,128]{1,0:T(1,128)S(1)}, u32[]{:S(2)}, u32[]{:S(2)}) %collective-permute-start.1) | collective-permute-done | bytes 544 | tf_op jit(solution)/shard_map/ppermute | solution.py:24
  14.5 0.0 collective-permute-done.cot_far
  14.5 3.1 %prepare.1 = (s32[4,40]{1,0:T(4,128)S(1)}, bf16[1,2,20,128,128]{4,3,2,1,0:T(8,128)(2,1)S(1)}, bf16[256,256]{1,0:T(8,128)(2,1)S(1)}, f32[256,256]{1,0:T(8,128)S(1...) custom-call(s32[1,2,20,2]{3,2,1,0:T(8,128)} %copy.12.coords, s32[1,2,20]{2,1,0:T(2,128)} %live.1, ...), custom_call_target="tpu_custom_call" | custom-call | tf_op jit(solution)/shard_map/prepare/pallas_call | solution.py:159
  17.7 0.0 collective-permute-done.3.arrived
  17.7 0.0 copy-done
  17.7 1.1 %forward_first.1.before = f32[512,256]{1,0:T(8,128)S(1)} custom-call(s32[4,40]{1,0:T(4,128)S(1)} %get-tuple-element.22.meta, bf16[1,2,20,128,128]{4,3,2,1,0:T(8,128)(2,1)S(1)} %get-tuple-element.23.tiles, bf16[512,256]{1,0:T(8,128)(2,1)S(1)} %copy-done, bf16[512,256]{1,0:T(8,128)(2,1)S(1)} %collective-permute-done.3.arrived), custom_call_target="tpu_custom_call" | custom-call | tf_op jit(solution)/shard_map/forward_first/pallas_call | solution.py:159
  18.8 0.0 copy-start.1
  18.9 0.0 copy-start.2
  18.9 4.2 %collective-permute-done.2.arrived = bf16[512,256]{1,0:T(8,128)(2,1)S(1)} collective-permute-done((bf16[512,256]{1,0:T(8,128)(2,1)}, bf16[512,256]{1,0:T(8,128)(2,1)S(1)}, u32[]{:S(2)}, u32[]{:S(2)}) %collective-permute-start.2) | collective-permute-done | bytes 262176 | tf_op jit(solution)/shard_map/ppermute | solution.py:24
  23.1 1.1 %forward_second.1 = (f32[256,256]{1,0:T(8,128)S(1)}, bf16[256,256]{1,0:T(8,128)(2,1)S(1)}) custom-call(s32[4,40]{1,0:T(4,128)S(1)} %get-tuple-element.22.meta, bf16[1,2,20,128,128]{4,3,2,1,0:T(8,128)(2,1)S(1)} %get-tuple-element.23.tiles, bf16[512,256]{1,0:T(8,128)(2,1)S(1)} %collective-permute-done.2.arrived, f32[512,256]{1,0:T(8,128)S(1)} %forward_first.1.before), custom_call_target="tpu_custom_call" | custom-call | tf_op jit(solution)/shard_map/forward_second/pallas_call | solution.py:159
  24.2 0.1 collective-permute-start.4
  24.3 1.3 %collective-permute-done.4 = bf16[256,256]{1,0:T(8,128)(2,1)S(1)} collective-permute-done((bf16[256,256]{1,0:T(8,128)(2,1)S(1)}, bf16[256,256]{1,0:T(8,128)(2,1)S(1)}, u32[]{:S(2)}, u32[]{:S(2)}) %collective-permute-start.4) | collective-permute-done | bytes 131104 | tf_op jit(solution)/shard_map/ppermute | solution.py:24
  25.7 0.1 collective-permute-start.5
  25.7 5.5 %collective-permute-done.5.far_sum = bf16[256,256]{1,0:T(8,128)(2,1)S(1)} collective-permute-done((bf16[256,256]{1,0:T(8,128)(2,1)S(1)}, bf16[256,256]{1,0:T(8,128)(2,1)S(1)}, u32[]{:S(2)}, u32[]{:S(2)}) %collective-permute-start.5) | collective-permute-done | bytes 131104 | tf_op jit(solution)/shard_map/ppermute | solution.py:24
  31.3 0.0 copy-done.1
  31.3 0.0 copy-done.2
  31.3 1.1 %middle.1 = (bf16[128,256]{1,0:T(8,128)(2,1)}, f32[128,256]{1,0:T(8,128)S(1)}, bf16[384,256]{1,0:T(8,128)(2,1)S(1)}, f32[128,256]{1,0:T(8,128)S(1)}) custom-call(f32[256,256]{1,0:T(8,128)S(1)} %get-tuple-element.41.chip_sum, bf16[256,256]{1,0:T(8,128)(2,1)S(1)} %collective-permute-done.5.far_sum, f32[256,256]{1,0:T(8,128)S(1)} %get-tuple-element.26.inv_root, ...), custom_call_target="tpu_custom_call" | custom-call | tf_op jit(solution)/shard_map/middle/pallas_call | solution.py:159
  32.4 0.0 collective-permute-start.6
  32.4 1.4 %collective-permute-done.6.other = bf16[384,256]{1,0:T(8,128)(2,1)S(1)} collective-permute-done((bf16[384,256]{1,0:T(8,128)(2,1)S(1)}, bf16[384,256]{1,0:T(8,128)(2,1)S(1)}, u32[]{:S(2)}, u32[]{:S(2)}) %collective-permute-start.6) | collective-permute-done | bytes 196640 | tf_op jit(solution)/shard_map/ppermute | solution.py:24
  33.9 1.1 %collective-permute-start.12 = (bf16[128,256]{1,0:T(8,128)(2,1)S(1)}, bf16[128,256]{1,0:T(8,128)(2,1)S(1)}, u32[]{:S(2)}, u32[]{:S(2)}) collective-permute-start(bf16[128,256]{1,0:T(8,128)(2,1)S(1)} %add_convert_fusion.3), channel_id=1, source_target_pairs={{0,16},{1,17},{2,18},{3,19},{4,20},{5,21},{6,22},{7,23},{8,24},{9,... | collective-permute-start | bytes 196616 | tf_op jit(solution)/shard_map/ppermute | solution.py:24
  35.0 1.6 %backward.1 = (bf16[256,256]{1,0:T(8,128)(2,1)S(1)}, bf16[256,256]{1,0:T(8,128)(2,1)S(1)}, bf16[256,256]{1,0:T(8,128)(2,1)S(1)}, bf16[256,256]{1,0:T(8,128)(2,1)S(1)}) custom-call(s32[4,40]{1,0:T(4,128)S(1)} %get-tuple-element.22.meta, bf16[1,2,20,128,128]{4,3,2,1,0:T(8,128)(2,1)S(1)} %get-tuple-element.23.tiles, ...), custom_call_target="tpu_custom_call" | custom-call | tf_op jit(solution)/shard_map/backward/pallas_call | solution.py:159
  36.6 1.7 %collective-permute-start.7 = (bf16[256,256]{1,0:T(8,128)(2,1)S(1)}, bf16[256,256]{1,0:T(8,128)(2,1)S(1)}, u32[]{:S(2)}, u32[]{:S(2)}) collective-permute-start(bf16[256,256]{1,0:T(8,128)(2,1)S(1)} %get-tuple-element.33), channel_id=1, source_target_pairs={{0,18},{1,27},{2,4},{3,13},{4,22},{5,31},{6,8},{7,17},{8,26},{9,3}... | collective-permute-start | bytes 393224 | tf_op jit(solution)/shard_map/ppermute | solution.py:24
  38.3 1.1 %collective-permute-done.12 = bf16[128,256]{1,0:T(8,128)(2,1)S(1)} collective-permute-done((bf16[128,256]{1,0:T(8,128)(2,1)S(1)}, bf16[128,256]{1,0:T(8,128)(2,1)S(1)}, u32[]{:S(2)}, u32[]{:S(2)}) %collective-permute-start.12) | collective-permute-done | bytes 65568 | tf_op jit(solution)/shard_map/ppermute | solution.py:24
  39.4 0.1 collective-permute-start.13
  39.5 4.9 %collective-permute-start.10 = (bf16[256,256]{1,0:T(8,128)(2,1)S(1)}, bf16[256,256]{1,0:T(8,128)(2,1)S(1)}, u32[]{:S(2)}, u32[]{:S(2)}) collective-permute-start(bf16[256,256]{1,0:T(8,128)(2,1)S(1)} %get-tuple-element.36), channel_id=1, source_target_pairs={{0,20},{1,29},{2,2},{3,11},{4,24},{5,1},{6,6},{7,15},{8,28},{9,5},... | collective-permute-start | bytes 393224 | tf_op jit(solution)/shard_map/ppermute | solution.py:24
  44.4 0.2 collective-permute-start.8
  44.6 0.0 collective-permute-start.9
  44.6 0.1 collective-permute-done.13
  44.7 1.4 %collective-permute-done.7 = bf16[256,256]{1,0:T(8,128)(2,1)S(1)} collective-permute-done((bf16[256,256]{1,0:T(8,128)(2,1)S(1)}, bf16[256,256]{1,0:T(8,128)(2,1)S(1)}, u32[]{:S(2)}, u32[]{:S(2)}) %collective-permute-start.7) | collective-permute-done | bytes 131104 | tf_op jit(solution)/shard_map/ppermute | solution.py:24
  46.1 0.4 collective-permute-start.14
  46.5 1.9 %collective-permute-done.10 = bf16[256,256]{1,0:T(8,128)(2,1)S(1)} collective-permute-done((bf16[256,256]{1,0:T(8,128)(2,1)S(1)}, bf16[256,256]{1,0:T(8,128)(2,1)S(1)}, u32[]{:S(2)}, u32[]{:S(2)}) %collective-permute-start.10) | collective-permute-done | bytes 131104 | tf_op jit(solution)/shard_map/ppermute | solution.py:24
  48.4 7.5 %collective-permute-done.8 = bf16[256,256]{1,0:T(8,128)(2,1)S(1)} collective-permute-done((bf16[256,256]{1,0:T(8,128)(2,1)S(1)}, bf16[256,256]{1,0:T(8,128)(2,1)S(1)}, u32[]{:S(2)}, u32[]{:S(2)}) %collective-permute-start.8) | collective-permute-done | bytes 131104 | tf_op jit(solution)/shard_map/ppermute | solution.py:24
  55.9 0.0 collective-permute-done.9
  55.9 0.1 convert_add_fusion
  56.0 0.0 collective-permute-done.14
  56.0 0.1 collective-permute-start.15
  56.1 0.1 collective-permute-start.11
  56.2 4.1 %collective-permute-done.15 = bf16[128,256]{1,0:T(8,128)(2,1)S(1)} collective-permute-done((bf16[128,256]{1,0:T(8,128)(2,1)S(1)}, bf16[128,256]{1,0:T(8,128)(2,1)S(1)}, u32[]{:S(2)}, u32[]{:S(2)}) %collective-permute-start.15) | collective-permute-done | bytes 65568 | tf_op jit(solution)/shard_map/ppermute | solution.py:24
  60.4 0.1 collective-permute-start.16
  60.4 0.0 collective-permute-done.11
  60.4 0.7 %fusion.1 = bf16[128,256]{1,0:T(8,128)(2,1)} fusion(f32[128,256]{1,0:T(8,128)S(1)} %get-tuple-element.31, bf16[128,256]{1,0:T(8,128)(2,1)S(1)} %collective-permute-done.11, f32[2,128,256]{2,1,0:T(8,128)S(1)} %bitcast.18, s32[]{:T(128)S(6)} %select_n.48), kind=kLoop, calls=%fused_computation.8 | loop fusion | flops 131072 | bytes 393220 | tf_op jit(solution)/shard_map/convert_element_type | solution.py:279
  61.1 0.6 %collective-permute-done.16 = bf16[2,128,256]{2,1,0:T(8,128)(2,1)S(1)} collective-permute-done((bf16[2,128,256]{2,1,0:T(8,128)(2,1)S(1)}, bf16[2,128,256]{2,1,0:T(8,128)(2,1)S(1)}, u32[]{:S(2)}, u32[]{:S(2)}) %collective-permute-start.16) | collective-permute-done | bytes 131104 | tf_op jit(solution)/shard_map/ppermute | solution.py:24
  61.8 0.1 convert_multiply_fusion
  61.8 0.8 %fusion.4 = (f32[1,2,128,256]{3,2,0,1:T(8,128)}, f32[1,2,128,256]{3,2,0,1:T(8,128)}) fusion(f32[2,2,128,256]{3,2,0,1:T(8,128)S(1)} %convert_multiply_fusion), kind=kLoop, calls=%fused_computation.16 | loop fusion | bytes 1048576 | tf_op jit(solution)/shard_map/slice | solution.py:280
  (10 shorter events, 0.2 us)
Async XLA Ops:
  0.6 17.1 %copy-start = (bf16[512,256]{1,0:T(8,128)(2,1)S(1)}, bf16[512,256]{1,0:T(8,128)(2,1)}, u32[]{:S(2)}) copy-start(bf16[512,256]{1,0:T(8,128)(2,1)} %local.1) | copy-start | bytes 786436
  0.6 17.0 %collective-permute-start.3 = (bf16[512,256]{1,0:T(8,128)(2,1)}, bf16[512,256]{1,0:T(8,128)(2,1)S(1)}, u32[]{:S(2)}, u32[]{:S(2)}) collective-permute-start(bf16[512,256]{1,0:T(8,128)(2,1)} %local.1), channel_id=1, source_target_pairs={{16,0},{26,1},{11,3},{20,4},{30,5},{15,7},{24,8},{2,9},{19,11},{28... | collective-permute-start | bytes 786440 | tf_op jit(solution)/shard_map/ppermute | solution.py:197
  6.7 16.3 %collective-permute-start.2 = (bf16[512,256]{1,0:T(8,128)(2,1)}, bf16[512,256]{1,0:T(8,128)(2,1)S(1)}, u32[]{:S(2)}, u32[]{:S(2)}) collective-permute-start(bf16[512,256]{1,0:T(8,128)(2,1)} %local.1), channel_id=1, source_target_pairs={{0,12},{1,5},{2,30},{3,23},{4,16},{5,9},{6,2},{7,27},{8,20},{9,13}... | collective-permute-start | bytes 786440 | tf_op jit(solution)/shard_map/ppermute | solution.py:24
  9.3 5.2 %collective-permute-start = (bf16[128,256]{1,0:T(8,128)(2,1)}, bf16[128,256]{1,0:T(8,128)(2,1)S(1)}, u32[]{:S(2)}, u32[]{:S(2)}) collective-permute-start(bf16[128,256]{1,0:T(8,128)(2,1)} %cot_own.1), channel_id=1, source_target_pairs={{0,2},{1,3},{2,0},{3,1},{4,6},{5,7},{6,4},{7,5},{8,10},{9,11},{10,... | collective-permute-start | bytes 196616 | tf_op jit(solution)/shard_map/ppermute | solution.py:24
  9.9 4.7 %collective-permute-start.1 = (s32[1,128]{1,0:T(1,128)}, s32[1,128]{1,0:T(1,128)S(1)}, u32[]{:S(2)}, u32[]{:S(2)}) collective-permute-start(s32[1,128]{1,0:T(1,128)} %bitcast.26), channel_id=1, source_target_pairs={{0,2},{1,3},{2,0},{3,1},{4,6},{5,7},{6,4},{7,5},{8,10},{9,11},{10,... | collective-permute-start | bytes 1544 | tf_op jit(solution)/shard_map/ppermute | solution.py:24
  18.8 12.4 %copy-start.1 = (bf16[256,256]{1,0:T(8,128)(2,1)S(1)}, bf16[256,256]{1,0:T(8,128)(2,1)}, u32[]{:S(2)}) copy-start(bf16[256,256]{1,0:T(8,128)(2,1)} %w_self.3) | copy-start | bytes 393220
  18.9 12.4 %copy-start.2 = (bf16[256,256]{1,0:T(8,128)(2,1)S(1)}, bf16[256,256]{1,0:T(8,128)(2,1)}, u32[]{:S(2)}) copy-start(bf16[256,256]{1,0:T(8,128)(2,1)} %w_neigh.1) | copy-start | bytes 393220
  24.2 1.4 %collective-permute-start.4 = (bf16[256,256]{1,0:T(8,128)(2,1)S(1)}, bf16[256,256]{1,0:T(8,128)(2,1)S(1)}, u32[]{:S(2)}, u32[]{:S(2)}) collective-permute-start(bf16[256,256]{1,0:T(8,128)(2,1)S(1)} %get-tuple-element.25), channel_id=1, source_target_pairs={{0,1},{1,0},{2,3},{3,2},{4,5},{5,4},{6,7},{7,6},{8,9},{9,8},{10,11... | collective-permute-start | bytes 393224 | tf_op jit(solution)/shard_map/ppermute | solution.py:24
  25.7 5.6 %collective-permute-start.5 = (bf16[256,256]{1,0:T(8,128)(2,1)S(1)}, bf16[256,256]{1,0:T(8,128)(2,1)S(1)}, u32[]{:S(2)}, u32[]{:S(2)}) collective-permute-start(bf16[256,256]{1,0:T(8,128)(2,1)S(1)} %get-tuple-element.40), channel_id=1, source_target_pairs={{0,2},{1,3},{2,0},{3,1},{4,6},{5,7},{6,4},{7,5},{8,10},{9,11},{10,... | collective-permute-start | bytes 393224 | tf_op jit(solution)/shard_map/ppermute | solution.py:24
  32.4 1.4 %collective-permute-start.6 = (bf16[384,256]{1,0:T(8,128)(2,1)S(1)}, bf16[384,256]{1,0:T(8,128)(2,1)S(1)}, u32[]{:S(2)}, u32[]{:S(2)}) collective-permute-start(bf16[384,256]{1,0:T(8,128)(2,1)S(1)} %get-tuple-element.32.own), channel_id=1, source_target_pairs={{0,1},{1,0},{2,3},{3,2},{4,5},{5,4},{6,7},{7,6},{8,9},{9,8},{10,11... | collective-permute-start | bytes 589832 | tf_op jit(solution)/shard_map/ppermute | solution.py:24
  33.9 5.5 %collective-permute-start.12 = (bf16[128,256]{1,0:T(8,128)(2,1)S(1)}, bf16[128,256]{1,0:T(8,128)(2,1)S(1)}, u32[]{:S(2)}, u32[]{:S(2)}) collective-permute-start(bf16[128,256]{1,0:T(8,128)(2,1)S(1)} %add_convert_fusion.3), channel_id=1, source_target_pairs={{0,16},{1,17},{2,18},{3,19},{4,20},{5,21},{6,22},{7,23},{8,24},{9,... | collective-permute-start | bytes 196616 | tf_op jit(solution)/shard_map/ppermute | solution.py:24
  36.6 9.5 %collective-permute-start.7 = (bf16[256,256]{1,0:T(8,128)(2,1)S(1)}, bf16[256,256]{1,0:T(8,128)(2,1)S(1)}, u32[]{:S(2)}, u32[]{:S(2)}) collective-permute-start(bf16[256,256]{1,0:T(8,128)(2,1)S(1)} %get-tuple-element.33), channel_id=1, source_target_pairs={{0,18},{1,27},{2,4},{3,13},{4,22},{5,31},{6,8},{7,17},{8,26},{9,3}... | collective-permute-start | bytes 393224 | tf_op jit(solution)/shard_map/ppermute | solution.py:24
  39.4 5.3 %collective-permute-start.13 = (bf16[128,256]{1,0:T(8,128)(2,1)S(1)}, bf16[128,256]{1,0:T(8,128)(2,1)S(1)}, u32[]{:S(2)}, u32[]{:S(2)}) collective-permute-start(bf16[128,256]{1,0:T(8,128)(2,1)S(1)} %add_convert_fusion.2), channel_id=1, source_target_pairs={{0,8},{1,9},{2,10},{3,11},{4,12},{5,13},{6,14},{7,15},{8,0},{9,1},... | collective-permute-start | bytes 196616 | tf_op jit(solution)/shard_map/ppermute | solution.py:24
  39.5 8.8 %collective-permute-start.10 = (bf16[256,256]{1,0:T(8,128)(2,1)S(1)}, bf16[256,256]{1,0:T(8,128)(2,1)S(1)}, u32[]{:S(2)}, u32[]{:S(2)}) collective-permute-start(bf16[256,256]{1,0:T(8,128)(2,1)S(1)} %get-tuple-element.36), channel_id=1, source_target_pairs={{0,20},{1,29},{2,2},{3,11},{4,24},{5,1},{6,6},{7,15},{8,28},{9,5},... | collective-permute-start | bytes 393224 | tf_op jit(solution)/shard_map/ppermute | solution.py:24
  44.4 11.5 %collective-permute-start.8 = (bf16[256,256]{1,0:T(8,128)(2,1)S(1)}, bf16[256,256]{1,0:T(8,128)(2,1)S(1)}, u32[]{:S(2)}, u32[]{:S(2)}) collective-permute-start(bf16[256,256]{1,0:T(8,128)(2,1)S(1)} %get-tuple-element.34), channel_id=1, source_target_pairs={{0,16},{1,25},{2,6},{3,15},{4,20},{5,29},{6,10},{7,19},{8,24},{9,1... | collective-permute-start | bytes 393224 | tf_op jit(solution)/shard_map/ppermute | solution.py:24
  44.6 11.3 %collective-permute-start.9 = (bf16[256,256]{1,0:T(8,128)(2,1)S(1)}, bf16[256,256]{1,0:T(8,128)(2,1)S(1)}, u32[]{:S(2)}, u32[]{:S(2)}) collective-permute-start(bf16[256,256]{1,0:T(8,128)(2,1)S(1)} %get-tuple-element.35), channel_id=1, source_target_pairs={{0,22},{1,31},{2,0},{3,9},{4,26},{5,3},{6,4},{7,13},{8,30},{9,7},{... | collective-permute-start | bytes 393224 | tf_op jit(solution)/shard_map/ppermute | solution.py:24
  46.1 9.9 %collective-permute-start.14 = (bf16[128,256]{1,0:T(8,128)(2,1)S(1)}, bf16[128,256]{1,0:T(8,128)(2,1)S(1)}, u32[]{:S(2)}, u32[]{:S(2)}) collective-permute-start(bf16[128,256]{1,0:T(8,128)(2,1)S(1)} %add_convert_fusion.1), channel_id=1, source_target_pairs={{0,4},{1,5},{2,6},{3,7},{4,0},{5,1},{6,2},{7,3},{8,12},{9,13},{10,... | collective-permute-start | bytes 196616 | tf_op jit(solution)/shard_map/ppermute | solution.py:24
  56.0 4.3 %collective-permute-start.15 = (bf16[128,256]{1,0:T(8,128)(2,1)S(1)}, bf16[128,256]{1,0:T(8,128)(2,1)S(1)}, u32[]{:S(2)}, u32[]{:S(2)}) collective-permute-start(bf16[128,256]{1,0:T(8,128)(2,1)S(1)} %add_convert_fusion), channel_id=1, source_target_pairs={{0,2},{1,3},{2,0},{3,1},{4,6},{5,7},{6,4},{7,5},{8,10},{9,11},{10,... | collective-permute-start | bytes 196616 | tf_op jit(solution)/shard_map/ppermute | solution.py:24
  56.1 4.3 %collective-permute-start.11 = (bf16[128,256]{1,0:T(8,128)(2,1)S(1)}, bf16[128,256]{1,0:T(8,128)(2,1)S(1)}, u32[]{:S(2)}, u32[]{:S(2)}) collective-permute-start(bf16[128,256]{1,0:T(8,128)(2,1)S(1)} %fusion.2), channel_id=1, source_target_pairs={{0,1},{1,0},{2,3},{3,2},{4,5},{5,4},{6,7},{7,6},{8,9},{9,8},{10,11... | collective-permute-start | bytes 196616 | tf_op jit(solution)/shard_map/ppermute | solution.py:24
  60.4 1.4 %collective-permute-start.16 = (bf16[2,128,256]{2,1,0:T(8,128)(2,1)S(1)}, bf16[2,128,256]{2,1,0:T(8,128)(2,1)S(1)}, u32[]{:S(2)}, u32[]{:S(2)}) collective-permute-start(bf16[2,128,256]{2,1,0:T(8,128)(2,1)S(1)} %maximum_select_fusion.2), channel_id=1, source_target_pairs={{0,1},{1,0},{2,3},{3,2},{4,5},{5,4},{6,7},{7,6},{8,9},{9,8},{10,11... | collective-permute-start | bytes 393224 | tf_op jit(solution)/shard_map/ppermute | solution.py:24

commit v3 on v2

v3 whole, which is shorter than its diff:
```python
import functools
import math

import jax
import jax.numpy as jnp
from jax import lax
from jax.experimental import pallas as pl
from jax.experimental.pallas import tpu as pltpu
from jax.sharding import PartitionSpec as P

BOTH = ("blk", "rep")
PIECES = 1
BF16 = jnp.bfloat16
F32 = jnp.float32
VMEM = pl.BlockSpec(memory_space=pltpu.VMEM)
SMEM = pl.BlockSpec(memory_space=pltpu.SMEM)


def exchange(value, target):
    part_total, rep_count = lax.axis_size("blk"), lax.axis_size("rep")
    pairs = []
    for part in range(part_total):
        for rep in range(rep_count):
            to_part, to_rep = target(part, rep)
            pairs.append((part * rep_count + rep, (to_part % part_total) * rep_count + to_rep))
    return lax.ppermute(value, BOTH, pairs)


def dot(lhs, rhs, contract):
    return lax.dot_general(lhs, rhs, (contract, ((), ())), preferred_element_type=F32)


def place_tiles(slot, out_axis, meta, tiles, source, total):
    size = tiles.shape[-1]
    tile_count = tiles.shape[-3]
    for k in range(tile_count):
        to = meta[out_axis, slot * tile_count + k]
        take = meta[3 - out_axis, slot * tile_count + k]
        block = source[pl.ds(pl.multiple_of(take * size, size), size), :]
        rows = pl.ds(pl.multiple_of(to * size, size), size)
        total[rows, :] += dot(tiles[slot, k], block, ((1 - out_axis,), (0,)))


def forward_first(meta, tiles, arrived, out, total):
    total[...] = jnp.zeros_like(total)
    place_tiles(0, 0, meta, tiles, arrived, total)
    out[...] = total[: out.shape[0], :]


def forward_second(swap, meta, tiles, arrived, panel, before, keep, send, source, total):
    rows = before.shape[0]
    total[:rows, :] = before[...]
    total[rows:, :] = jnp.zeros((total.shape[0] - rows, total.shape[1]), F32)
    is_local = near_is_local(swap, lax.axis_index("blk"), lax.axis_index("rep"))

    @pl.when(is_local)
    def _():
        source[...] = panel[...]

    @pl.when(jnp.logical_not(is_local))
    def _():
        source[...] = arrived[...]

    place_tiles(1, 0, meta, tiles, source, total)
    core = lax.rem(lax.axis_index("rep"), 2)
    share = rows // 4
    for h in range(2):
        mine = pl.ds(pl.multiple_of((2 * h + core) * share, share), share)
        other = pl.ds(pl.multiple_of((2 * h + 1 - core) * share, share), share)
        keep[h * share : (h + 1) * share, :] = total[mine, :]
        send[h * share : (h + 1) * share, :] = total[other, :].astype(BF16)


def prepare(
    swap, coords, live, far_note, tiles, features, cot_own, deg_own, w_self, cot_far, deg_far, *rest,
):
    moved = rest[:-9]
    meta, kept_tiles, panel, self_term, cot, inv_root, deg_near, weights, sems = rest[-9:]
    rep = lax.axis_index("rep")
    core, plane = lax.rem(rep, 2), lax.div(rep, 2)
    share = cot_own.shape[0]
    near = pl.ds(pl.multiple_of(plane * share, share), share)
    away = pl.ds(pl.multiple_of((1 - plane) * share, share), share)
    pairs = [(cot_own, cot.at[near]), (deg_own, deg_near), (w_self, weights), (features, panel)]
    copies = [pltpu.make_async_copy(*pair, sems.at[i]) for i, pair in enumerate(pairs)]
    for copy in copies:
        copy.start()

    swaps = swaps_slot(swap, lax.axis_index("blk"), rep)
    far_moved = jnp.logical_and(swaps, plane == 1)
    near_moved = jnp.logical_and(swaps, plane == 0)
    slot_of = (plane, jnp.where(far_moved, 1, 1 - plane))
    tile_copies = []
    for order, is_moved in enumerate((far_moved, near_moved)):
        place = kept_tiles.at[order]
        here = pltpu.make_async_copy(tiles.at[0, slot_of[order]], place, sems.at[len(tile_copies) + 5])
        tile_copies.append((jnp.logical_not(is_moved), here))
        start = 0
        for piece in moved:
            part = place.at[start : start + piece.shape[0]]
            tile_copies.append((is_moved, pltpu.make_async_copy(piece, part, sems.at[len(tile_copies) + 5])))
            start += piece.shape[0]
    for is_needed, copy in tile_copies:
        pl.when(is_needed)(copy.start)

    tile_count = live.shape[2]
    spare = features.shape[0] // kept_tiles.shape[-1]
    for order, is_moved in enumerate((far_moved, near_moved)):
        slot = slot_of[order]
        for k in range(tile_count):
            at = order * tile_count + k
            row = jnp.where(is_moved, far_note[share + 2 * k], coords[0, slot, k, 0])
            column = jnp.where(is_moved, far_note[share + 2 * k + 1], coords[0, slot, k, 1])
            present = jnp.where(is_moved, far_note[share + 2 * tile_count + k], live[0, slot, k]) != 0
            meta[0, at] = jnp.where(present, row, spare)
            meta[1, at] = jnp.where(present, column, spare)
            meta[2, at] = row
            meta[3, at] = column
    for copy in copies:
        copy.wait()
    cot[away, :] = cot_far[...]
    width = inv_root.shape[1]
    for where, deg in ((near, deg_near[...]), (away, deg_far[:1, :])):
        inv_root[where, :] = jnp.transpose(jnp.broadcast_to(1.0 / jnp.sqrt(deg.astype(F32)), (width, share)))
    for h in range(2):
        rows = panel[pl.ds(pl.multiple_of((2 * h + core) * share, share), share), :]
        self_term[h * share : (h + 1) * share, :] = dot(rows, weights[...], ((1,), (0,)))
    for is_needed, copy in tile_copies:
        pl.when(is_needed)(copy.wait)


def middle(chip_sum, far_sum, inv_root, self_term, cot, panel, w_self, w_neigh, hidden, own_term, message, kept_grad, grads):
    rep = lax.axis_index("rep")
    core, plane = lax.rem(rep, 2), lax.div(rep, 2)
    half, share = chip_sum.shape[0], hidden.shape[0]
    inv = inv_root[...]
    aggregate = ((chip_sum[...] + far_sum[...].astype(F32)) * inv).astype(BF16)
    preact = self_term[...] + dot(aggregate, w_neigh[...], ((1,), (0,)))
    sig = jax.nn.sigmoid(preact)
    slope = sig * (1.0 + preact * (1.0 - sig))
    grad = (cot[...].astype(F32) * slope).astype(BF16)
    message[:half, :] = (dot(grad, w_neigh[...], ((1,), (1,))) * inv).astype(BF16)

    @pl.when(plane == 0)
    def _():
        own = [panel[pl.ds(pl.multiple_of((2 * h + core) * share, share), share), :] for h in range(2)]
        grads[...] = dot(own[0], grad[:share], ((0,), (0,))) + dot(own[1], grad[share:], ((0,), (0,)))

    @pl.when(plane != 0)
    def _():
        grads[...] = dot(aggregate, grad, ((0,), (0,)))

    rows = kept_grad.shape[0]
    kept_grad[...] = grads[pl.ds(pl.multiple_of(core * rows, rows), rows), :]
    message[half:, :] = grads[pl.ds(pl.multiple_of((1 - core) * rows, rows), rows), :].astype(BF16)
    value = (preact * sig).astype(BF16)
    term = dot(grad, w_self[...], ((1,), (1,)))

    @pl.when(plane == 0)
    def _():
        hidden[...] = value[:share]
        own_term[...] = term[:share]

    @pl.when(plane != 0)
    def _():
        hidden[...] = value[share:]
        own_term[...] = term[share:]


def backward(swap, meta, tiles, own, other, far_cross, far_same, near_first, near_last, source, total):
    rep = lax.axis_index("rep")
    core, plane = lax.rem(rep, 2), lax.div(rep, 2)
    share = source.shape[0] // 4
    for h in range(2):
        part = slice(h * share, (h + 1) * share)
        source[pl.ds(pl.multiple_of((2 * h + core) * share, share), share), :] = own[part, :]
        source[pl.ds(pl.multiple_of((2 * h + 1 - core) * share, share), share), :] = other[part, :]
    half = 2 * share
    same_first = home_first(swap, lax.axis_index("blk"), rep)
    to_plane = jnp.where(same_first, plane, 1 - plane)
    for slot, outs in enumerate(((far_cross, far_same), (near_first, near_last))):
        total[...] = jnp.zeros_like(total)
        place_tiles(slot, 1, meta, tiles, source, total)
        first = 1 - plane if slot == 0 else to_plane
        for out, which in zip(outs, (first, 1 - first)):
            out[...] = total[pl.ds(pl.multiple_of(which * half, half), half), :].astype(BF16)


def swaps_slot(swap, part, rep):
    return (part % 2 == 0) & (rep % 2 == 0) & swap


def near_is_local(swap, part, rep):
    return rep == (2 * (part % 2) if swap else 2)


def home_first(swap, part, rep):
    return (rep == 2 * (part % 2)) & swap


def kernel_call(kernel, name, outs, args, scratch=(), in_specs=None, out_specs=None):
    return pl.pallas_call(
        kernel,
        out_shape=[jax.ShapeDtypeStruct(*out) for out in outs],
        in_specs=in_specs or [VMEM] * len(args),
        out_specs=out_specs or [VMEM] * len(outs),
        scratch_shapes=scratch,
        compiler_params=pltpu.CompilerParams(vmem_limit_bytes=8 * 2**20),
        name=name,
    )(*args)


def on_device(tile_vals, tile_coords, tile_live, features, degree, w_self, w_neigh, cotangent):
    part_total = lax.axis_size("blk")
    rep_count = lax.axis_size("rep")
    rep = lax.axis_index("rep")
    core, plane = rep % 2, rep // 2
    slots, tile_count, tile_size = tile_vals.shape[1:4]
    half_span = slots * rep_count // 2
    rows, dim = features.shape
    half, share = rows // 2, rows // rep_count

    swap = part_total == slots * rep_count

    def far(part, r):
        if swap and r == 2 and part % 2 == 0:
            return 1 - half_span
        return slots * r + r // 2 - half_span

    def near(part, r):
        if swap and r in (0, 2) and part % 2 == 0:
            return 0 if r == 0 else 1
        return slots * r + 1 - r // 2 - half_span

    def flip_core(value):
        return exchange(value, lambda b, r: (b, r ^ 1))

    def flip_plane(value):
        return exchange(value, lambda b, r: (b, r ^ 2))

    def fetch(shift):
        pairs = []
        for part in range(part_total):
            for r in range(rep_count):
                if shift(part, r):
                    pairs.append((((part + shift(part, r)) % part_total) * rep_count + r, part * rep_count + r))
        return lax.ppermute(features, BOTH, pairs)

    panel_far, panel_near = fetch(far), fetch(near)

    def note_of(slot):
        parts = [degree, tile_coords[0, slot].reshape(-1), tile_live[0, slot]]
        parts.append(jnp.zeros((2 * share - sum(p.size for p in parts),), jnp.int32))
        return jnp.concatenate(parts)

    far_note = flip_plane(jnp.where(plane == 0, note_of(1), note_of(0)))
    cot_far = flip_plane(cotangent)
    moved = []
    if swap:
        pairs = []
        for part in range(0, part_total, 2):
            pairs += [(part * rep_count, part * rep_count + 2), (part * rep_count + 2, part * rep_count)]
        cuts = [tile_count * i // PIECES for i in range(PIECES + 1)]
        for low, high in zip(cuts, cuts[1:]):
            piece = jnp.where(plane == 0, tile_vals[0, 1, low:high], tile_vals[0, 0, low:high])
            moved.append(lax.ppermute(piece, BOTH, pairs))
    wide = (half, dim)
    raw = [tile_vals, features, cotangent, degree.reshape(1, share), w_self]
    raw = [pltpu.with_memory_space_constraint(a, pltpu.HBM) for a in raw]
    meta, tiles, panel, self_term, cot, inv_root = kernel_call(
        functools.partial(prepare, swap),
        "prepare",
        [((4, slots * tile_count), jnp.int32), (tile_vals.shape[1:], BF16), ((rows, dim), BF16), (wide, F32), (wide, BF16), (wide, F32)],
        [tile_coords, tile_live, far_note] + raw + [cot_far, far_note.reshape(2, share)] + moved,
        [pltpu.VMEM((1, share), jnp.int32), pltpu.VMEM(w_self.shape, BF16), pltpu.SemaphoreType.DMA((7 + 2 * len(moved),))],
        [SMEM] * 3 + [pl.BlockSpec(memory_space=pltpu.HBM)] * 5 + [VMEM] * 2 + [pl.BlockSpec(memory_space=pl.ANY)] * len(moved),
        [SMEM] + [VMEM] * 5,
    )

    source, total = pltpu.VMEM((rows, dim), BF16), pltpu.VMEM((rows + tile_size, dim), F32)
    first = kernel_call(
        forward_first, "forward_first", [((rows, dim), F32)], [meta, tiles, panel_far], [total], [SMEM] + [VMEM] * 2
    )[0]
    keep, send = kernel_call(
        functools.partial(forward_second, swap), "forward_second", [(wide, F32), (wide, BF16)],
        [meta, tiles, panel_near, panel, first], [source, total], [SMEM] + [VMEM] * 4,
    )
    chip_sum = keep + flip_core(send).astype(F32)
    far_sum = flip_plane(chip_sum.astype(BF16))

    grad_rows = dim // 2
    hidden, own_term, message, kept_grad = kernel_call(
        middle,
        "middle",
        [((share, dim), BF16), ((share, dim), F32), ((half + grad_rows, dim), BF16), ((grad_rows, dim), F32)],
        [chip_sum, far_sum, inv_root, self_term, cot, panel, w_self, w_neigh],
        [pltpu.VMEM((dim, dim), F32)],
    )
    other = flip_core(message)
    sends = kernel_call(
        functools.partial(backward, swap), "backward", [(wide, BF16)] * 4, [meta, tiles, message, other], [source, total], [SMEM] + [VMEM] * 3
    )

    def others(value, bit, rep_bit=0):
        return exchange(value, lambda b, r: (b ^ bit, r ^ rep_bit))

    def added(one, two):
        return (one.astype(F32) + two.astype(F32)).astype(BF16)

    def tied(value, *after):
        return lax.optimization_barrier((value,) + after)[0]

    sends = list(sends)
    rounded = (kept_grad + other[half:].astype(F32)).astype(BF16)
    top = part_total.bit_length() - 2
    def near_first(part, r, flip):
        return (part + near(part, r), r if bool(home_first(swap, part, r)) != flip else r ^ 2)

    arrived = [
        exchange(sends[0], lambda b, r: (b + far(b, r), r ^ 2)),
        exchange(sends[1], lambda b, r: (b + far(b, r), r)),
        exchange(sends[2], lambda b, r: near_first(b, r, False)),
        exchange(sends[3], lambda b, r: near_first(b, r, True)),
    ]

    rounded = added(rounded, tied(others(rounded, 1 << top), sends[0]))
    rounded = added(rounded, tied(others(rounded, 2), arrived[0]))
    rounded = added(rounded, tied(others(rounded, 1), arrived[1]))
    twin = flip_plane(rounded)
    by_plane = jnp.where(plane == 0, jnp.stack([rounded, twin]), jnp.stack([twin, rounded]))
    twin = flip_core(by_plane)
    by_core = jnp.where(core == 0, jnp.stack([by_plane, twin], 1), jnp.stack([twin, by_plane], 1))
    grad_scale = 1.0 / math.sqrt(rows * part_total)
    totals = by_core.reshape(2, dim, dim).astype(F32) * grad_scale

    neighbour = sum(a.astype(F32) for a in arrived).reshape(2, share, dim)
    twin = flip_core(lax.dynamic_index_in_dim(neighbour, 1 - core, 0, keepdims=False).astype(BF16))
    neighbour = lax.dynamic_index_in_dim(neighbour, core, 0, keepdims=False) + twin.astype(F32)
    grad_features = (own_term + neighbour).astype(BF16)
    return (hidden, grad_features, totals[0], totals[1])


def solution(mesh):
    return jax.shard_map(
        on_device,
        mesh=mesh,
        in_specs=(
            P("blk", "rep", None, None, None),
            P("blk", "rep", None, None),
            P("blk", "rep", None),
            P("blk", None),
            P(("blk", "rep")),
            P(),
            P(),
            P(("blk", "rep"), None),
        ),
        out_specs=(P(("blk", "rep"), None), P(("blk", "rep"), None), P(), P()),
        check_vma=False,
    )
```

time: 63.5 us -> 59.9 us (0.943)
  waiting for transfers between devices: 31.1 us -> 19 us
  starting transfers between devices: 19.4 us -> 27.5 us
  other arithmetic: 0.94 us -> 2.45 us
  local copies, waits for them, and re-layouts: 2.25 us -> 1.37 us
    ppermute x16 -> x15, waiting for transfers between devices: 31.1 us -> 19 us  [exchange(): return lax.ppermute(value, BOTH, pairs)]
    ppermute x16 -> x15, starting transfers between devices: 13.3 us -> 18.3 us  [exchange(): return lax.ppermute(value, BOTH, pairs)]
    ppermute x1 -> x3, starting transfers between devices: 6.08 us -> 9.23 us  [the longest x1 4.85 us: on_device(): moved.append(lax.ppermute(piece, BOTH, pairs))]
    select_n x0 -> x2, other arithmetic: none -> 1.52 us  [the longest x1 1.44 us: on_device(): jnp.where(plane == 0, tile_vals[0, 1, low:high], tile_vals[0, 0, low:high])]
    unnamed x7 -> x15, local copies, waits for them, and re-layouts: 1.4 us -> 0.14 us
  transfers between devices with their start and end apart: 17 -> 18, of which waited for: 12 -> 11; matrix products, arithmetic and copies ran while one was open for 4% -> 2% of each run, Pallas kernels for 9% -> 10%
where the time goes in v3:
time: 59.9 us; the launch traced here: 59.7 us
  starting transfers between devices  27.5 us (46%)
  waiting for transfers between devices  19 us (32%)
  Pallas kernels  8.38 us (14%)
  other arithmetic  2.45 us (4%)
  local copies, waits for them, and re-layouts  1.37 us (2%)
  between operations  0.91 us (2%)
    ppermute x15, waiting for transfers between devices, exchange(): return lax.ppermute(value, BOTH, pairs)  19 us
    ppermute x15, starting transfers between devices, exchange(): return lax.ppermute(value, BOTH, pairs)  18.3 us
    pallas_call x5, Pallas kernels, kernel_call(): pl.pallas_call(kernel, out_shape=[jax.ShapeDtypeStruct(*out) for out in o...  8.38 us
    ppermute x1, starting transfers between devices, on_device(): moved.append(lax.ppermute(piece, BOTH, pairs))  4.85 us
    ppermute x2, starting transfers between devices, fetch(): return lax.ppermute(features, BOTH, pairs)  4.38 us
    select_n x1, other arithmetic, on_device(): jnp.where(plane == 0, tile_vals[0, 1, low:high], tile_vals[0, 0, low:high])  1.44 us
  transfers between devices with their start and end apart: 18, of which 11 were waited for; matrix products, arithmetic and copies ran while one was open for 2% of the time, Pallas kernels for 10%

profile of v3, /device:TPU:0, one launch (start us, length us, event | category | flops | bytes accessed | tf_op | source)
XLA Modules:
  0.0 59.7 jit_solution(3758279672881051572)
XLA Ops:
  0.6 0.0 copy-start.3
  0.6 0.0 copy-start.4
  0.7 0.0 copy-start.5
  0.7 0.0 copy-start.2
  0.7 0.0 copy-start.6
  0.7 1.4 %select_bitcast_fusion = bf16[20,128,128]{2,1,0:T(8,128)(2,1)S(1)} fusion(bf16[1,2,20,128,128]{4,3,2,1,0:T(8,128)(2,1)} %tiles.1, pred[]{:T(512)S(6)} %eq.10), kind=kLoop, calls=%fused_computation | loop fusion | flops 327680 | bytes 1966081 | tf_op jit(solution)/shard_map/jit(_where)/select_n | solution.py:265
  2.1 4.8 %collective-permute-start.2 = (bf16[20,128,128]{2,1,0:T(8,128)(2,1)S(1)}, bf16[20,128,128]{2,1,0:T(8,128)(2,1)S(1)}, u32[]{:S(2)}, u32[]{:S(2)}) collective-permute-start(bf16[20,128,128]{2,1,0:T(8,128)(2,1)S(1)} %select_bitcast_fusion), channel_id=1, source_target_pairs={{0,2},{2,0},{8,10},{10,8},{16,18},{18,16},{24,26},{26,24}} | collective-permute-start | bytes 1966088 | tf_op jit(solution)/shard_map/ppermute | solution.py:266
  7.0 0.0 copy-done.3
  7.0 2.6 %collective-permute-start.4 = (bf16[512,256]{1,0:T(8,128)(2,1)S(1)}, bf16[512,256]{1,0:T(8,128)(2,1)S(1)}, u32[]{:S(2)}, u32[]{:S(2)}) collective-permute-start(bf16[512,256]{1,0:T(8,128)(2,1)S(1)} %copy-done.3), channel_id=1, source_target_pairs={{16,0},{25,1},{22,2},{15,3},{20,4},{29,5},{10,6},{19,7},{24,8},{1,... | collective-permute-start | bytes 786440 | tf_op jit(solution)/shard_map/ppermute | solution.py:247
  9.7 1.7 %collective-permute-start.3 = (bf16[512,256]{1,0:T(8,128)(2,1)S(1)}, bf16[512,256]{1,0:T(8,128)(2,1)S(1)}, u32[]{:S(2)}, u32[]{:S(2)}) collective-permute-start(bf16[512,256]{1,0:T(8,128)(2,1)S(1)} %copy-done.3), channel_id=1, source_target_pairs={{29,1},{6,2},{11,3},{24,4},{1,5},{15,7},{5,9},{14,10},{19,11},{0,1... | collective-permute-start | bytes 786440 | tf_op jit(solution)/shard_map/ppermute | solution.py:247
  11.4 0.0 copy-done.4
  11.4 0.4 collective-permute-start.1
  11.8 0.0 copy-done.5
  11.8 0.1 copy.15
  11.9 0.1 reshape_squeeze.6
  12.0 0.1 copy.16
  12.1 0.1 reshape_squeeze.7
  12.2 0.0 copy-done.6
  12.2 0.1 fusion.5
  12.3 1.7 %collective-permute-start = (s32[256]{0:T(256)S(1)}, s32[256]{0:T(256)S(1)}, u32[]{:S(2)}, u32[]{:S(2)}) collective-permute-start(s32[256]{0:T(256)S(1)} %fusion.5), channel_id=1, source_target_pairs={{0,2},{1,3},{2,0},{3,1},{4,6},{5,7},{6,4},{7,5},{8,10},{9,11},{10,... | collective-permute-start | bytes 3080 | tf_op jit(solution)/shard_map/ppermute | solution.py:26
  14.0 0.1 copy.17.coords
  14.1 2.9 %collective-permute-done.far_note = s32[256]{0:T(256)S(1)} collective-permute-done((s32[256]{0:T(256)S(1)}, s32[256]{0:T(256)S(1)}, u32[]{:S(2)}, u32[]{:S(2)}) %collective-permute-start) | collective-permute-done | bytes 1056 | tf_op jit(solution)/shard_map/ppermute | solution.py:26
  17.0 0.0 collective-permute-done.1.cot_far
  17.0 0.0 collective-permute-done.2.rest_0_
  17.0 3.0 %prepare.1 = (s32[4,40]{1,0:T(4,128)S(1)}, bf16[2,20,128,128]{3,2,1,0:T(8,128)(2,1)S(1)}, bf16[512,256]{1,0:T(8,128)(2,1)S(1)}, f32[256,256]{1,0:T(8,128)S(1)}, ...) custom-call(s32[1,2,20,2]{3,2,1,0:T(8,128)S(1)} %copy.17.coords, s32[1,2,20]{2,1,0:T(2,128)S(1)} %copy-done.2, ...), custom_call_target="tpu_custom_call" | custom-call | tf_op jit(solution)/shard_map/prepare/pallas_call | solution.py:202
  20.0 0.0 collective-permute-done.4.arrived
  20.0 1.1 %forward_first.1.before = f32[512,256]{1,0:T(8,128)S(1)} custom-call(s32[4,40]{1,0:T(4,128)S(1)} %get-tuple-element.23.meta, bf16[2,20,128,128]{3,2,1,0:T(8,128)(2,1)S(1)} %get-tuple-element.24.tiles, bf16[512,256]{1,0:T(8,128)(2,1)S(1)} %collective-permute-done.4.arrived), custom_call_target="tpu_custom_call" | custom-call | tf_op jit(solution)/shard_map/forward_first/pallas_call | solution.py:202
  21.1 0.0 collective-permute-done.3.arrived
  21.1 0.0 copy-start
  21.2 0.0 copy-start.1
  21.2 1.2 %forward_second.1 = (f32[256,256]{1,0:T(8,128)S(1)}, bf16[256,256]{1,0:T(8,128)(2,1)S(1)}) custom-call(s32[4,40]{1,0:T(4,128)S(1)} %get-tuple-element.23.meta, bf16[2,20,128,128]{3,2,1,0:T(8,128)(2,1)S(1)} %get-tuple-element.24.tiles, bf16[512,256]{1,0:T(8,128)(2,1)S(1)} %collective-permute-done.3.arrived, bf16[512,256]{1,0:T(8,128)(2,1)S(1)} %get-tuple-element.25.panel, ...), custom_call_target="tpu_custom_call" | custom-call | tf_op jit(solution)/shard_map/forward_second/pallas_call | solution.py:202
  22.4 0.1 collective-permute-start.5
  22.4 1.3 %collective-permute-done.5 = bf16[256,256]{1,0:T(8,128)(2,1)S(1)} collective-permute-done((bf16[256,256]{1,0:T(8,128)(2,1)S(1)}, bf16[256,256]{1,0:T(8,128)(2,1)S(1)}, u32[]{:S(2)}, u32[]{:S(2)}) %collective-permute-start.5) | collective-permute-done | bytes 131104 | tf_op jit(solution)/shard_map/ppermute | solution.py:26
  23.8 2.1 %collective-permute-start.6 = (bf16[256,256]{1,0:T(8,128)(2,1)S(1)}, bf16[256,256]{1,0:T(8,128)(2,1)S(1)}, u32[]{:S(2)}, u32[]{:S(2)}) collective-permute-start(bf16[256,256]{1,0:T(8,128)(2,1)S(1)} %get-tuple-element.42), channel_id=1, source_target_pairs={{0,2},{1,3},{2,0},{3,1},{4,6},{5,7},{6,4},{7,5},{8,10},{9,11},{10,... | collective-permute-start | bytes 393224 | tf_op jit(solution)/shard_map/ppermute | solution.py:26
  26.0 3.8 %collective-permute-done.6.far_sum = bf16[256,256]{1,0:T(8,128)(2,1)S(1)} collective-permute-done((bf16[256,256]{1,0:T(8,128)(2,1)S(1)}, bf16[256,256]{1,0:T(8,128)(2,1)S(1)}, u32[]{:S(2)}, u32[]{:S(2)}) %collective-permute-start.6) | collective-permute-done | bytes 131104 | tf_op jit(solution)/shard_map/ppermute | solution.py:26
  29.8 0.0 copy-done.1
  29.8 1.5 %middle.1 = (bf16[128,256]{1,0:T(8,128)(2,1)}, f32[128,256]{1,0:T(8,128)S(1)}, bf16[384,256]{1,0:T(8,128)(2,1)S(1)}, f32[128,256]{1,0:T(8,128)S(1)}) custom-call(f32[256,256]{1,0:T(8,128)S(1)} %get-tuple-element.43.chip_sum, bf16[256,256]{1,0:T(8,128)(2,1)S(1)} %collective-permute-done.6.far_sum, f32[256,256]{1,0:T(8,128)S(1)} %get-tuple-element.28.inv_root, ...), custom_call_target="tpu_custom_call" | custom-call | tf_op jit(solution)/shard_map/middle/pallas_call | solution.py:202
  31.3 0.0 collective-permute-start.7
  31.3 1.4 %collective-permute-done.7.other = bf16[384,256]{1,0:T(8,128)(2,1)S(1)} collective-permute-done((bf16[384,256]{1,0:T(8,128)(2,1)S(1)}, bf16[384,256]{1,0:T(8,128)(2,1)S(1)}, u32[]{:S(2)}, u32[]{:S(2)}) %collective-permute-start.7) | collective-permute-done | bytes 196640 | tf_op jit(solution)/shard_map/ppermute | solution.py:26
  32.7 2.8 %collective-permute-start.13 = (bf16[128,256]{1,0:T(8,128)(2,1)S(1)}, bf16[128,256]{1,0:T(8,128)(2,1)S(1)}, u32[]{:S(2)}, u32[]{:S(2)}) collective-permute-start(bf16[128,256]{1,0:T(8,128)(2,1)S(1)} %add_convert_fusion.3), channel_id=1, source_target_pairs={{0,16},{1,17},{2,18},{3,19},{4,20},{5,21},{6,22},{7,23},{8,24},{9,... | collective-permute-start | bytes 196616 | tf_op jit(solution)/shard_map/ppermute | solution.py:26
  35.6 1.6 %backward.1 = (bf16[256,256]{1,0:T(8,128)(2,1)S(1)}, bf16[256,256]{1,0:T(8,128)(2,1)S(1)}, bf16[256,256]{1,0:T(8,128)(2,1)S(1)}, bf16[256,256]{1,0:T(8,128)(2,1)S(1)}) custom-call(s32[4,40]{1,0:T(4,128)S(1)} %get-tuple-element.23.meta, bf16[2,20,128,128]{3,2,1,0:T(8,128)(2,1)S(1)} %get-tuple-element.24.tiles, bf16[384,256]{1,0:T(8,128)(2,1)S(1)} %get-tuple-element.33.own, ...), custom_call_target="tpu_custom_call" | custom-call | tf_op jit(solution)/shard_map/backward/pallas_call | solution.py:202
  37.2 1.4 %collective-permute-start.8 = (bf16[256,256]{1,0:T(8,128)(2,1)S(1)}, bf16[256,256]{1,0:T(8,128)(2,1)S(1)}, u32[]{:S(2)}, u32[]{:S(2)}) collective-permute-start(bf16[256,256]{1,0:T(8,128)(2,1)S(1)} %get-tuple-element.34), channel_id=1, source_target_pairs={{0,18},{1,27},{2,20},{3,13},{4,22},{5,31},{6,8},{7,17},{8,26},{9,3... | collective-permute-start | bytes 393224 | tf_op jit(solution)/shard_map/ppermute | solution.py:26
  38.6 0.8 %collective-permute-done.13 = bf16[128,256]{1,0:T(8,128)(2,1)S(1)} collective-permute-done((bf16[128,256]{1,0:T(8,128)(2,1)S(1)}, bf16[128,256]{1,0:T(8,128)(2,1)S(1)}, u32[]{:S(2)}, u32[]{:S(2)}) %collective-permute-start.13) | collective-permute-done | bytes 65568 | tf_op jit(solution)/shard_map/ppermute | solution.py:26
  39.4 0.8 %collective-permute-start.14 = (bf16[128,256]{1,0:T(8,128)(2,1)S(1)}, bf16[128,256]{1,0:T(8,128)(2,1)S(1)}, u32[]{:S(2)}, u32[]{:S(2)}) collective-permute-start(bf16[128,256]{1,0:T(8,128)(2,1)S(1)} %add_convert_fusion.2), channel_id=1, source_target_pairs={{0,8},{1,9},{2,10},{3,11},{4,12},{5,13},{6,14},{7,15},{8,0},{9,1},... | collective-permute-start | bytes 196616 | tf_op jit(solution)/shard_map/ppermute | solution.py:26
  40.2 3.3 %collective-permute-start.9 = (bf16[256,256]{1,0:T(8,128)(2,1)S(1)}, bf16[256,256]{1,0:T(8,128)(2,1)S(1)}, u32[]{:S(2)}, u32[]{:S(2)}) collective-permute-start(bf16[256,256]{1,0:T(8,128)(2,1)S(1)} %get-tuple-element.35), channel_id=1, source_target_pairs={{0,16},{1,25},{2,22},{3,15},{4,20},{5,29},{6,10},{7,19},{8,24},{9,... | collective-permute-start | bytes 393224 | tf_op jit(solution)/shard_map/ppermute | solution.py:26
  43.6 0.7 %collective-permute-start.10 = (bf16[256,256]{1,0:T(8,128)(2,1)S(1)}, bf16[256,256]{1,0:T(8,128)(2,1)S(1)}, u32[]{:S(2)}, u32[]{:S(2)}) collective-permute-start(bf16[256,256]{1,0:T(8,128)(2,1)S(1)} %get-tuple-element.36), channel_id=1, source_target_pairs={{0,0},{1,31},{2,4},{3,9},{4,26},{5,3},{6,6},{7,13},{8,8},{9,7},{10... | collective-permute-start | bytes 393224 | tf_op jit(solution)/shard_map/ppermute | solution.py:26
  44.2 2.5 %collective-permute-start.11 = (bf16[256,256]{1,0:T(8,128)(2,1)S(1)}, bf16[256,256]{1,0:T(8,128)(2,1)S(1)}, u32[]{:S(2)}, u32[]{:S(2)}) collective-permute-start(bf16[256,256]{1,0:T(8,128)(2,1)S(1)} %get-tuple-element.37), channel_id=1, source_target_pairs={{0,2},{1,29},{2,6},{3,11},{4,24},{5,1},{6,4},{7,15},{8,10},{9,5},{... | collective-permute-start | bytes 393224 | tf_op jit(solution)/shard_map/ppermute | solution.py:26
  46.7 0.5 collective-permute-done.8
  47.2 0.0 collective-permute-done.14
  47.2 1.4 %collective-permute-start.15 = (bf16[128,256]{1,0:T(8,128)(2,1)S(1)}, bf16[128,256]{1,0:T(8,128)(2,1)S(1)}, u32[]{:S(2)}, u32[]{:S(2)}) collective-permute-start(bf16[128,256]{1,0:T(8,128)(2,1)S(1)} %add_convert_fusion.1), channel_id=1, source_target_pairs={{0,4},{1,5},{2,6},{3,7},{4,0},{5,1},{6,2},{7,3},{8,12},{9,13},{10,... | collective-permute-start | bytes 196616 | tf_op jit(solution)/shard_map/ppermute | solution.py:26
  48.6 1.9 %collective-permute-done.9 = bf16[256,256]{1,0:T(8,128)(2,1)S(1)} collective-permute-done((bf16[256,256]{1,0:T(8,128)(2,1)S(1)}, bf16[256,256]{1,0:T(8,128)(2,1)S(1)}, u32[]{:S(2)}, u32[]{:S(2)}) %collective-permute-start.9) | collective-permute-done | bytes 131104 | tf_op jit(solution)/shard_map/ppermute | solution.py:26
  50.6 0.0 collective-permute-done.10
  50.6 2.2 %collective-permute-done.11 = bf16[256,256]{1,0:T(8,128)(2,1)S(1)} collective-permute-done((bf16[256,256]{1,0:T(8,128)(2,1)S(1)}, bf16[256,256]{1,0:T(8,128)(2,1)S(1)}, u32[]{:S(2)}, u32[]{:S(2)}) %collective-permute-start.11) | collective-permute-done | bytes 131104 | tf_op jit(solution)/shard_map/ppermute | solution.py:26
  52.8 0.1 convert_add_fusion
  52.9 0.1 collective-permute-done.15
  53.0 0.9 %collective-permute-start.16 = (bf16[128,256]{1,0:T(8,128)(2,1)S(1)}, bf16[128,256]{1,0:T(8,128)(2,1)S(1)}, u32[]{:S(2)}, u32[]{:S(2)}) collective-permute-start(bf16[128,256]{1,0:T(8,128)(2,1)S(1)} %add_convert_fusion), channel_id=1, source_target_pairs={{0,2},{1,3},{2,0},{3,1},{4,6},{5,7},{6,4},{7,5},{8,10},{9,11},{10,... | collective-permute-start | bytes 196616 | tf_op jit(solution)/shard_map/ppermute | solution.py:26
  53.9 0.1 collective-permute-start.12
  54.0 3.3 %collective-permute-done.16 = bf16[128,256]{1,0:T(8,128)(2,1)S(1)} collective-permute-done((bf16[128,256]{1,0:T(8,128)(2,1)S(1)}, bf16[128,256]{1,0:T(8,128)(2,1)S(1)}, u32[]{:S(2)}, u32[]{:S(2)}) %collective-permute-start.16) | collective-permute-done | bytes 65568 | tf_op jit(solution)/shard_map/ppermute | solution.py:26
  57.4 0.1 collective-permute-start.17
  57.4 0.0 collective-permute-done.12
  57.4 0.7 %fusion.1 = bf16[128,256]{1,0:T(8,128)(2,1)} fusion(f32[128,256]{1,0:T(8,128)S(1)} %get-tuple-element.32, bf16[128,256]{1,0:T(8,128)(2,1)S(1)} %collective-permute-done.12, f32[2,128,256]{2,1,0:T(8,128)S(1)} %bitcast.26, s32[]{:T(128)S(6)} %select_n.73), kind=kLoop, calls=%fused_computation.9 | loop fusion | flops 131072 | bytes 393220 | tf_op jit(solution)/shard_map/convert_element_type | solution.py:339
  58.1 0.6 %collective-permute-done.17 = bf16[2,128,256]{2,1,0:T(8,128)(2,1)S(1)} collective-permute-done((bf16[2,128,256]{2,1,0:T(8,128)(2,1)S(1)}, bf16[2,128,256]{2,1,0:T(8,128)(2,1)S(1)}, u32[]{:S(2)}, u32[]{:S(2)}) %collective-permute-start.17) | collective-permute-done | bytes 131104 | tf_op jit(solution)/shard_map/ppermute | solution.py:26
  58.8 0.1 convert_multiply_fusion
  58.8 0.8 %fusion.7 = (f32[1,2,128,256]{3,2,0,1:T(8,128)}, f32[1,2,128,256]{3,2,0,1:T(8,128)}) fusion(f32[2,2,128,256]{3,2,0,1:T(8,128)S(1)} %convert_multiply_fusion), kind=kLoop, calls=%fused_computation.26 | loop fusion | bytes 1048576 | tf_op jit(solution)/shard_map/slice | solution.py:340
  (13 shorter events, 0.2 us)
Async XLA Ops:
  0.6 6.4 %copy-start.3 = (bf16[512,256]{1,0:T(8,128)(2,1)S(1)}, bf16[512,256]{1,0:T(8,128)(2,1)}, u32[]{:S(2)}) copy-start(bf16[512,256]{1,0:T(8,128)(2,1)} %features.1) | copy-start | bytes 786436
  0.6 10.8 %copy-start.4 = (bf16[128,256]{1,0:T(8,128)(2,1)S(1)}, bf16[128,256]{1,0:T(8,128)(2,1)}, u32[]{:S(2)}) copy-start(bf16[128,256]{1,0:T(8,128)(2,1)} %cot_own.1) | copy-start | bytes 196612
  0.7 11.1 %copy-start.5 = (s32[1,2,20,2]{2,3,1,0:T(2,128)S(1)}, s32[1,2,20,2]{2,3,1,0:T(2,128)}, u32[]{:S(2)}) copy-start(s32[1,2,20,2]{2,3,1,0:T(2,128)} %param.9) | copy-start | bytes 964
  0.7 11.5 %copy-start.2 = (s32[1,2,20]{2,1,0:T(2,128)S(1)}, s32[1,2,20]{2,1,0:T(2,128)}, u32[]{:S(2)}) copy-start(s32[1,2,20]{2,1,0:T(2,128)} %live.1) | copy-start | bytes 484
  0.7 11.5 %copy-start.6 = (s32[128]{0:T(128)S(1)}, s32[128]{0:T(128)}, u32[]{:S(2)}) copy-start(s32[128]{0:T(128)} %param.12) | copy-start | bytes 1540
  2.1 14.9 %collective-permute-start.2 = (bf16[20,128,128]{2,1,0:T(8,128)(2,1)S(1)}, bf16[20,128,128]{2,1,0:T(8,128)(2,1)S(1)}, u32[]{:S(2)}, u32[]{:S(2)}) collective-permute-start(bf16[20,128,128]{2,1,0:T(8,128)(2,1)S(1)} %select_bitcast_fusion), channel_id=1, source_target_pairs={{0,2},{2,0},{8,10},{10,8},{16,18},{18,16},{24,26},{26,24}} | collective-permute-start | bytes 1966088 | tf_op jit(solution)/shard_map/ppermute | solution.py:266
  7.0 13.0 %collective-permute-start.4 = (bf16[512,256]{1,0:T(8,128)(2,1)S(1)}, bf16[512,256]{1,0:T(8,128)(2,1)S(1)}, u32[]{:S(2)}, u32[]{:S(2)}) collective-permute-start(bf16[512,256]{1,0:T(8,128)(2,1)S(1)} %copy-done.3), channel_id=1, source_target_pairs={{16,0},{25,1},{22,2},{15,3},{20,4},{29,5},{10,6},{19,7},{24,8},{1,... | collective-permute-start | bytes 786440 | tf_op jit(solution)/shard_map/ppermute | solution.py:247
  9.7 11.5 %collective-permute-start.3 = (bf16[512,256]{1,0:T(8,128)(2,1)S(1)}, bf16[512,256]{1,0:T(8,128)(2,1)S(1)}, u32[]{:S(2)}, u32[]{:S(2)}) collective-permute-start(bf16[512,256]{1,0:T(8,128)(2,1)S(1)} %copy-done.3), channel_id=1, source_target_pairs={{29,1},{6,2},{11,3},{24,4},{1,5},{15,7},{5,9},{14,10},{19,11},{0,1... | collective-permute-start | bytes 786440 | tf_op jit(solution)/shard_map/ppermute | solution.py:247
  11.4 5.6 %collective-permute-start.1 = (bf16[128,256]{1,0:T(8,128)(2,1)S(1)}, bf16[128,256]{1,0:T(8,128)(2,1)S(1)}, u32[]{:S(2)}, u32[]{:S(2)}) collective-permute-start(bf16[128,256]{1,0:T(8,128)(2,1)S(1)} %copy-done.4), channel_id=1, source_target_pairs={{0,2},{1,3},{2,0},{3,1},{4,6},{5,7},{6,4},{7,5},{8,10},{9,11},{10,... | collective-permute-start | bytes 196616 | tf_op jit(solution)/shard_map/ppermute | solution.py:26
  12.3 4.7 %collective-permute-start = (s32[256]{0:T(256)S(1)}, s32[256]{0:T(256)S(1)}, u32[]{:S(2)}, u32[]{:S(2)}) collective-permute-start(s32[256]{0:T(256)S(1)} %fusion.5), channel_id=1, source_target_pairs={{0,2},{1,3},{2,0},{3,1},{4,6},{5,7},{6,4},{7,5},{8,10},{9,11},{10,... | collective-permute-start | bytes 3080 | tf_op jit(solution)/shard_map/ppermute | solution.py:26
  21.1 8.6 %copy-start = (bf16[256,256]{1,0:T(8,128)(2,1)S(1)}, bf16[256,256]{1,0:T(8,128)(2,1)}, u32[]{:S(2)}) copy-start(bf16[256,256]{1,0:T(8,128)(2,1)} %w_self.3) | copy-start | bytes 393220
  21.2 8.6 %copy-start.1 = (bf16[256,256]{1,0:T(8,128)(2,1)S(1)}, bf16[256,256]{1,0:T(8,128)(2,1)}, u32[]{:S(2)}) copy-start(bf16[256,256]{1,0:T(8,128)(2,1)} %w_neigh.1) | copy-start | bytes 393220
  22.4 1.4 %collective-permute-start.5 = (bf16[256,256]{1,0:T(8,128)(2,1)S(1)}, bf16[256,256]{1,0:T(8,128)(2,1)S(1)}, u32[]{:S(2)}, u32[]{:S(2)}) collective-permute-start(bf16[256,256]{1,0:T(8,128)(2,1)S(1)} %get-tuple-element.27), channel_id=1, source_target_pairs={{0,1},{1,0},{2,3},{3,2},{4,5},{5,4},{6,7},{7,6},{8,9},{9,8},{10,11... | collective-permute-start | bytes 393224 | tf_op jit(solution)/shard_map/ppermute | solution.py:26
  23.8 5.9 %collective-permute-start.6 = (bf16[256,256]{1,0:T(8,128)(2,1)S(1)}, bf16[256,256]{1,0:T(8,128)(2,1)S(1)}, u32[]{:S(2)}, u32[]{:S(2)}) collective-permute-start(bf16[256,256]{1,0:T(8,128)(2,1)S(1)} %get-tuple-element.42), channel_id=1, source_target_pairs={{0,2},{1,3},{2,0},{3,1},{4,6},{5,7},{6,4},{7,5},{8,10},{9,11},{10,... | collective-permute-start | bytes 393224 | tf_op jit(solution)/shard_map/ppermute | solution.py:26
  31.3 1.4 %collective-permute-start.7 = (bf16[384,256]{1,0:T(8,128)(2,1)S(1)}, bf16[384,256]{1,0:T(8,128)(2,1)S(1)}, u32[]{:S(2)}, u32[]{:S(2)}) collective-permute-start(bf16[384,256]{1,0:T(8,128)(2,1)S(1)} %get-tuple-element.33.own), channel_id=1, source_target_pairs={{0,1},{1,0},{2,3},{3,2},{4,5},{5,4},{6,7},{7,6},{8,9},{9,8},{10,11... | collective-permute-start | bytes 589832 | tf_op jit(solution)/shard_map/ppermute | solution.py:26
  32.7 6.6 %collective-permute-start.13 = (bf16[128,256]{1,0:T(8,128)(2,1)S(1)}, bf16[128,256]{1,0:T(8,128)(2,1)S(1)}, u32[]{:S(2)}, u32[]{:S(2)}) collective-permute-start(bf16[128,256]{1,0:T(8,128)(2,1)S(1)} %add_convert_fusion.3), channel_id=1, source_target_pairs={{0,16},{1,17},{2,18},{3,19},{4,20},{5,21},{6,22},{7,23},{8,24},{9,... | collective-permute-start | bytes 196616 | tf_op jit(solution)/shard_map/ppermute | solution.py:26
  37.2 10.0 %collective-permute-start.8 = (bf16[256,256]{1,0:T(8,128)(2,1)S(1)}, bf16[256,256]{1,0:T(8,128)(2,1)S(1)}, u32[]{:S(2)}, u32[]{:S(2)}) collective-permute-start(bf16[256,256]{1,0:T(8,128)(2,1)S(1)} %get-tuple-element.34), channel_id=1, source_target_pairs={{0,18},{1,27},{2,20},{3,13},{4,22},{5,31},{6,8},{7,17},{8,26},{9,3... | collective-permute-start | bytes 393224 | tf_op jit(solution)/shard_map/ppermute | solution.py:26
  39.4 7.8 %collective-permute-start.14 = (bf16[128,256]{1,0:T(8,128)(2,1)S(1)}, bf16[128,256]{1,0:T(8,128)(2,1)S(1)}, u32[]{:S(2)}, u32[]{:S(2)}) collective-permute-start(bf16[128,256]{1,0:T(8,128)(2,1)S(1)} %add_convert_fusion.2), channel_id=1, source_target_pairs={{0,8},{1,9},{2,10},{3,11},{4,12},{5,13},{6,14},{7,15},{8,0},{9,1},... | collective-permute-start | bytes 196616 | tf_op jit(solution)/shard_map/ppermute | solution.py:26
  40.2 10.3 %collective-permute-start.9 = (bf16[256,256]{1,0:T(8,128)(2,1)S(1)}, bf16[256,256]{1,0:T(8,128)(2,1)S(1)}, u32[]{:S(2)}, u32[]{:S(2)}) collective-permute-start(bf16[256,256]{1,0:T(8,128)(2,1)S(1)} %get-tuple-element.35), channel_id=1, source_target_pairs={{0,16},{1,25},{2,22},{3,15},{4,20},{5,29},{6,10},{7,19},{8,24},{9,... | collective-permute-start | bytes 393224 | tf_op jit(solution)/shard_map/ppermute | solution.py:26
  43.6 7.0 %collective-permute-start.10 = (bf16[256,256]{1,0:T(8,128)(2,1)S(1)}, bf16[256,256]{1,0:T(8,128)(2,1)S(1)}, u32[]{:S(2)}, u32[]{:S(2)}) collective-permute-start(bf16[256,256]{1,0:T(8,128)(2,1)S(1)} %get-tuple-element.36), channel_id=1, source_target_pairs={{0,0},{1,31},{2,4},{3,9},{4,26},{5,3},{6,6},{7,13},{8,8},{9,7},{10... | collective-permute-start | bytes 393224 | tf_op jit(solution)/shard_map/ppermute | solution.py:26
  44.2 8.6 %collective-permute-start.11 = (bf16[256,256]{1,0:T(8,128)(2,1)S(1)}, bf16[256,256]{1,0:T(8,128)(2,1)S(1)}, u32[]{:S(2)}, u32[]{:S(2)}) collective-permute-start(bf16[256,256]{1,0:T(8,128)(2,1)S(1)} %get-tuple-element.37), channel_id=1, source_target_pairs={{0,2},{1,29},{2,6},{3,11},{4,24},{5,1},{6,4},{7,15},{8,10},{9,5},{... | collective-permute-start | bytes 393224 | tf_op jit(solution)/shard_map/ppermute | solution.py:26
  47.2 5.7 %collective-permute-start.15 = (bf16[128,256]{1,0:T(8,128)(2,1)S(1)}, bf16[128,256]{1,0:T(8,128)(2,1)S(1)}, u32[]{:S(2)}, u32[]{:S(2)}) collective-permute-start(bf16[128,256]{1,0:T(8,128)(2,1)S(1)} %add_convert_fusion.1), channel_id=1, source_target_pairs={{0,4},{1,5},{2,6},{3,7},{4,0},{5,1},{6,2},{7,3},{8,12},{9,13},{10,... | collective-permute-start | bytes 196616 | tf_op jit(solution)/shard_map/ppermute | solution.py:26
  53.0 4.3 %collective-permute-start.16 = (bf16[128,256]{1,0:T(8,128)(2,1)S(1)}, bf16[128,256]{1,0:T(8,128)(2,1)S(1)}, u32[]{:S(2)}, u32[]{:S(2)}) collective-permute-start(bf16[128,256]{1,0:T(8,128)(2,1)S(1)} %add_convert_fusion), channel_id=1, source_target_pairs={{0,2},{1,3},{2,0},{3,1},{4,6},{5,7},{6,4},{7,5},{8,10},{9,11},{10,... | collective-permute-start | bytes 196616 | tf_op jit(solution)/shard_map/ppermute | solution.py:26
  53.9 3.6 %collective-permute-start.12 = (bf16[128,256]{1,0:T(8,128)(2,1)S(1)}, bf16[128,256]{1,0:T(8,128)(2,1)S(1)}, u32[]{:S(2)}, u32[]{:S(2)}) collective-permute-start(bf16[128,256]{1,0:T(8,128)(2,1)S(1)} %fusion.2), channel_id=1, source_target_pairs={{0,1},{1,0},{2,3},{3,2},{4,5},{5,4},{6,7},{7,6},{8,9},{9,8},{10,11... | collective-permute-start | bytes 196616 | tf_op jit(solution)/shard_map/ppermute | solution.py:26
  57.4 1.4 %collective-permute-start.17 = (bf16[2,128,256]{2,1,0:T(8,128)(2,1)S(1)}, bf16[2,128,256]{2,1,0:T(8,128)(2,1)S(1)}, u32[]{:S(2)}, u32[]{:S(2)}) collective-permute-start(bf16[2,128,256]{2,1,0:T(8,128)(2,1)S(1)} %maximum_select_fusion.2), channel_id=1, source_target_pairs={{0,1},{1,0},{2,3},{3,2},{4,5},{5,4},{6,7},{7,6},{8,9},{9,8},{10,11... | collective-permute-start | bytes 393224 | tf_op jit(solution)/shard_map/ppermute | solution.py:26

commit v4 on v3

--- a/solution.py
+++ b/solution.py
@@ -9,7 +9,6 @@
 from jax.sharding import PartitionSpec as P
 
 BOTH = ("blk", "rep")
-PIECES = 1
 BF16 = jnp.bfloat16
 F32 = jnp.float32
 VMEM = pl.BlockSpec(memory_space=pltpu.VMEM)
@@ -30,27 +29,33 @@
     return lax.dot_general(lhs, rhs, (contract, ((), ())), preferred_element_type=F32)
 
 
-def place_tiles(slot, out_axis, meta, tiles, source, total):
-    size = tiles.shape[-1]
-    tile_count = tiles.shape[-3]
+def slot_of(swap, order, rep, part):
+    plane = lax.div(rep, 2)
+    swaps = swaps_slot(swap, part, rep)
+    moved = jnp.logical_and(swaps, plane == 1 - order)
+    if order == 0:
+        return moved, plane
+    return moved, jnp.where(jnp.logical_and(swaps, plane == 1), 1, 1 - plane)
+
+
+def place_tiles(swap, order, out_axis, coords, live, note, tiles, source, total):
+    size, tile_count = tiles.shape[-1], tiles.shape[-3]
+    spare = total.shape[0] // size - 1
+    moved, slot = slot_of(swap, order, lax.axis_index("rep"), lax.axis_index("blk"))
+    at = note.shape[0] // 2
     for k in range(tile_count):
-        to = meta[out_axis, slot * tile_count + k]
-        take = meta[3 - out_axis, slot * tile_count + k]
+        places = [jnp.where(moved, note[at + 2 * k + axis], coords[0, slot, axis, k]) for axis in range(2)]
+        present = jnp.where(moved, note[at + 2 * tile_count + k], live[0, slot, k]) != 0
+        take, to = places[1 - out_axis], jnp.where(present, places[out_axis], spare)
         block = source[pl.ds(pl.multiple_of(take * size, size), size), :]
         rows = pl.ds(pl.multiple_of(to * size, size), size)
-        total[rows, :] += dot(tiles[slot, k], block, ((1 - out_axis,), (0,)))
-
-
-def forward_first(meta, tiles, arrived, out, total):
+        total[rows, :] += dot(tiles[order, k], block, ((1 - out_axis,), (0,)))
+
+
+def forward(swap, coords, live, note, tiles, far, near, panel, keep, send, source, total):
+    rows = panel.shape[0]
     total[...] = jnp.zeros_like(total)
-    place_tiles(0, 0, meta, tiles, arrived, total)
-    out[...] = total[: out.shape[0], :]
-
-
-def forward_second(swap, meta, tiles, arrived, panel, before, keep, send, source, total):
-    rows = before.shape[0]
-    total[:rows, :] = before[...]
-    total[rows:, :] = jnp.zeros((total.shape[0] - rows, total.shape[1]), F32)
+    place_tiles(swap, 0, 0, coords, live, note, tiles, far, total)
     is_local = near_is_local(swap, lax.axis_index("blk"), lax.axis_index("rep"))
 
     @pl.when(is_local)
@@ -59,9 +64,9 @@
 
     @pl.when(jnp.logical_not(is_local))
     def _():
-        source[...] = arrived[...]
-
-    place_tiles(1, 0, meta, tiles, source, total)
+        source[...] = near[...]
+
+    place_tiles(swap, 1, 0, coords, live, note, tiles, source, total)
     core = lax.rem(lax.axis_index("rep"), 2)
     share = rows // 4
     for h in range(2):
@@ -71,11 +76,21 @@
         send[h * share : (h + 1) * share, :] = total[other, :].astype(BF16)
 
 
+def picked_slot(tiles, picked, sem):
+    rep = lax.axis_index("rep")
+
+    @pl.when(swaps_slot(True, lax.axis_index("blk"), rep))
+    def _():
+        copy = pltpu.make_async_copy(tiles.at[0, 1 - lax.div(rep, 2)], picked, sem)
+        copy.start()
+        copy.wait()
+
+
 def prepare(
-    swap, coords, live, far_note, tiles, features, cot_own, deg_own, w_self, cot_far, deg_far, *rest,
+    swap, tiles, features, cot_own, deg_own, w_self, cot_far, deg_far, *rest,
 ):
-    moved = rest[:-9]
-    meta, kept_tiles, panel, self_term, cot, inv_root, deg_near, weights, sems = rest[-9:]
+    moved = rest[:-8]
+    kept_tiles, panel, self_term, cot, inv_root, deg_near, weights, sems = rest[-8:]
     rep = lax.axis_index("rep")
     core, plane = lax.rem(rep, 2), lax.div(rep, 2)
     share = cot_own.shape[0]
@@ -86,36 +101,17 @@
     for copy in copies:
         copy.start()
 
-    swaps = swaps_slot(swap, lax.axis_index("blk"), rep)
-    far_moved = jnp.logical_and(swaps, plane == 1)
-    near_moved = jnp.logical_and(swaps, plane == 0)
-    slot_of = (plane, jnp.where(far_moved, 1, 1 - plane))
     tile_copies = []
-    for order, is_moved in enumerate((far_moved, near_moved)):
+    for order in range(2):
+        is_moved, slot = slot_of(swap, order, rep, lax.axis_index("blk"))
         place = kept_tiles.at[order]
-        here = pltpu.make_async_copy(tiles.at[0, slot_of[order]], place, sems.at[len(tile_copies) + 5])
+        here = pltpu.make_async_copy(tiles.at[0, slot], place, sems.at[len(tile_copies) + 5])
         tile_copies.append((jnp.logical_not(is_moved), here))
-        start = 0
-        for piece in moved:
-            part = place.at[start : start + piece.shape[0]]
-            tile_copies.append((is_moved, pltpu.make_async_copy(piece, part, sems.at[len(tile_copies) + 5])))
-            start += piece.shape[0]
+        if moved:
+            come = pltpu.make_async_copy(moved[0], place, sems.at[len(tile_copies) + 5])
+            tile_copies.append((is_moved, come))
     for is_needed, copy in tile_copies:
         pl.when(is_needed)(copy.start)
-
-    tile_count = live.shape[2]
-    spare = features.shape[0] // kept_tiles.shape[-1]
-    for order, is_moved in enumerate((far_moved, near_moved)):
-        slot = slot_of[order]
-        for k in range(tile_count):
-            at = order * tile_count + k
-            row = jnp.where(is_moved, far_note[share + 2 * k], coords[0, slot, k, 0])
-            column = jnp.where(is_moved, far_note[share + 2 * k + 1], coords[0, slot, k, 1])
-            present = jnp.where(is_moved, far_note[share + 2 * tile_count + k], live[0, slot, k]) != 0
-            meta[0, at] = jnp.where(present, row, spare)
-            meta[1, at] = jnp.where(present, column, spare)
-            meta[2, at] = row
-            meta[3, at] = column
     for copy in copies:
         copy.wait()
     cot[away, :] = cot_far[...]
@@ -167,7 +163,7 @@
         own_term[...] = term[share:]
 
 
-def backward(swap, meta, tiles, own, other, far_cross, far_same, near_first, near_last, source, total):
+def backward(swap, coords, live, note, tiles, own, other, far_cross, far_same, near_first, near_last, source, total):
     rep = lax.axis_index("rep")
     core, plane = lax.rem(rep, 2), lax.div(rep, 2)
     share = source.shape[0] // 4
@@ -180,7 +176,7 @@
     to_plane = jnp.where(same_first, plane, 1 - plane)
     for slot, outs in enumerate(((far_cross, far_same), (near_first, near_last))):
         total[...] = jnp.zeros_like(total)
-        place_tiles(slot, 1, meta, tiles, source, total)
+        place_tiles(swap, slot, 1, coords, live, note, tiles, source, total)
         first = 1 - plane if slot == 0 else to_plane
         for out, which in zip(outs, (first, 1 - first)):
             out[...] = total[pl.ds(pl.multiple_of(which * half, half), half), :].astype(BF16)
@@ -215,7 +211,7 @@
     rep_count = lax.axis_size("rep")
     rep = lax.axis_index("rep")
     core, plane = rep % 2, rep // 2
-    slots, tile_count, tile_size = tile_vals.shape[1:4]
+    slots, tile_size = tile_vals.shape[1], tile_vals.shape[3]
     half_span = slots * rep_count // 2
     rows, dim = features.shape
     half, share = rows // 2, rows // rep_count
@@ -260,30 +256,28 @@
         pairs = []
         for part in range(0, part_total, 2):
             pairs += [(part * rep_count, part * rep_count + 2), (part * rep_count + 2, part * rep_count)]
-        cuts = [tile_count * i // PIECES for i in range(PIECES + 1)]
-        for low, high in zip(cuts, cuts[1:]):
-            piece = jnp.where(plane == 0, tile_vals[0, 1, low:high], tile_vals[0, 0, low:high])
-            moved.append(lax.ppermute(piece, BOTH, pairs))
+        picked = kernel_call(
+            picked_slot, "picked_slot", [(tile_vals.shape[2:], BF16)], [pltpu.with_memory_space_constraint(tile_vals, pltpu.HBM)],
+            [pltpu.SemaphoreType.DMA], [pl.BlockSpec(memory_space=pltpu.HBM)],
+        )[0]
+        moved.append(lax.ppermute(picked, BOTH, pairs))
     wide = (half, dim)
     raw = [tile_vals, features, cotangent, degree.reshape(1, share), w_self]
     raw = [pltpu.with_memory_space_constraint(a, pltpu.HBM) for a in raw]
-    meta, tiles, panel, self_term, cot, inv_root = kernel_call(
+    tiles, panel, self_term, cot, inv_root = kernel_call(
         functools.partial(prepare, swap),
         "prepare",
-        [((4, slots * tile_count), jnp.int32), (tile_vals.shape[1:], BF16), ((rows, dim), BF16), (wide, F32), (wide, BF16), (wide, F32)],
-        [tile_coords, tile_live, far_note] + raw + [cot_far, far_note.reshape(2, share)] + moved,
+        [(tile_vals.shape[1:], BF16), ((rows, dim), BF16), (wide, F32), (wide, BF16), (wide, F32)],
+        raw + [cot_far, far_note.reshape(2, share)] + moved,
         [pltpu.VMEM((1, share), jnp.int32), pltpu.VMEM(w_self.shape, BF16), pltpu.SemaphoreType.DMA((7 + 2 * len(moved),))],
-        [SMEM] * 3 + [pl.BlockSpec(memory_space=pltpu.HBM)] * 5 + [VMEM] * 2 + [pl.BlockSpec(memory_space=pl.ANY)] * len(moved),
-        [SMEM] + [VMEM] * 5,
+        [pl.BlockSpec(memory_space=pltpu.HBM)] * 5 + [VMEM] * 2 + [pl.BlockSpec(memory_space=pl.ANY)] * len(moved),
     )
 
     source, total = pltpu.VMEM((rows, dim), BF16), pltpu.VMEM((rows + tile_size, dim), F32)
-    first = kernel_call(
-        forward_first, "forward_first", [((rows, dim), F32)], [meta, tiles, panel_far], [total], [SMEM] + [VMEM] * 2
-    )[0]
+    scalars = [tile_coords.transpose(0, 1, 3, 2), tile_live, far_note]
     keep, send = kernel_call(
-        functools.partial(forward_second, swap), "forward_second", [(wide, F32), (wide, BF16)],
-        [meta, tiles, panel_near, panel, first], [source, total], [SMEM] + [VMEM] * 4,
+        functools.partial(forward, swap), "forward", [(wide, F32), (wide, BF16)], scalars + [tiles, panel_far, panel_near, panel],
+        [source, total], [SMEM] * 3 + [VMEM] * 4,
     )
     chip_sum = keep + flip_core(send).astype(F32)
     far_sum = flip_plane(chip_sum.astype(BF16))
@@ -298,7 +292,8 @@
     )
     other = flip_core(message)
     sends = kernel_call(
-        functools.partial(backward, swap), "backward", [(wide, BF16)] * 4, [meta, tiles, message, other], [source, total], [SMEM] + [VMEM] * 3
+        functools.partial(backward, swap), "backward", [(wide, BF16)] * 4, scalars + [tiles, message, other], [source, total],
+        [SMEM] * 3 + [VMEM] * 3,
     )
 
     def others(value, bit, rep_bit=0):

time: 59.9 us -> 58.6 us (0.978)
  waiting for transfers between devices: 19 us -> 22.6 us
  starting transfers between devices: 27.5 us -> 25.2 us
  other arithmetic: 2.45 us -> 1.01 us
  Pallas kernels: 8.38 us -> 7.43 us
    ppermute x15, waiting for transfers between devices: 19 us -> 21.1 us  [exchange(): return lax.ppermute(value, BOTH, pairs)]
    ppermute x15, starting transfers between devices: 18.3 us -> 16.4 us  [exchange(): return lax.ppermute(value, BOTH, pairs)]
    ppermute x2, waiting for transfers between devices: 0.01 us -> 1.56 us  [fetch(): return lax.ppermute(features, BOTH, pairs)]
    select_n x1 -> x0, other arithmetic: 1.44 us -> none  [on_device(): jnp.where(plane == 0, tile_vals[0, 1, low:high], tile_vals[0, 0, low:high])]
    pallas_call x5, Pallas kernels: 8.38 us -> 7.43 us  [kernel_call(): pl.pallas_call(kernel, out_shape=[jax.ShapeDtypeStruct(*out) for out in o...]
  transfers between devices with their start and end apart: 18 -> 18, of which waited for: 11 -> 10; matrix products, arithmetic and copies ran while one was open for 2% -> 2% of each run, Pallas kernels for 10% -> 5%
where the time goes in v4:
time: 58.6 us; the launch traced here: 58.4 us
  starting transfers between devices  25.2 us (43%)
  waiting for transfers between devices  22.6 us (39%)
  Pallas kernels  7.43 us (13%)
  local copies, waits for them, and re-layouts  1.26 us (2%)
  other arithmetic  1.01 us (2%)
  between operations  0.91 us (2%)
    ppermute x15, waiting for transfers between devices, exchange(): return lax.ppermute(value, BOTH, pairs)  21.1 us
    ppermute x15, starting transfers between devices, exchange(): return lax.ppermute(value, BOTH, pairs)  16.4 us
    pallas_call x5, Pallas kernels, kernel_call(): pl.pallas_call(kernel, out_shape=[jax.ShapeDtypeStruct(*out) for out in o...  7.43 us
    ppermute x1, starting transfers between devices, on_device(): moved.append(lax.ppermute(picked, BOTH, pairs))  4.85 us
    ppermute x2, starting transfers between devices, fetch(): return lax.ppermute(features, BOTH, pairs)  3.93 us
    ppermute x2, waiting for transfers between devices, fetch(): return lax.ppermute(features, BOTH, pairs)  1.56 us
  transfers between devices with their start and end apart: 18, of which 10 were waited for; matrix products, arithmetic and copies ran while one was open for 2% of the time, Pallas kernels for 5%

profile of v4, /device:TPU:0, one launch (start us, length us, event | category | flops | bytes accessed | tf_op | source)
XLA Modules:
  0.0 58.4 jit_solution(5544044722509186784)
XLA Ops:
  0.6 0.0 copy-start.4
  0.6 0.0 copy-start.5
  0.7 0.0 copy-start.2
  0.7 0.0 copy-start.3
  0.7 0.0 copy-start.6
  0.7 1.2 %picked_slot.1 = bf16[20,128,128]{2,1,0:T(8,128)(2,1)S(1)} custom-call(bf16[1,2,20,128,128]{4,3,2,1,0:T(8,128)(2,1)} %tiles.3), custom_call_target="tpu_custom_call" | custom-call | tf_op jit(solution)/shard_map/picked_slot/pallas_call | solution.py:198
  1.9 4.8 %collective-permute-start.2 = (bf16[20,128,128]{2,1,0:T(8,128)(2,1)S(1)}, bf16[20,128,128]{2,1,0:T(8,128)(2,1)S(1)}, u32[]{:S(2)}, u32[]{:S(2)}) collective-permute-start(bf16[20,128,128]{2,1,0:T(8,128)(2,1)S(1)} %picked_slot.1), channel_id=1, source_target_pairs={{0,2},{2,0},{8,10},{10,8},{16,18},{18,16},{24,26},{26,24}} | collective-permute-start | bytes 1966088 | tf_op jit(solution)/shard_map/ppermute | solution.py:263
  6.7 0.0 copy-done.4
  6.8 2.6 %collective-permute-start.3 = (bf16[512,256]{1,0:T(8,128)(2,1)S(1)}, bf16[512,256]{1,0:T(8,128)(2,1)S(1)}, u32[]{:S(2)}, u32[]{:S(2)}) collective-permute-start(bf16[512,256]{1,0:T(8,128)(2,1)S(1)} %copy-done.4), channel_id=1, source_target_pairs={{16,0},{25,1},{22,2},{15,3},{20,4},{29,5},{10,6},{19,7},{24,8},{1,... | collective-permute-start | bytes 786440 | tf_op jit(solution)/shard_map/ppermute | solution.py:243
  9.4 1.3 %collective-permute-start.4 = (bf16[512,256]{1,0:T(8,128)(2,1)S(1)}, bf16[512,256]{1,0:T(8,128)(2,1)S(1)}, u32[]{:S(2)}, u32[]{:S(2)}) collective-permute-start(bf16[512,256]{1,0:T(8,128)(2,1)S(1)} %copy-done.4), channel_id=1, source_target_pairs={{29,1},{6,2},{11,3},{24,4},{1,5},{15,7},{5,9},{14,10},{19,11},{0,1... | collective-permute-start | bytes 786440 | tf_op jit(solution)/shard_map/ppermute | solution.py:243
  10.7 0.0 copy-done.5
  10.7 0.1 collective-permute-start.1
  10.8 0.0 copy-done.2
  10.8 0.1 copy.14
  10.9 0.1 reshape_squeeze.6
  11.0 0.1 copy.15
  11.1 0.1 reshape_squeeze.7
  11.2 0.0 copy-done.3
  11.2 0.0 copy-done.6
  11.3 0.1 fusion.5
  11.3 2.0 %collective-permute-start = (s32[256]{0:T(256)S(1)}, s32[256]{0:T(256)S(1)}, u32[]{:S(2)}, u32[]{:S(2)}) collective-permute-start(s32[256]{0:T(256)S(1)} %fusion.5), channel_id=1, source_target_pairs={{0,2},{1,3},{2,0},{3,1},{4,6},{5,7},{6,4},{7,5},{8,10},{9,11},{10,... | collective-permute-start | bytes 3080 | tf_op jit(solution)/shard_map/ppermute | solution.py:25
  13.3 3.4 %collective-permute-done.note = s32[256]{0:T(256)S(1)} collective-permute-done((s32[256]{0:T(256)S(1)}, s32[256]{0:T(256)S(1)}, u32[]{:S(2)}, u32[]{:S(2)}) %collective-permute-start) | collective-permute-done | bytes 1056 | tf_op jit(solution)/shard_map/ppermute | solution.py:25
  16.8 0.0 collective-permute-done.1.cot_far
  16.8 0.0 collective-permute-done.2.rest_0_
  16.8 1.4 %prepare.1 = (bf16[2,20,128,128]{3,2,1,0:T(8,128)(2,1)S(1)}, bf16[512,256]{1,0:T(8,128)(2,1)S(1)}, f32[256,256]{1,0:T(8,128)S(1)}, bf16[256,256]{1,0:T(8,128)(2,1)S(1)}, f32[256,256]{1,0:T(8,128)S(1)}) custom-call(bf16[1,2,20,128,128]{4,3,2,1,0:T(8,128)(2,1)} %tiles.3, bf16[512,256]{1,0:T(8,128)(2,1)} %features.1, bf16[128,256]{1,0:T(8,128)(2,1)} %cot_own.1, ...), custom_call_target="tpu_custom_call" | custom-call | tf_op jit(solution)/shard_map/prepare/pallas_call | solution.py:198
  18.1 1.6 %collective-permute-done.3.far = bf16[512,256]{1,0:T(8,128)(2,1)S(1)} collective-permute-done((bf16[512,256]{1,0:T(8,128)(2,1)S(1)}, bf16[512,256]{1,0:T(8,128)(2,1)S(1)}, u32[]{:S(2)}, u32[]{:S(2)}) %collective-permute-start.3) | collective-permute-done | bytes 262176 | tf_op jit(solution)/shard_map/ppermute | solution.py:243
  19.7 0.0 collective-permute-done.4.near
  19.7 0.0 copy-start
  19.7 0.0 copy-start.1
  19.7 1.7 %forward.1 = (f32[256,256]{1,0:T(8,128)S(1)}, bf16[256,256]{1,0:T(8,128)(2,1)S(1)}) custom-call(s32[1,2,2,20]{3,2,1,0:T(2,128)S(1)} %bitcast.23, s32[1,2,20]{2,1,0:T(2,128)S(1)} %copy-done.3, s32[256]{0:T(256)S(1)} %collective-permute-done.note, bf16[2,20,128,128]{3,2,1,0:T(8,128)(2,1)S(1)} %get-tuple-element.22.tiles, ...), custom_call_target="tpu_custom_call" | custom-call | tf_op jit(solution)/shard_map/forward/pallas_call | solution.py:198
  21.4 0.1 collective-permute-start.5
  21.5 1.3 %collective-permute-done.5 = bf16[256,256]{1,0:T(8,128)(2,1)S(1)} collective-permute-done((bf16[256,256]{1,0:T(8,128)(2,1)S(1)}, bf16[256,256]{1,0:T(8,128)(2,1)S(1)}, u32[]{:S(2)}, u32[]{:S(2)}) %collective-permute-start.5) | collective-permute-done | bytes 131104 | tf_op jit(solution)/shard_map/ppermute | solution.py:25
  22.9 0.6 %collective-permute-start.6 = (bf16[256,256]{1,0:T(8,128)(2,1)S(1)}, bf16[256,256]{1,0:T(8,128)(2,1)S(1)}, u32[]{:S(2)}, u32[]{:S(2)}) collective-permute-start(bf16[256,256]{1,0:T(8,128)(2,1)S(1)} %get-tuple-element.40), channel_id=1, source_target_pairs={{0,2},{1,3},{2,0},{3,1},{4,6},{5,7},{6,4},{7,5},{8,10},{9,11},{10,... | collective-permute-start | bytes 393224 | tf_op jit(solution)/shard_map/ppermute | solution.py:25
  23.5 5.0 %collective-permute-done.6.far_sum = bf16[256,256]{1,0:T(8,128)(2,1)S(1)} collective-permute-done((bf16[256,256]{1,0:T(8,128)(2,1)S(1)}, bf16[256,256]{1,0:T(8,128)(2,1)S(1)}, u32[]{:S(2)}, u32[]{:S(2)}) %collective-permute-start.6) | collective-permute-done | bytes 131104 | tf_op jit(solution)/shard_map/ppermute | solution.py:25
  28.5 0.0 copy-done
  28.5 0.0 copy-done.1
  28.5 1.5 %middle.1 = (bf16[128,256]{1,0:T(8,128)(2,1)}, f32[128,256]{1,0:T(8,128)S(1)}, bf16[384,256]{1,0:T(8,128)(2,1)S(1)}, f32[128,256]{1,0:T(8,128)S(1)}) custom-call(f32[256,256]{1,0:T(8,128)S(1)} %get-tuple-element.41.chip_sum, bf16[256,256]{1,0:T(8,128)(2,1)S(1)} %collective-permute-done.6.far_sum, f32[256,256]{1,0:T(8,128)S(1)} %get-tuple-element.26.inv_root, ...), custom_call_target="tpu_custom_call" | custom-call | tf_op jit(solution)/shard_map/middle/pallas_call | solution.py:198
  30.0 0.0 collective-permute-start.7
  30.0 1.4 %collective-permute-done.7.other = bf16[384,256]{1,0:T(8,128)(2,1)S(1)} collective-permute-done((bf16[384,256]{1,0:T(8,128)(2,1)S(1)}, bf16[384,256]{1,0:T(8,128)(2,1)S(1)}, u32[]{:S(2)}, u32[]{:S(2)}) %collective-permute-start.7) | collective-permute-done | bytes 196640 | tf_op jit(solution)/shard_map/ppermute | solution.py:25
  31.5 1.7 %collective-permute-start.13 = (bf16[128,256]{1,0:T(8,128)(2,1)S(1)}, bf16[128,256]{1,0:T(8,128)(2,1)S(1)}, u32[]{:S(2)}, u32[]{:S(2)}) collective-permute-start(bf16[128,256]{1,0:T(8,128)(2,1)S(1)} %add_convert_fusion.3), channel_id=1, source_target_pairs={{0,16},{1,17},{2,18},{3,19},{4,20},{5,21},{6,22},{7,23},{8,24},{9,... | collective-permute-start | bytes 196616 | tf_op jit(solution)/shard_map/ppermute | solution.py:25
  33.1 1.7 %backward.1 = (bf16[256,256]{1,0:T(8,128)(2,1)S(1)}, bf16[256,256]{1,0:T(8,128)(2,1)S(1)}, bf16[256,256]{1,0:T(8,128)(2,1)S(1)}, bf16[256,256]{1,0:T(8,128)(2,1)S(1)}) custom-call(s32[1,2,2,20]{3,2,1,0:T(2,128)S(1)} %bitcast.24, s32[1,2,20]{2,1,0:T(2,128)S(1)} %copy-done.3, s32[256]{0:T(256)S(1)} %collective-permute-done.note, ...), custom_call_target="tpu_custom_call" | custom-call | tf_op jit(solution)/shard_map/backward/pallas_call | solution.py:198
  34.8 1.3 %collective-permute-start.8 = (bf16[256,256]{1,0:T(8,128)(2,1)S(1)}, bf16[256,256]{1,0:T(8,128)(2,1)S(1)}, u32[]{:S(2)}, u32[]{:S(2)}) collective-permute-start(bf16[256,256]{1,0:T(8,128)(2,1)S(1)} %get-tuple-element.32), channel_id=1, source_target_pairs={{0,18},{1,27},{2,20},{3,13},{4,22},{5,31},{6,8},{7,17},{8,26},{9,3... | collective-permute-start | bytes 393224 | tf_op jit(solution)/shard_map/ppermute | solution.py:25
  36.1 1.8 %collective-permute-done.13 = bf16[128,256]{1,0:T(8,128)(2,1)S(1)} collective-permute-done((bf16[128,256]{1,0:T(8,128)(2,1)S(1)}, bf16[128,256]{1,0:T(8,128)(2,1)S(1)}, u32[]{:S(2)}, u32[]{:S(2)}) %collective-permute-start.13) | collective-permute-done | bytes 65568 | tf_op jit(solution)/shard_map/ppermute | solution.py:25
  38.0 0.2 collective-permute-start.14
  38.2 2.9 %collective-permute-start.9 = (bf16[256,256]{1,0:T(8,128)(2,1)S(1)}, bf16[256,256]{1,0:T(8,128)(2,1)S(1)}, u32[]{:S(2)}, u32[]{:S(2)}) collective-permute-start(bf16[256,256]{1,0:T(8,128)(2,1)S(1)} %get-tuple-element.33), channel_id=1, source_target_pairs={{0,16},{1,25},{2,22},{3,15},{4,20},{5,29},{6,10},{7,19},{8,24},{9,... | collective-permute-start | bytes 393224 | tf_op jit(solution)/shard_map/ppermute | solution.py:25
  41.1 0.7 %collective-permute-start.10 = (bf16[256,256]{1,0:T(8,128)(2,1)S(1)}, bf16[256,256]{1,0:T(8,128)(2,1)S(1)}, u32[]{:S(2)}, u32[]{:S(2)}) collective-permute-start(bf16[256,256]{1,0:T(8,128)(2,1)S(1)} %get-tuple-element.34), channel_id=1, source_target_pairs={{0,0},{1,31},{2,4},{3,9},{4,26},{5,3},{6,6},{7,13},{8,8},{9,7},{10... | collective-permute-start | bytes 393224 | tf_op jit(solution)/shard_map/ppermute | solution.py:25
  41.8 3.3 %collective-permute-start.11 = (bf16[256,256]{1,0:T(8,128)(2,1)S(1)}, bf16[256,256]{1,0:T(8,128)(2,1)S(1)}, u32[]{:S(2)}, u32[]{:S(2)}) collective-permute-start(bf16[256,256]{1,0:T(8,128)(2,1)S(1)} %get-tuple-element.35), channel_id=1, source_target_pairs={{0,2},{1,29},{2,6},{3,11},{4,24},{5,1},{6,4},{7,15},{8,10},{9,5},{... | collective-permute-start | bytes 393224 | tf_op jit(solution)/shard_map/ppermute | solution.py:25
  45.0 0.0 collective-permute-done.8
  45.0 0.0 collective-permute-done.14
  45.1 2.4 %collective-permute-start.15 = (bf16[128,256]{1,0:T(8,128)(2,1)S(1)}, bf16[128,256]{1,0:T(8,128)(2,1)S(1)}, u32[]{:S(2)}, u32[]{:S(2)}) collective-permute-start(bf16[128,256]{1,0:T(8,128)(2,1)S(1)} %add_convert_fusion.1), channel_id=1, source_target_pairs={{0,4},{1,5},{2,6},{3,7},{4,0},{5,1},{6,2},{7,3},{8,12},{9,13},{10,... | collective-permute-start | bytes 196616 | tf_op jit(solution)/shard_map/ppermute | solution.py:25
  47.5 1.2 %collective-permute-done.9 = bf16[256,256]{1,0:T(8,128)(2,1)S(1)} collective-permute-done((bf16[256,256]{1,0:T(8,128)(2,1)S(1)}, bf16[256,256]{1,0:T(8,128)(2,1)S(1)}, u32[]{:S(2)}, u32[]{:S(2)}) %collective-permute-start.9) | collective-permute-done | bytes 131104 | tf_op jit(solution)/shard_map/ppermute | solution.py:25
  48.7 0.0 collective-permute-done.10
  48.7 3.0 %collective-permute-done.11 = bf16[256,256]{1,0:T(8,128)(2,1)S(1)} collective-permute-done((bf16[256,256]{1,0:T(8,128)(2,1)S(1)}, bf16[256,256]{1,0:T(8,128)(2,1)S(1)}, u32[]{:S(2)}, u32[]{:S(2)}) %collective-permute-start.11) | collective-permute-done | bytes 131104 | tf_op jit(solution)/shard_map/ppermute | solution.py:25
  51.7 0.1 convert_add_fusion
  51.7 0.0 collective-permute-done.15
  51.8 1.0 %collective-permute-start.16 = (bf16[128,256]{1,0:T(8,128)(2,1)S(1)}, bf16[128,256]{1,0:T(8,128)(2,1)S(1)}, u32[]{:S(2)}, u32[]{:S(2)}) collective-permute-start(bf16[128,256]{1,0:T(8,128)(2,1)S(1)} %add_convert_fusion), channel_id=1, source_target_pairs={{0,2},{1,3},{2,0},{3,1},{4,6},{5,7},{6,4},{7,5},{8,10},{9,11},{10,... | collective-permute-start | bytes 196616 | tf_op jit(solution)/shard_map/ppermute | solution.py:25
  52.8 0.1 collective-permute-start.12
  52.9 3.2 %collective-permute-done.16 = bf16[128,256]{1,0:T(8,128)(2,1)S(1)} collective-permute-done((bf16[128,256]{1,0:T(8,128)(2,1)S(1)}, bf16[128,256]{1,0:T(8,128)(2,1)S(1)}, u32[]{:S(2)}, u32[]{:S(2)}) %collective-permute-start.16) | collective-permute-done | bytes 65568 | tf_op jit(solution)/shard_map/ppermute | solution.py:25
  56.1 0.1 collective-permute-start.17
  56.2 0.0 collective-permute-done.12
  56.2 0.7 %fusion.1 = bf16[128,256]{1,0:T(8,128)(2,1)} fusion(f32[128,256]{1,0:T(8,128)S(1)} %get-tuple-element.30, bf16[128,256]{1,0:T(8,128)(2,1)S(1)} %collective-permute-done.12, f32[2,128,256]{2,1,0:T(8,128)S(1)} %bitcast.27, s32[]{:T(128)S(6)} %select_n.59), kind=kLoop, calls=%fused_computation.8 | loop fusion | flops 131072 | bytes 393220 | tf_op jit(solution)/shard_map/convert_element_type | solution.py:334
  56.9 0.6 %collective-permute-done.17 = bf16[2,128,256]{2,1,0:T(8,128)(2,1)S(1)} collective-permute-done((bf16[2,128,256]{2,1,0:T(8,128)(2,1)S(1)}, bf16[2,128,256]{2,1,0:T(8,128)(2,1)S(1)}, u32[]{:S(2)}, u32[]{:S(2)}) %collective-permute-start.17) | collective-permute-done | bytes 131104 | tf_op jit(solution)/shard_map/ppermute | solution.py:25
  57.5 0.1 convert_multiply_fusion
  57.6 0.8 %fusion.7 = (f32[1,2,128,256]{3,2,0,1:T(8,128)}, f32[1,2,128,256]{3,2,0,1:T(8,128)}) fusion(f32[2,2,128,256]{3,2,0,1:T(8,128)S(1)} %convert_multiply_fusion), kind=kLoop, calls=%fused_computation.25 | loop fusion | bytes 1048576 | tf_op jit(solution)/shard_map/slice | solution.py:335
  (11 shorter events, 0.2 us)
Async XLA Ops:
  0.6 6.1 %copy-start.4 = (bf16[512,256]{1,0:T(8,128)(2,1)S(1)}, bf16[512,256]{1,0:T(8,128)(2,1)}, u32[]{:S(2)}) copy-start(bf16[512,256]{1,0:T(8,128)(2,1)} %features.1) | copy-start | bytes 786436
  0.6 10.1 %copy-start.5 = (bf16[128,256]{1,0:T(8,128)(2,1)S(1)}, bf16[128,256]{1,0:T(8,128)(2,1)}, u32[]{:S(2)}) copy-start(bf16[128,256]{1,0:T(8,128)(2,1)} %cot_own.1) | copy-start | bytes 196612
  0.7 10.2 %copy-start.2 = (s32[1,2,20,2]{2,3,1,0:T(2,128)S(1)}, s32[1,2,20,2]{2,3,1,0:T(2,128)}, u32[]{:S(2)}) copy-start(s32[1,2,20,2]{2,3,1,0:T(2,128)} %param.9) | copy-start | bytes 964
  0.7 10.6 %copy-start.3 = (s32[1,2,20]{2,1,0:T(2,128)S(1)}, s32[1,2,20]{2,1,0:T(2,128)}, u32[]{:S(2)}) copy-start(s32[1,2,20]{2,1,0:T(2,128)} %live.3) | copy-start | bytes 484
  0.7 10.6 %copy-start.6 = (s32[128]{0:T(128)S(1)}, s32[128]{0:T(128)}, u32[]{:S(2)}) copy-start(s32[128]{0:T(128)} %param.12) | copy-start | bytes 1540
  1.9 14.9 %collective-permute-start.2 = (bf16[20,128,128]{2,1,0:T(8,128)(2,1)S(1)}, bf16[20,128,128]{2,1,0:T(8,128)(2,1)S(1)}, u32[]{:S(2)}, u32[]{:S(2)}) collective-permute-start(bf16[20,128,128]{2,1,0:T(8,128)(2,1)S(1)} %picked_slot.1), channel_id=1, source_target_pairs={{0,2},{2,0},{8,10},{10,8},{16,18},{18,16},{24,26},{26,24}} | collective-permute-start | bytes 1966088 | tf_op jit(solution)/shard_map/ppermute | solution.py:263
  6.8 12.9 %collective-permute-start.3 = (bf16[512,256]{1,0:T(8,128)(2,1)S(1)}, bf16[512,256]{1,0:T(8,128)(2,1)S(1)}, u32[]{:S(2)}, u32[]{:S(2)}) collective-permute-start(bf16[512,256]{1,0:T(8,128)(2,1)S(1)} %copy-done.4), channel_id=1, source_target_pairs={{16,0},{25,1},{22,2},{15,3},{20,4},{29,5},{10,6},{19,7},{24,8},{1,... | collective-permute-start | bytes 786440 | tf_op jit(solution)/shard_map/ppermute | solution.py:243
  9.4 10.3 %collective-permute-start.4 = (bf16[512,256]{1,0:T(8,128)(2,1)S(1)}, bf16[512,256]{1,0:T(8,128)(2,1)S(1)}, u32[]{:S(2)}, u32[]{:S(2)}) collective-permute-start(bf16[512,256]{1,0:T(8,128)(2,1)S(1)} %copy-done.4), channel_id=1, source_target_pairs={{29,1},{6,2},{11,3},{24,4},{1,5},{15,7},{5,9},{14,10},{19,11},{0,1... | collective-permute-start | bytes 786440 | tf_op jit(solution)/shard_map/ppermute | solution.py:243
  10.7 6.1 %collective-permute-start.1 = (bf16[128,256]{1,0:T(8,128)(2,1)S(1)}, bf16[128,256]{1,0:T(8,128)(2,1)S(1)}, u32[]{:S(2)}, u32[]{:S(2)}) collective-permute-start(bf16[128,256]{1,0:T(8,128)(2,1)S(1)} %copy-done.5), channel_id=1, source_target_pairs={{0,2},{1,3},{2,0},{3,1},{4,6},{5,7},{6,4},{7,5},{8,10},{9,11},{10,... | collective-permute-start | bytes 196616 | tf_op jit(solution)/shard_map/ppermute | solution.py:25
  11.3 5.4 %collective-permute-start = (s32[256]{0:T(256)S(1)}, s32[256]{0:T(256)S(1)}, u32[]{:S(2)}, u32[]{:S(2)}) collective-permute-start(s32[256]{0:T(256)S(1)} %fusion.5), channel_id=1, source_target_pairs={{0,2},{1,3},{2,0},{3,1},{4,6},{5,7},{6,4},{7,5},{8,10},{9,11},{10,... | collective-permute-start | bytes 3080 | tf_op jit(solution)/shard_map/ppermute | solution.py:25
  19.7 8.8 %copy-start = (bf16[256,256]{1,0:T(8,128)(2,1)S(1)}, bf16[256,256]{1,0:T(8,128)(2,1)}, u32[]{:S(2)}) copy-start(bf16[256,256]{1,0:T(8,128)(2,1)} %w_self.3) | copy-start | bytes 393220
  19.7 8.8 %copy-start.1 = (bf16[256,256]{1,0:T(8,128)(2,1)S(1)}, bf16[256,256]{1,0:T(8,128)(2,1)}, u32[]{:S(2)}) copy-start(bf16[256,256]{1,0:T(8,128)(2,1)} %w_neigh.1) | copy-start | bytes 393220
  21.4 1.4 %collective-permute-start.5 = (bf16[256,256]{1,0:T(8,128)(2,1)S(1)}, bf16[256,256]{1,0:T(8,128)(2,1)S(1)}, u32[]{:S(2)}, u32[]{:S(2)}) collective-permute-start(bf16[256,256]{1,0:T(8,128)(2,1)S(1)} %get-tuple-element.25), channel_id=1, source_target_pairs={{0,1},{1,0},{2,3},{3,2},{4,5},{5,4},{6,7},{7,6},{8,9},{9,8},{10,11... | collective-permute-start | bytes 393224 | tf_op jit(solution)/shard_map/ppermute | solution.py:25
  22.9 5.6 %collective-permute-start.6 = (bf16[256,256]{1,0:T(8,128)(2,1)S(1)}, bf16[256,256]{1,0:T(8,128)(2,1)S(1)}, u32[]{:S(2)}, u32[]{:S(2)}) collective-permute-start(bf16[256,256]{1,0:T(8,128)(2,1)S(1)} %get-tuple-element.40), channel_id=1, source_target_pairs={{0,2},{1,3},{2,0},{3,1},{4,6},{5,7},{6,4},{7,5},{8,10},{9,11},{10,... | collective-permute-start | bytes 393224 | tf_op jit(solution)/shard_map/ppermute | solution.py:25
  30.0 1.4 %collective-permute-start.7 = (bf16[384,256]{1,0:T(8,128)(2,1)S(1)}, bf16[384,256]{1,0:T(8,128)(2,1)S(1)}, u32[]{:S(2)}, u32[]{:S(2)}) collective-permute-start(bf16[384,256]{1,0:T(8,128)(2,1)S(1)} %get-tuple-element.31.own), channel_id=1, source_target_pairs={{0,1},{1,0},{2,3},{3,2},{4,5},{5,4},{6,7},{7,6},{8,9},{9,8},{10,11... | collective-permute-start | bytes 589832 | tf_op jit(solution)/shard_map/ppermute | solution.py:25
  31.5 6.5 %collective-permute-start.13 = (bf16[128,256]{1,0:T(8,128)(2,1)S(1)}, bf16[128,256]{1,0:T(8,128)(2,1)S(1)}, u32[]{:S(2)}, u32[]{:S(2)}) collective-permute-start(bf16[128,256]{1,0:T(8,128)(2,1)S(1)} %add_convert_fusion.3), channel_id=1, source_target_pairs={{0,16},{1,17},{2,18},{3,19},{4,20},{5,21},{6,22},{7,23},{8,24},{9,... | collective-permute-start | bytes 196616 | tf_op jit(solution)/shard_map/ppermute | solution.py:25
  34.8 10.2 %collective-permute-start.8 = (bf16[256,256]{1,0:T(8,128)(2,1)S(1)}, bf16[256,256]{1,0:T(8,128)(2,1)S(1)}, u32[]{:S(2)}, u32[]{:S(2)}) collective-permute-start(bf16[256,256]{1,0:T(8,128)(2,1)S(1)} %get-tuple-element.32), channel_id=1, source_target_pairs={{0,18},{1,27},{2,20},{3,13},{4,22},{5,31},{6,8},{7,17},{8,26},{9,3... | collective-permute-start | bytes 393224 | tf_op jit(solution)/shard_map/ppermute | solution.py:25
  38.0 7.0 %collective-permute-start.14 = (bf16[128,256]{1,0:T(8,128)(2,1)S(1)}, bf16[128,256]{1,0:T(8,128)(2,1)S(1)}, u32[]{:S(2)}, u32[]{:S(2)}) collective-permute-start(bf16[128,256]{1,0:T(8,128)(2,1)S(1)} %add_convert_fusion.2), channel_id=1, source_target_pairs={{0,8},{1,9},{2,10},{3,11},{4,12},{5,13},{6,14},{7,15},{8,0},{9,1},... | collective-permute-start | bytes 196616 | tf_op jit(solution)/shard_map/ppermute | solution.py:25
  38.2 10.5 %collective-permute-start.9 = (bf16[256,256]{1,0:T(8,128)(2,1)S(1)}, bf16[256,256]{1,0:T(8,128)(2,1)S(1)}, u32[]{:S(2)}, u32[]{:S(2)}) collective-permute-start(bf16[256,256]{1,0:T(8,128)(2,1)S(1)} %get-tuple-element.33), channel_id=1, source_target_pairs={{0,16},{1,25},{2,22},{3,15},{4,20},{5,29},{6,10},{7,19},{8,24},{9,... | collective-permute-start | bytes 393224 | tf_op jit(solution)/shard_map/ppermute | solution.py:25
  41.1 7.6 %collective-permute-start.10 = (bf16[256,256]{1,0:T(8,128)(2,1)S(1)}, bf16[256,256]{1,0:T(8,128)(2,1)S(1)}, u32[]{:S(2)}, u32[]{:S(2)}) collective-permute-start(bf16[256,256]{1,0:T(8,128)(2,1)S(1)} %get-tuple-element.34), channel_id=1, source_target_pairs={{0,0},{1,31},{2,4},{3,9},{4,26},{5,3},{6,6},{7,13},{8,8},{9,7},{10... | collective-permute-start | bytes 393224 | tf_op jit(solution)/shard_map/ppermute | solution.py:25
  41.8 9.9 %collective-permute-start.11 = (bf16[256,256]{1,0:T(8,128)(2,1)S(1)}, bf16[256,256]{1,0:T(8,128)(2,1)S(1)}, u32[]{:S(2)}, u32[]{:S(2)}) collective-permute-start(bf16[256,256]{1,0:T(8,128)(2,1)S(1)} %get-tuple-element.35), channel_id=1, source_target_pairs={{0,2},{1,29},{2,6},{3,11},{4,24},{5,1},{6,4},{7,15},{8,10},{9,5},{... | collective-permute-start | bytes 393224 | tf_op jit(solution)/shard_map/ppermute | solution.py:25
  45.1 6.7 %collective-permute-start.15 = (bf16[128,256]{1,0:T(8,128)(2,1)S(1)}, bf16[128,256]{1,0:T(8,128)(2,1)S(1)}, u32[]{:S(2)}, u32[]{:S(2)}) collective-permute-start(bf16[128,256]{1,0:T(8,128)(2,1)S(1)} %add_convert_fusion.1), channel_id=1, source_target_pairs={{0,4},{1,5},{2,6},{3,7},{4,0},{5,1},{6,2},{7,3},{8,12},{9,13},{10,... | collective-permute-start | bytes 196616 | tf_op jit(solution)/shard_map/ppermute | solution.py:25
  51.8 4.3 %collective-permute-start.16 = (bf16[128,256]{1,0:T(8,128)(2,1)S(1)}, bf16[128,256]{1,0:T(8,128)(2,1)S(1)}, u32[]{:S(2)}, u32[]{:S(2)}) collective-permute-start(bf16[128,256]{1,0:T(8,128)(2,1)S(1)} %add_convert_fusion), channel_id=1, source_target_pairs={{0,2},{1,3},{2,0},{3,1},{4,6},{5,7},{6,4},{7,5},{8,10},{9,11},{10,... | collective-permute-start | bytes 196616 | tf_op jit(solution)/shard_map/ppermute | solution.py:25
  52.8 3.4 %collective-permute-start.12 = (bf16[128,256]{1,0:T(8,128)(2,1)S(1)}, bf16[128,256]{1,0:T(8,128)(2,1)S(1)}, u32[]{:S(2)}, u32[]{:S(2)}) collective-permute-start(bf16[128,256]{1,0:T(8,128)(2,1)S(1)} %fusion.2), channel_id=1, source_target_pairs={{0,1},{1,0},{2,3},{3,2},{4,5},{5,4},{6,7},{7,6},{8,9},{9,8},{10,11... | collective-permute-start | bytes 196616 | tf_op jit(solution)/shard_map/ppermute | solution.py:25
  56.1 1.4 %collective-permute-start.17 = (bf16[2,128,256]{2,1,0:T(8,128)(2,1)S(1)}, bf16[2,128,256]{2,1,0:T(8,128)(2,1)S(1)}, u32[]{:S(2)}, u32[]{:S(2)}) collective-permute-start(bf16[2,128,256]{2,1,0:T(8,128)(2,1)S(1)} %maximum_select_fusion.2), channel_id=1, source_target_pairs={{0,1},{1,0},{2,3},{3,2},{4,5},{5,4},{6,7},{7,6},{8,9},{9,8},{10,11... | collective-permute-start | bytes 393224 | tf_op jit(solution)/shard_map/ppermute | solution.py:25

commit v5 on v4

--- a/solution.py
+++ b/solution.py
@@ -136,16 +136,9 @@
     slope = sig * (1.0 + preact * (1.0 - sig))
     grad = (cot[...].astype(F32) * slope).astype(BF16)
     message[:half, :] = (dot(grad, w_neigh[...], ((1,), (1,))) * inv).astype(BF16)
-
-    @pl.when(plane == 0)
-    def _():
-        own = [panel[pl.ds(pl.multiple_of((2 * h + core) * share, share), share), :] for h in range(2)]
-        grads[...] = dot(own[0], grad[:share], ((0,), (0,))) + dot(own[1], grad[share:], ((0,), (0,)))
-
-    @pl.when(plane != 0)
-    def _():
-        grads[...] = dot(aggregate, grad, ((0,), (0,)))
-
+    own = [panel[pl.ds(pl.multiple_of((2 * h + core) * share, share), share), :] for h in range(2)]
+    left = jnp.where(plane == 0, jnp.concatenate(own).astype(F32), aggregate.astype(F32)).astype(BF16)
+    grads[...] = dot(left, grad, ((0,), (0,)))
     rows = kept_grad.shape[0]
     kept_grad[...] = grads[pl.ds(pl.multiple_of(core * rows, rows), rows), :]
     message[half:, :] = grads[pl.ds(pl.multiple_of((1 - core) * rows, rows), rows), :].astype(BF16)

time: 58.6 us -> 58.3 us (level)
  no operation moved by 1% of the time
where the time goes in v5:
time: 58.3 us; the launch traced here: 58.1 us
  starting transfers between devices  25.2 us (43%)
  waiting for transfers between devices  22.7 us (39%)
  Pallas kernels  7.05 us (12%)
  local copies, waits for them, and re-layouts  1.26 us (2%)
  other arithmetic  1.01 us (2%)
  between operations  0.91 us (2%)
    ppermute x15, waiting for transfers between devices, exchange(): return lax.ppermute(value, BOTH, pairs)  21.1 us
    ppermute x15, starting transfers between devices, exchange(): return lax.ppermute(value, BOTH, pairs)  16.4 us
    pallas_call x5, Pallas kernels, kernel_call(): pl.pallas_call(kernel, out_shape=[jax.ShapeDtypeStruct(*out) for out in o...  7.05 us
    ppermute x1, starting transfers between devices, on_device(): moved.append(lax.ppermute(picked, BOTH, pairs))  4.85 us
    ppermute x2, starting transfers between devices, fetch(): return lax.ppermute(features, BOTH, pairs)  3.93 us
    ppermute x2, waiting for transfers between devices, fetch(): return lax.ppermute(features, BOTH, pairs)  1.56 us
  transfers between devices with their start and end apart: 18, of which 10 were waited for; matrix products, arithmetic and copies ran while one was open for 2% of the time, Pallas kernels for 5%

profile of v5, /device:TPU:0, one launch (start us, length us, event | category | flops | bytes accessed | tf_op | source)
XLA Modules:
  0.0 58.1 jit_solution(3518915603351501822)
XLA Ops:
  0.6 0.0 copy-start.4
  0.6 0.0 copy-start.5
  0.7 0.0 copy-start.2
  0.7 0.0 copy-start.3
  0.7 0.0 copy-start.6
  0.7 1.2 %picked_slot.1 = bf16[20,128,128]{2,1,0:T(8,128)(2,1)S(1)} custom-call(bf16[1,2,20,128,128]{4,3,2,1,0:T(8,128)(2,1)} %tiles.3), custom_call_target="tpu_custom_call" | custom-call | tf_op jit(solution)/shard_map/picked_slot/pallas_call | solution.py:191
  1.9 4.8 %collective-permute-start.2 = (bf16[20,128,128]{2,1,0:T(8,128)(2,1)S(1)}, bf16[20,128,128]{2,1,0:T(8,128)(2,1)S(1)}, u32[]{:S(2)}, u32[]{:S(2)}) collective-permute-start(bf16[20,128,128]{2,1,0:T(8,128)(2,1)S(1)} %picked_slot.1), channel_id=1, source_target_pairs={{0,2},{2,0},{8,10},{10,8},{16,18},{18,16},{24,26},{26,24}} | collective-permute-start | bytes 1966088 | tf_op jit(solution)/shard_map/ppermute | solution.py:256
  6.7 0.0 copy-done.4
  6.8 2.6 %collective-permute-start.3 = (bf16[512,256]{1,0:T(8,128)(2,1)S(1)}, bf16[512,256]{1,0:T(8,128)(2,1)S(1)}, u32[]{:S(2)}, u32[]{:S(2)}) collective-permute-start(bf16[512,256]{1,0:T(8,128)(2,1)S(1)} %copy-done.4), channel_id=1, source_target_pairs={{16,0},{25,1},{22,2},{15,3},{20,4},{29,5},{10,6},{19,7},{24,8},{1,... | collective-permute-start | bytes 786440 | tf_op jit(solution)/shard_map/ppermute | solution.py:236
  9.4 1.3 %collective-permute-start.4 = (bf16[512,256]{1,0:T(8,128)(2,1)S(1)}, bf16[512,256]{1,0:T(8,128)(2,1)S(1)}, u32[]{:S(2)}, u32[]{:S(2)}) collective-permute-start(bf16[512,256]{1,0:T(8,128)(2,1)S(1)} %copy-done.4), channel_id=1, source_target_pairs={{29,1},{6,2},{11,3},{24,4},{1,5},{15,7},{5,9},{14,10},{19,11},{0,1... | collective-permute-start | bytes 786440 | tf_op jit(solution)/shard_map/ppermute | solution.py:236
  10.7 0.0 copy-done.5
  10.7 0.1 collective-permute-start.1
  10.8 0.0 copy-done.2
  10.8 0.1 copy.14
  10.9 0.1 reshape_squeeze.6
  11.0 0.1 copy.15
  11.1 0.1 reshape_squeeze.7
  11.2 0.0 copy-done.3
  11.2 0.0 copy-done.6
  11.3 0.1 fusion.5
  11.3 2.0 %collective-permute-start = (s32[256]{0:T(256)S(1)}, s32[256]{0:T(256)S(1)}, u32[]{:S(2)}, u32[]{:S(2)}) collective-permute-start(s32[256]{0:T(256)S(1)} %fusion.5), channel_id=1, source_target_pairs={{0,2},{1,3},{2,0},{3,1},{4,6},{5,7},{6,4},{7,5},{8,10},{9,11},{10,... | collective-permute-start | bytes 3080 | tf_op jit(solution)/shard_map/ppermute | solution.py:25
  13.3 3.4 %collective-permute-done.note = s32[256]{0:T(256)S(1)} collective-permute-done((s32[256]{0:T(256)S(1)}, s32[256]{0:T(256)S(1)}, u32[]{:S(2)}, u32[]{:S(2)}) %collective-permute-start) | collective-permute-done | bytes 1056 | tf_op jit(solution)/shard_map/ppermute | solution.py:25
  16.8 0.0 collective-permute-done.1.cot_far
  16.8 0.0 collective-permute-done.2.rest_0_
  16.8 1.4 %prepare.1 = (bf16[2,20,128,128]{3,2,1,0:T(8,128)(2,1)S(1)}, bf16[512,256]{1,0:T(8,128)(2,1)S(1)}, f32[256,256]{1,0:T(8,128)S(1)}, bf16[256,256]{1,0:T(8,128)(2,1)S(1)}, f32[256,256]{1,0:T(8,128)S(1)}) custom-call(bf16[1,2,20,128,128]{4,3,2,1,0:T(8,128)(2,1)} %tiles.3, bf16[512,256]{1,0:T(8,128)(2,1)} %features.1, bf16[128,256]{1,0:T(8,128)(2,1)} %cot_own.1, ...), custom_call_target="tpu_custom_call" | custom-call | tf_op jit(solution)/shard_map/prepare/pallas_call | solution.py:191
  18.1 1.6 %collective-permute-done.3.far = bf16[512,256]{1,0:T(8,128)(2,1)S(1)} collective-permute-done((bf16[512,256]{1,0:T(8,128)(2,1)S(1)}, bf16[512,256]{1,0:T(8,128)(2,1)S(1)}, u32[]{:S(2)}, u32[]{:S(2)}) %collective-permute-start.3) | collective-permute-done | bytes 262176 | tf_op jit(solution)/shard_map/ppermute | solution.py:236
  19.7 0.0 collective-permute-done.4.near
  19.7 0.0 copy-start
  19.7 0.0 copy-start.1
  19.7 1.7 %forward.1 = (f32[256,256]{1,0:T(8,128)S(1)}, bf16[256,256]{1,0:T(8,128)(2,1)S(1)}) custom-call(s32[1,2,2,20]{3,2,1,0:T(2,128)S(1)} %bitcast.23, s32[1,2,20]{2,1,0:T(2,128)S(1)} %copy-done.3, s32[256]{0:T(256)S(1)} %collective-permute-done.note, bf16[2,20,128,128]{3,2,1,0:T(8,128)(2,1)S(1)} %get-tuple-element.22.tiles, ...), custom_call_target="tpu_custom_call" | custom-call | tf_op jit(solution)/shard_map/forward/pallas_call | solution.py:191
  21.4 0.1 collective-permute-start.5
  21.5 1.3 %collective-permute-done.5 = bf16[256,256]{1,0:T(8,128)(2,1)S(1)} collective-permute-done((bf16[256,256]{1,0:T(8,128)(2,1)S(1)}, bf16[256,256]{1,0:T(8,128)(2,1)S(1)}, u32[]{:S(2)}, u32[]{:S(2)}) %collective-permute-start.5) | collective-permute-done | bytes 131104 | tf_op jit(solution)/shard_map/ppermute | solution.py:25
  22.9 0.6 %collective-permute-start.6 = (bf16[256,256]{1,0:T(8,128)(2,1)S(1)}, bf16[256,256]{1,0:T(8,128)(2,1)S(1)}, u32[]{:S(2)}, u32[]{:S(2)}) collective-permute-start(bf16[256,256]{1,0:T(8,128)(2,1)S(1)} %get-tuple-element.40), channel_id=1, source_target_pairs={{0,2},{1,3},{2,0},{3,1},{4,6},{5,7},{6,4},{7,5},{8,10},{9,11},{10,... | collective-permute-start | bytes 393224 | tf_op jit(solution)/shard_map/ppermute | solution.py:25
  23.5 5.0 %collective-permute-done.6.far_sum = bf16[256,256]{1,0:T(8,128)(2,1)S(1)} collective-permute-done((bf16[256,256]{1,0:T(8,128)(2,1)S(1)}, bf16[256,256]{1,0:T(8,128)(2,1)S(1)}, u32[]{:S(2)}, u32[]{:S(2)}) %collective-permute-start.6) | collective-permute-done | bytes 131104 | tf_op jit(solution)/shard_map/ppermute | solution.py:25
  28.5 0.0 copy-done
  28.5 0.0 copy-done.1
  28.5 1.1 %middle.1 = (bf16[128,256]{1,0:T(8,128)(2,1)}, f32[128,256]{1,0:T(8,128)S(1)}, bf16[384,256]{1,0:T(8,128)(2,1)S(1)}, f32[128,256]{1,0:T(8,128)S(1)}) custom-call(f32[256,256]{1,0:T(8,128)S(1)} %get-tuple-element.41.chip_sum, bf16[256,256]{1,0:T(8,128)(2,1)S(1)} %collective-permute-done.6.far_sum, f32[256,256]{1,0:T(8,128)S(1)} %get-tuple-element.26.inv_root, ...), custom_call_target="tpu_custom_call" | custom-call | tf_op jit(solution)/shard_map/middle/pallas_call | solution.py:191
  29.6 0.0 collective-permute-start.7
  29.6 1.4 %collective-permute-done.7.other = bf16[384,256]{1,0:T(8,128)(2,1)S(1)} collective-permute-done((bf16[384,256]{1,0:T(8,128)(2,1)S(1)}, bf16[384,256]{1,0:T(8,128)(2,1)S(1)}, u32[]{:S(2)}, u32[]{:S(2)}) %collective-permute-start.7) | collective-permute-done | bytes 196640 | tf_op jit(solution)/shard_map/ppermute | solution.py:25
  31.1 1.7 %collective-permute-start.13 = (bf16[128,256]{1,0:T(8,128)(2,1)S(1)}, bf16[128,256]{1,0:T(8,128)(2,1)S(1)}, u32[]{:S(2)}, u32[]{:S(2)}) collective-permute-start(bf16[128,256]{1,0:T(8,128)(2,1)S(1)} %add_convert_fusion.3), channel_id=1, source_target_pairs={{0,16},{1,17},{2,18},{3,19},{4,20},{5,21},{6,22},{7,23},{8,24},{9,... | collective-permute-start | bytes 196616 | tf_op jit(solution)/shard_map/ppermute | solution.py:25
  32.7 1.7 %backward.1 = (bf16[256,256]{1,0:T(8,128)(2,1)S(1)}, bf16[256,256]{1,0:T(8,128)(2,1)S(1)}, bf16[256,256]{1,0:T(8,128)(2,1)S(1)}, bf16[256,256]{1,0:T(8,128)(2,1)S(1)}) custom-call(s32[1,2,2,20]{3,2,1,0:T(2,128)S(1)} %bitcast.24, s32[1,2,20]{2,1,0:T(2,128)S(1)} %copy-done.3, s32[256]{0:T(256)S(1)} %collective-permute-done.note, ...), custom_call_target="tpu_custom_call" | custom-call | tf_op jit(solution)/shard_map/backward/pallas_call | solution.py:191
  34.4 1.4 %collective-permute-start.8 = (bf16[256,256]{1,0:T(8,128)(2,1)S(1)}, bf16[256,256]{1,0:T(8,128)(2,1)S(1)}, u32[]{:S(2)}, u32[]{:S(2)}) collective-permute-start(bf16[256,256]{1,0:T(8,128)(2,1)S(1)} %get-tuple-element.32), channel_id=1, source_target_pairs={{0,18},{1,27},{2,20},{3,13},{4,22},{5,31},{6,8},{7,17},{8,26},{9,3... | collective-permute-start | bytes 393224 | tf_op jit(solution)/shard_map/ppermute | solution.py:25
  35.8 1.8 %collective-permute-done.13 = bf16[128,256]{1,0:T(8,128)(2,1)S(1)} collective-permute-done((bf16[128,256]{1,0:T(8,128)(2,1)S(1)}, bf16[128,256]{1,0:T(8,128)(2,1)S(1)}, u32[]{:S(2)}, u32[]{:S(2)}) %collective-permute-start.13) | collective-permute-done | bytes 65568 | tf_op jit(solution)/shard_map/ppermute | solution.py:25
  37.6 0.2 collective-permute-start.14
  37.8 2.9 %collective-permute-start.9 = (bf16[256,256]{1,0:T(8,128)(2,1)S(1)}, bf16[256,256]{1,0:T(8,128)(2,1)S(1)}, u32[]{:S(2)}, u32[]{:S(2)}) collective-permute-start(bf16[256,256]{1,0:T(8,128)(2,1)S(1)} %get-tuple-element.33), channel_id=1, source_target_pairs={{0,16},{1,25},{2,22},{3,15},{4,20},{5,29},{6,10},{7,19},{8,24},{9,... | collective-permute-start | bytes 393224 | tf_op jit(solution)/shard_map/ppermute | solution.py:25
  40.7 0.7 %collective-permute-start.10 = (bf16[256,256]{1,0:T(8,128)(2,1)S(1)}, bf16[256,256]{1,0:T(8,128)(2,1)S(1)}, u32[]{:S(2)}, u32[]{:S(2)}) collective-permute-start(bf16[256,256]{1,0:T(8,128)(2,1)S(1)} %get-tuple-element.34), channel_id=1, source_target_pairs={{0,0},{1,31},{2,4},{3,9},{4,26},{5,3},{6,6},{7,13},{8,8},{9,7},{10... | collective-permute-start | bytes 393224 | tf_op jit(solution)/shard_map/ppermute | solution.py:25
  41.4 3.3 %collective-permute-start.11 = (bf16[256,256]{1,0:T(8,128)(2,1)S(1)}, bf16[256,256]{1,0:T(8,128)(2,1)S(1)}, u32[]{:S(2)}, u32[]{:S(2)}) collective-permute-start(bf16[256,256]{1,0:T(8,128)(2,1)S(1)} %get-tuple-element.35), channel_id=1, source_target_pairs={{0,2},{1,29},{2,6},{3,11},{4,24},{5,1},{6,4},{7,15},{8,10},{9,5},{... | collective-permute-start | bytes 393224 | tf_op jit(solution)/shard_map/ppermute | solution.py:25
  44.7 0.0 collective-permute-done.8
  44.7 0.0 collective-permute-done.14
  44.7 2.4 %collective-permute-start.15 = (bf16[128,256]{1,0:T(8,128)(2,1)S(1)}, bf16[128,256]{1,0:T(8,128)(2,1)S(1)}, u32[]{:S(2)}, u32[]{:S(2)}) collective-permute-start(bf16[128,256]{1,0:T(8,128)(2,1)S(1)} %add_convert_fusion.1), channel_id=1, source_target_pairs={{0,4},{1,5},{2,6},{3,7},{4,0},{5,1},{6,2},{7,3},{8,12},{9,13},{10,... | collective-permute-start | bytes 196616 | tf_op jit(solution)/shard_map/ppermute | solution.py:25
  47.1 1.2 %collective-permute-done.9 = bf16[256,256]{1,0:T(8,128)(2,1)S(1)} collective-permute-done((bf16[256,256]{1,0:T(8,128)(2,1)S(1)}, bf16[256,256]{1,0:T(8,128)(2,1)S(1)}, u32[]{:S(2)}, u32[]{:S(2)}) %collective-permute-start.9) | collective-permute-done | bytes 131104 | tf_op jit(solution)/shard_map/ppermute | solution.py:25
  48.3 0.0 collective-permute-done.10
  48.3 3.0 %collective-permute-done.11 = bf16[256,256]{1,0:T(8,128)(2,1)S(1)} collective-permute-done((bf16[256,256]{1,0:T(8,128)(2,1)S(1)}, bf16[256,256]{1,0:T(8,128)(2,1)S(1)}, u32[]{:S(2)}, u32[]{:S(2)}) %collective-permute-start.11) | collective-permute-done | bytes 131104 | tf_op jit(solution)/shard_map/ppermute | solution.py:25
  51.3 0.1 convert_add_fusion
  51.4 0.0 collective-permute-done.15
  51.4 1.0 %collective-permute-start.16 = (bf16[128,256]{1,0:T(8,128)(2,1)S(1)}, bf16[128,256]{1,0:T(8,128)(2,1)S(1)}, u32[]{:S(2)}, u32[]{:S(2)}) collective-permute-start(bf16[128,256]{1,0:T(8,128)(2,1)S(1)} %add_convert_fusion), channel_id=1, source_target_pairs={{0,2},{1,3},{2,0},{3,1},{4,6},{5,7},{6,4},{7,5},{8,10},{9,11},{10,... | collective-permute-start | bytes 196616 | tf_op jit(solution)/shard_map/ppermute | solution.py:25
  52.4 0.1 collective-permute-start.12
  52.5 3.3 %collective-permute-done.16 = bf16[128,256]{1,0:T(8,128)(2,1)S(1)} collective-permute-done((bf16[128,256]{1,0:T(8,128)(2,1)S(1)}, bf16[128,256]{1,0:T(8,128)(2,1)S(1)}, u32[]{:S(2)}, u32[]{:S(2)}) %collective-permute-start.16) | collective-permute-done | bytes 65568 | tf_op jit(solution)/shard_map/ppermute | solution.py:25
  55.8 0.1 collective-permute-start.17
  55.9 0.0 collective-permute-done.12
  55.9 0.7 %fusion.1 = bf16[128,256]{1,0:T(8,128)(2,1)} fusion(f32[128,256]{1,0:T(8,128)S(1)} %get-tuple-element.30, bf16[128,256]{1,0:T(8,128)(2,1)S(1)} %collective-permute-done.12, f32[2,128,256]{2,1,0:T(8,128)S(1)} %bitcast.27, s32[]{:T(128)S(6)} %select_n.59), kind=kLoop, calls=%fused_computation.8 | loop fusion | flops 131072 | bytes 393220 | tf_op jit(solution)/shard_map/convert_element_type | solution.py:327
  56.6 0.6 %collective-permute-done.17 = bf16[2,128,256]{2,1,0:T(8,128)(2,1)S(1)} collective-permute-done((bf16[2,128,256]{2,1,0:T(8,128)(2,1)S(1)}, bf16[2,128,256]{2,1,0:T(8,128)(2,1)S(1)}, u32[]{:S(2)}, u32[]{:S(2)}) %collective-permute-start.17) | collective-permute-done | bytes 131104 | tf_op jit(solution)/shard_map/ppermute | solution.py:25
  57.2 0.1 convert_multiply_fusion
  57.3 0.8 %fusion.7 = (f32[1,2,128,256]{3,2,0,1:T(8,128)}, f32[1,2,128,256]{3,2,0,1:T(8,128)}) fusion(f32[2,2,128,256]{3,2,0,1:T(8,128)S(1)} %convert_multiply_fusion), kind=kLoop, calls=%fused_computation.25 | loop fusion | bytes 1048576 | tf_op jit(solution)/shard_map/slice | solution.py:328
  (11 shorter events, 0.2 us)
Async XLA Ops:
  0.6 6.1 %copy-start.4 = (bf16[512,256]{1,0:T(8,128)(2,1)S(1)}, bf16[512,256]{1,0:T(8,128)(2,1)}, u32[]{:S(2)}) copy-start(bf16[512,256]{1,0:T(8,128)(2,1)} %features.1) | copy-start | bytes 786436
  0.6 10.1 %copy-start.5 = (bf16[128,256]{1,0:T(8,128)(2,1)S(1)}, bf16[128,256]{1,0:T(8,128)(2,1)}, u32[]{:S(2)}) copy-start(bf16[128,256]{1,0:T(8,128)(2,1)} %cot_own.1) | copy-start | bytes 196612
  0.7 10.2 %copy-start.2 = (s32[1,2,20,2]{2,3,1,0:T(2,128)S(1)}, s32[1,2,20,2]{2,3,1,0:T(2,128)}, u32[]{:S(2)}) copy-start(s32[1,2,20,2]{2,3,1,0:T(2,128)} %param.9) | copy-start | bytes 964
  0.7 10.6 %copy-start.3 = (s32[1,2,20]{2,1,0:T(2,128)S(1)}, s32[1,2,20]{2,1,0:T(2,128)}, u32[]{:S(2)}) copy-start(s32[1,2,20]{2,1,0:T(2,128)} %live.3) | copy-start | bytes 484
  0.7 10.6 %copy-start.6 = (s32[128]{0:T(128)S(1)}, s32[128]{0:T(128)}, u32[]{:S(2)}) copy-start(s32[128]{0:T(128)} %param.12) | copy-start | bytes 1540
  1.9 14.9 %collective-permute-start.2 = (bf16[20,128,128]{2,1,0:T(8,128)(2,1)S(1)}, bf16[20,128,128]{2,1,0:T(8,128)(2,1)S(1)}, u32[]{:S(2)}, u32[]{:S(2)}) collective-permute-start(bf16[20,128,128]{2,1,0:T(8,128)(2,1)S(1)} %picked_slot.1), channel_id=1, source_target_pairs={{0,2},{2,0},{8,10},{10,8},{16,18},{18,16},{24,26},{26,24}} | collective-permute-start | bytes 1966088 | tf_op jit(solution)/shard_map/ppermute | solution.py:256
  6.8 12.9 %collective-permute-start.3 = (bf16[512,256]{1,0:T(8,128)(2,1)S(1)}, bf16[512,256]{1,0:T(8,128)(2,1)S(1)}, u32[]{:S(2)}, u32[]{:S(2)}) collective-permute-start(bf16[512,256]{1,0:T(8,128)(2,1)S(1)} %copy-done.4), channel_id=1, source_target_pairs={{16,0},{25,1},{22,2},{15,3},{20,4},{29,5},{10,6},{19,7},{24,8},{1,... | collective-permute-start | bytes 786440 | tf_op jit(solution)/shard_map/ppermute | solution.py:236
  9.4 10.3 %collective-permute-start.4 = (bf16[512,256]{1,0:T(8,128)(2,1)S(1)}, bf16[512,256]{1,0:T(8,128)(2,1)S(1)}, u32[]{:S(2)}, u32[]{:S(2)}) collective-permute-start(bf16[512,256]{1,0:T(8,128)(2,1)S(1)} %copy-done.4), channel_id=1, source_target_pairs={{29,1},{6,2},{11,3},{24,4},{1,5},{15,7},{5,9},{14,10},{19,11},{0,1... | collective-permute-start | bytes 786440 | tf_op jit(solution)/shard_map/ppermute | solution.py:236
  10.7 6.1 %collective-permute-start.1 = (bf16[128,256]{1,0:T(8,128)(2,1)S(1)}, bf16[128,256]{1,0:T(8,128)(2,1)S(1)}, u32[]{:S(2)}, u32[]{:S(2)}) collective-permute-start(bf16[128,256]{1,0:T(8,128)(2,1)S(1)} %copy-done.5), channel_id=1, source_target_pairs={{0,2},{1,3},{2,0},{3,1},{4,6},{5,7},{6,4},{7,5},{8,10},{9,11},{10,... | collective-permute-start | bytes 196616 | tf_op jit(solution)/shard_map/ppermute | solution.py:25
  11.3 5.4 %collective-permute-start = (s32[256]{0:T(256)S(1)}, s32[256]{0:T(256)S(1)}, u32[]{:S(2)}, u32[]{:S(2)}) collective-permute-start(s32[256]{0:T(256)S(1)} %fusion.5), channel_id=1, source_target_pairs={{0,2},{1,3},{2,0},{3,1},{4,6},{5,7},{6,4},{7,5},{8,10},{9,11},{10,... | collective-permute-start | bytes 3080 | tf_op jit(solution)/shard_map/ppermute | solution.py:25
  19.7 8.8 %copy-start = (bf16[256,256]{1,0:T(8,128)(2,1)S(1)}, bf16[256,256]{1,0:T(8,128)(2,1)}, u32[]{:S(2)}) copy-start(bf16[256,256]{1,0:T(8,128)(2,1)} %w_self.3) | copy-start | bytes 393220
  19.7 8.8 %copy-start.1 = (bf16[256,256]{1,0:T(8,128)(2,1)S(1)}, bf16[256,256]{1,0:T(8,128)(2,1)}, u32[]{:S(2)}) copy-start(bf16[256,256]{1,0:T(8,128)(2,1)} %w_neigh.1) | copy-start | bytes 393220
  21.4 1.4 %collective-permute-start.5 = (bf16[256,256]{1,0:T(8,128)(2,1)S(1)}, bf16[256,256]{1,0:T(8,128)(2,1)S(1)}, u32[]{:S(2)}, u32[]{:S(2)}) collective-permute-start(bf16[256,256]{1,0:T(8,128)(2,1)S(1)} %get-tuple-element.25), channel_id=1, source_target_pairs={{0,1},{1,0},{2,3},{3,2},{4,5},{5,4},{6,7},{7,6},{8,9},{9,8},{10,11... | collective-permute-start | bytes 393224 | tf_op jit(solution)/shard_map/ppermute | solution.py:25
  22.9 5.6 %collective-permute-start.6 = (bf16[256,256]{1,0:T(8,128)(2,1)S(1)}, bf16[256,256]{1,0:T(8,128)(2,1)S(1)}, u32[]{:S(2)}, u32[]{:S(2)}) collective-permute-start(bf16[256,256]{1,0:T(8,128)(2,1)S(1)} %get-tuple-element.40), channel_id=1, source_target_pairs={{0,2},{1,3},{2,0},{3,1},{4,6},{5,7},{6,4},{7,5},{8,10},{9,11},{10,... | collective-permute-start | bytes 393224 | tf_op jit(solution)/shard_map/ppermute | solution.py:25
  29.6 1.4 %collective-permute-start.7 = (bf16[384,256]{1,0:T(8,128)(2,1)S(1)}, bf16[384,256]{1,0:T(8,128)(2,1)S(1)}, u32[]{:S(2)}, u32[]{:S(2)}) collective-permute-start(bf16[384,256]{1,0:T(8,128)(2,1)S(1)} %get-tuple-element.31.own), channel_id=1, source_target_pairs={{0,1},{1,0},{2,3},{3,2},{4,5},{5,4},{6,7},{7,6},{8,9},{9,8},{10,11... | collective-permute-start | bytes 589832 | tf_op jit(solution)/shard_map/ppermute | solution.py:25
  31.1 6.5 %collective-permute-start.13 = (bf16[128,256]{1,0:T(8,128)(2,1)S(1)}, bf16[128,256]{1,0:T(8,128)(2,1)S(1)}, u32[]{:S(2)}, u32[]{:S(2)}) collective-permute-start(bf16[128,256]{1,0:T(8,128)(2,1)S(1)} %add_convert_fusion.3), channel_id=1, source_target_pairs={{0,16},{1,17},{2,18},{3,19},{4,20},{5,21},{6,22},{7,23},{8,24},{9,... | collective-permute-start | bytes 196616 | tf_op jit(solution)/shard_map/ppermute | solution.py:25
  34.4 10.3 %collective-permute-start.8 = (bf16[256,256]{1,0:T(8,128)(2,1)S(1)}, bf16[256,256]{1,0:T(8,128)(2,1)S(1)}, u32[]{:S(2)}, u32[]{:S(2)}) collective-permute-start(bf16[256,256]{1,0:T(8,128)(2,1)S(1)} %get-tuple-element.32), channel_id=1, source_target_pairs={{0,18},{1,27},{2,20},{3,13},{4,22},{5,31},{6,8},{7,17},{8,26},{9,3... | collective-permute-start | bytes 393224 | tf_op jit(solution)/shard_map/ppermute | solution.py:25
  37.6 7.1 %collective-permute-start.14 = (bf16[128,256]{1,0:T(8,128)(2,1)S(1)}, bf16[128,256]{1,0:T(8,128)(2,1)S(1)}, u32[]{:S(2)}, u32[]{:S(2)}) collective-permute-start(bf16[128,256]{1,0:T(8,128)(2,1)S(1)} %add_convert_fusion.2), channel_id=1, source_target_pairs={{0,8},{1,9},{2,10},{3,11},{4,12},{5,13},{6,14},{7,15},{8,0},{9,1},... | collective-permute-start | bytes 196616 | tf_op jit(solution)/shard_map/ppermute | solution.py:25
  37.8 10.5 %collective-permute-start.9 = (bf16[256,256]{1,0:T(8,128)(2,1)S(1)}, bf16[256,256]{1,0:T(8,128)(2,1)S(1)}, u32[]{:S(2)}, u32[]{:S(2)}) collective-permute-start(bf16[256,256]{1,0:T(8,128)(2,1)S(1)} %get-tuple-element.33), channel_id=1, source_target_pairs={{0,16},{1,25},{2,22},{3,15},{4,20},{5,29},{6,10},{7,19},{8,24},{9,... | collective-permute-start | bytes 393224 | tf_op jit(solution)/shard_map/ppermute | solution.py:25
  40.7 7.6 %collective-permute-start.10 = (bf16[256,256]{1,0:T(8,128)(2,1)S(1)}, bf16[256,256]{1,0:T(8,128)(2,1)S(1)}, u32[]{:S(2)}, u32[]{:S(2)}) collective-permute-start(bf16[256,256]{1,0:T(8,128)(2,1)S(1)} %get-tuple-element.34), channel_id=1, source_target_pairs={{0,0},{1,31},{2,4},{3,9},{4,26},{5,3},{6,6},{7,13},{8,8},{9,7},{10... | collective-permute-start | bytes 393224 | tf_op jit(solution)/shard_map/ppermute | solution.py:25
  41.4 9.9 %collective-permute-start.11 = (bf16[256,256]{1,0:T(8,128)(2,1)S(1)}, bf16[256,256]{1,0:T(8,128)(2,1)S(1)}, u32[]{:S(2)}, u32[]{:S(2)}) collective-permute-start(bf16[256,256]{1,0:T(8,128)(2,1)S(1)} %get-tuple-element.35), channel_id=1, source_target_pairs={{0,2},{1,29},{2,6},{3,11},{4,24},{5,1},{6,4},{7,15},{8,10},{9,5},{... | collective-permute-start | bytes 393224 | tf_op jit(solution)/shard_map/ppermute | solution.py:25
  44.7 6.7 %collective-permute-start.15 = (bf16[128,256]{1,0:T(8,128)(2,1)S(1)}, bf16[128,256]{1,0:T(8,128)(2,1)S(1)}, u32[]{:S(2)}, u32[]{:S(2)}) collective-permute-start(bf16[128,256]{1,0:T(8,128)(2,1)S(1)} %add_convert_fusion.1), channel_id=1, source_target_pairs={{0,4},{1,5},{2,6},{3,7},{4,0},{5,1},{6,2},{7,3},{8,12},{9,13},{10,... | collective-permute-start | bytes 196616 | tf_op jit(solution)/shard_map/ppermute | solution.py:25
  51.4 4.3 %collective-permute-start.16 = (bf16[128,256]{1,0:T(8,128)(2,1)S(1)}, bf16[128,256]{1,0:T(8,128)(2,1)S(1)}, u32[]{:S(2)}, u32[]{:S(2)}) collective-permute-start(bf16[128,256]{1,0:T(8,128)(2,1)S(1)} %add_convert_fusion), channel_id=1, source_target_pairs={{0,2},{1,3},{2,0},{3,1},{4,6},{5,7},{6,4},{7,5},{8,10},{9,11},{10,... | collective-permute-start | bytes 196616 | tf_op jit(solution)/shard_map/ppermute | solution.py:25
  52.4 3.4 %collective-permute-start.12 = (bf16[128,256]{1,0:T(8,128)(2,1)S(1)}, bf16[128,256]{1,0:T(8,128)(2,1)S(1)}, u32[]{:S(2)}, u32[]{:S(2)}) collective-permute-start(bf16[128,256]{1,0:T(8,128)(2,1)S(1)} %fusion.2), channel_id=1, source_target_pairs={{0,1},{1,0},{2,3},{3,2},{4,5},{5,4},{6,7},{7,6},{8,9},{9,8},{10,11... | collective-permute-start | bytes 196616 | tf_op jit(solution)/shard_map/ppermute | solution.py:25
  55.8 1.4 %collective-permute-start.17 = (bf16[2,128,256]{2,1,0:T(8,128)(2,1)S(1)}, bf16[2,128,256]{2,1,0:T(8,128)(2,1)S(1)}, u32[]{:S(2)}, u32[]{:S(2)}) collective-permute-start(bf16[2,128,256]{2,1,0:T(8,128)(2,1)S(1)} %maximum_select_fusion.2), channel_id=1, source_target_pairs={{0,1},{1,0},{2,3},{3,2},{4,5},{5,4},{6,7},{7,6},{8,9},{9,8},{10,11... | collective-permute-start | bytes 393224 | tf_op jit(solution)/shard_map/ppermute | solution.py:25

commit v6 on v5

--- a/solution.py
+++ b/solution.py
@@ -312,6 +312,8 @@
     ]
 
     rounded = added(rounded, tied(others(rounded, 1 << top), sends[0]))
+    for i in range(top - 1, 1, -1):
+        rounded = added(rounded, others(rounded, 1 << i))
     rounded = added(rounded, tied(others(rounded, 2), arrived[0]))
     rounded = added(rounded, tied(others(rounded, 1), arrived[1]))
     twin = flip_plane(rounded)

time: 58.3 us -> 58.3 us (level)
  no operation moved by 1% of the time
where the time goes in v6:
time: 58.3 us; the launch traced here: 58.1 us
  starting transfers between devices  25.2 us (43%)
  waiting for transfers between devices  22.7 us (39%)
  Pallas kernels  7.05 us (12%)
  local copies, waits for them, and re-layouts  1.26 us (2%)
  other arithmetic  1.01 us (2%)
  between operations  0.91 us (2%)
    ppermute x15, waiting for transfers between devices, exchange(): return lax.ppermute(value, BOTH, pairs)  21.1 us
    ppermute x15, starting transfers between devices, exchange(): return lax.ppermute(value, BOTH, pairs)  16.4 us
    pallas_call x5, Pallas kernels, kernel_call(): pl.pallas_call(kernel, out_shape=[jax.ShapeDtypeStruct(*out) for out in o...  7.05 us
    ppermute x1, starting transfers between devices, on_device(): moved.append(lax.ppermute(picked, BOTH, pairs))  4.85 us
    ppermute x2, starting transfers between devices, fetch(): return lax.ppermute(features, BOTH, pairs)  3.93 us
    ppermute x2, waiting for transfers between devices, fetch(): return lax.ppermute(features, BOTH, pairs)  1.56 us
  transfers between devices with their start and end apart: 18, of which 10 were waited for; matrix products, arithmetic and copies ran while one was open for 2% of the time, Pallas kernels for 5%

profile of v6, /device:TPU:0, one launch (start us, length us, event | category | flops | bytes accessed | tf_op | source)
XLA Modules:
  0.0 58.1 jit_solution(3518915603351501822)
XLA Ops:
  0.6 0.0 copy-start.4
  0.6 0.0 copy-start.5
  0.7 0.0 copy-start.2
  0.7 0.0 copy-start.3
  0.7 0.0 copy-start.6
  0.7 1.2 %picked_slot.1 = bf16[20,128,128]{2,1,0:T(8,128)(2,1)S(1)} custom-call(bf16[1,2,20,128,128]{4,3,2,1,0:T(8,128)(2,1)} %tiles.3), custom_call_target="tpu_custom_call" | custom-call | tf_op jit(solution)/shard_map/picked_slot/pallas_call | solution.py:191
  1.9 4.8 %collective-permute-start.2 = (bf16[20,128,128]{2,1,0:T(8,128)(2,1)S(1)}, bf16[20,128,128]{2,1,0:T(8,128)(2,1)S(1)}, u32[]{:S(2)}, u32[]{:S(2)}) collective-permute-start(bf16[20,128,128]{2,1,0:T(8,128)(2,1)S(1)} %picked_slot.1), channel_id=1, source_target_pairs={{0,2},{2,0},{8,10},{10,8},{16,18},{18,16},{24,26},{26,24}} | collective-permute-start | bytes 1966088 | tf_op jit(solution)/shard_map/ppermute | solution.py:256
  6.7 0.0 copy-done.4
  6.8 2.6 %collective-permute-start.3 = (bf16[512,256]{1,0:T(8,128)(2,1)S(1)}, bf16[512,256]{1,0:T(8,128)(2,1)S(1)}, u32[]{:S(2)}, u32[]{:S(2)}) collective-permute-start(bf16[512,256]{1,0:T(8,128)(2,1)S(1)} %copy-done.4), channel_id=1, source_target_pairs={{16,0},{25,1},{22,2},{15,3},{20,4},{29,5},{10,6},{19,7},{24,8},{1,... | collective-permute-start | bytes 786440 | tf_op jit(solution)/shard_map/ppermute | solution.py:236
  9.4 1.3 %collective-permute-start.4 = (bf16[512,256]{1,0:T(8,128)(2,1)S(1)}, bf16[512,256]{1,0:T(8,128)(2,1)S(1)}, u32[]{:S(2)}, u32[]{:S(2)}) collective-permute-start(bf16[512,256]{1,0:T(8,128)(2,1)S(1)} %copy-done.4), channel_id=1, source_target_pairs={{29,1},{6,2},{11,3},{24,4},{1,5},{15,7},{5,9},{14,10},{19,11},{0,1... | collective-permute-start | bytes 786440 | tf_op jit(solution)/shard_map/ppermute | solution.py:236
  10.7 0.0 copy-done.5
  10.7 0.1 collective-permute-start.1
  10.8 0.0 copy-done.2
  10.8 0.1 copy.14
  10.9 0.1 reshape_squeeze.6
  11.0 0.1 copy.15
  11.1 0.1 reshape_squeeze.7
  11.2 0.0 copy-done.3
  11.2 0.0 copy-done.6
  11.3 0.1 fusion.5
  11.3 2.0 %collective-permute-start = (s32[256]{0:T(256)S(1)}, s32[256]{0:T(256)S(1)}, u32[]{:S(2)}, u32[]{:S(2)}) collective-permute-start(s32[256]{0:T(256)S(1)} %fusion.5), channel_id=1, source_target_pairs={{0,2},{1,3},{2,0},{3,1},{4,6},{5,7},{6,4},{7,5},{8,10},{9,11},{10,... | collective-permute-start | bytes 3080 | tf_op jit(solution)/shard_map/ppermute | solution.py:25
  13.3 3.4 %collective-permute-done.note = s32[256]{0:T(256)S(1)} collective-permute-done((s32[256]{0:T(256)S(1)}, s32[256]{0:T(256)S(1)}, u32[]{:S(2)}, u32[]{:S(2)}) %collective-permute-start) | collective-permute-done | bytes 1056 | tf_op jit(solution)/shard_map/ppermute | solution.py:25
  16.8 0.0 collective-permute-done.1.cot_far
  16.8 0.0 collective-permute-done.2.rest_0_
  16.8 1.4 %prepare.1 = (bf16[2,20,128,128]{3,2,1,0:T(8,128)(2,1)S(1)}, bf16[512,256]{1,0:T(8,128)(2,1)S(1)}, f32[256,256]{1,0:T(8,128)S(1)}, bf16[256,256]{1,0:T(8,128)(2,1)S(1)}, f32[256,256]{1,0:T(8,128)S(1)}) custom-call(bf16[1,2,20,128,128]{4,3,2,1,0:T(8,128)(2,1)} %tiles.3, bf16[512,256]{1,0:T(8,128)(2,1)} %features.1, bf16[128,256]{1,0:T(8,128)(2,1)} %cot_own.1, ...), custom_call_target="tpu_custom_call" | custom-call | tf_op jit(solution)/shard_map/prepare/pallas_call | solution.py:191
  18.1 1.6 %collective-permute-done.3.far = bf16[512,256]{1,0:T(8,128)(2,1)S(1)} collective-permute-done((bf16[512,256]{1,0:T(8,128)(2,1)S(1)}, bf16[512,256]{1,0:T(8,128)(2,1)S(1)}, u32[]{:S(2)}, u32[]{:S(2)}) %collective-permute-start.3) | collective-permute-done | bytes 262176 | tf_op jit(solution)/shard_map/ppermute | solution.py:236
  19.7 0.0 collective-permute-done.4.near
  19.7 0.0 copy-start
  19.7 0.0 copy-start.1
  19.7 1.7 %forward.1 = (f32[256,256]{1,0:T(8,128)S(1)}, bf16[256,256]{1,0:T(8,128)(2,1)S(1)}) custom-call(s32[1,2,2,20]{3,2,1,0:T(2,128)S(1)} %bitcast.23, s32[1,2,20]{2,1,0:T(2,128)S(1)} %copy-done.3, s32[256]{0:T(256)S(1)} %collective-permute-done.note, bf16[2,20,128,128]{3,2,1,0:T(8,128)(2,1)S(1)} %get-tuple-element.22.tiles, ...), custom_call_target="tpu_custom_call" | custom-call | tf_op jit(solution)/shard_map/forward/pallas_call | solution.py:191
  21.4 0.1 collective-permute-start.5
  21.5 1.3 %collective-permute-done.5 = bf16[256,256]{1,0:T(8,128)(2,1)S(1)} collective-permute-done((bf16[256,256]{1,0:T(8,128)(2,1)S(1)}, bf16[256,256]{1,0:T(8,128)(2,1)S(1)}, u32[]{:S(2)}, u32[]{:S(2)}) %collective-permute-start.5) | collective-permute-done | bytes 131104 | tf_op jit(solution)/shard_map/ppermute | solution.py:25
  22.9 0.6 %collective-permute-start.6 = (bf16[256,256]{1,0:T(8,128)(2,1)S(1)}, bf16[256,256]{1,0:T(8,128)(2,1)S(1)}, u32[]{:S(2)}, u32[]{:S(2)}) collective-permute-start(bf16[256,256]{1,0:T(8,128)(2,1)S(1)} %get-tuple-element.40), channel_id=1, source_target_pairs={{0,2},{1,3},{2,0},{3,1},{4,6},{5,7},{6,4},{7,5},{8,10},{9,11},{10,... | collective-permute-start | bytes 393224 | tf_op jit(solution)/shard_map/ppermute | solution.py:25
  23.5 5.0 %collective-permute-done.6.far_sum = bf16[256,256]{1,0:T(8,128)(2,1)S(1)} collective-permute-done((bf16[256,256]{1,0:T(8,128)(2,1)S(1)}, bf16[256,256]{1,0:T(8,128)(2,1)S(1)}, u32[]{:S(2)}, u32[]{:S(2)}) %collective-permute-start.6) | collective-permute-done | bytes 131104 | tf_op jit(solution)/shard_map/ppermute | solution.py:25
  28.5 0.0 copy-done
  28.5 0.0 copy-done.1
  28.5 1.1 %middle.1 = (bf16[128,256]{1,0:T(8,128)(2,1)}, f32[128,256]{1,0:T(8,128)S(1)}, bf16[384,256]{1,0:T(8,128)(2,1)S(1)}, f32[128,256]{1,0:T(8,128)S(1)}) custom-call(f32[256,256]{1,0:T(8,128)S(1)} %get-tuple-element.41.chip_sum, bf16[256,256]{1,0:T(8,128)(2,1)S(1)} %collective-permute-done.6.far_sum, f32[256,256]{1,0:T(8,128)S(1)} %get-tuple-element.26.inv_root, ...), custom_call_target="tpu_custom_call" | custom-call | tf_op jit(solution)/shard_map/middle/pallas_call | solution.py:191
  29.6 0.0 collective-permute-start.7
  29.6 1.4 %collective-permute-done.7.other = bf16[384,256]{1,0:T(8,128)(2,1)S(1)} collective-permute-done((bf16[384,256]{1,0:T(8,128)(2,1)S(1)}, bf16[384,256]{1,0:T(8,128)(2,1)S(1)}, u32[]{:S(2)}, u32[]{:S(2)}) %collective-permute-start.7) | collective-permute-done | bytes 196640 | tf_op jit(solution)/shard_map/ppermute | solution.py:25
  31.1 1.7 %collective-permute-start.13 = (bf16[128,256]{1,0:T(8,128)(2,1)S(1)}, bf16[128,256]{1,0:T(8,128)(2,1)S(1)}, u32[]{:S(2)}, u32[]{:S(2)}) collective-permute-start(bf16[128,256]{1,0:T(8,128)(2,1)S(1)} %add_convert_fusion.3), channel_id=1, source_target_pairs={{0,16},{1,17},{2,18},{3,19},{4,20},{5,21},{6,22},{7,23},{8,24},{9,... | collective-permute-start | bytes 196616 | tf_op jit(solution)/shard_map/ppermute | solution.py:25
  32.7 1.7 %backward.1 = (bf16[256,256]{1,0:T(8,128)(2,1)S(1)}, bf16[256,256]{1,0:T(8,128)(2,1)S(1)}, bf16[256,256]{1,0:T(8,128)(2,1)S(1)}, bf16[256,256]{1,0:T(8,128)(2,1)S(1)}) custom-call(s32[1,2,2,20]{3,2,1,0:T(2,128)S(1)} %bitcast.24, s32[1,2,20]{2,1,0:T(2,128)S(1)} %copy-done.3, s32[256]{0:T(256)S(1)} %collective-permute-done.note, ...), custom_call_target="tpu_custom_call" | custom-call | tf_op jit(solution)/shard_map/backward/pallas_call | solution.py:191
  34.4 1.4 %collective-permute-start.8 = (bf16[256,256]{1,0:T(8,128)(2,1)S(1)}, bf16[256,256]{1,0:T(8,128)(2,1)S(1)}, u32[]{:S(2)}, u32[]{:S(2)}) collective-permute-start(bf16[256,256]{1,0:T(8,128)(2,1)S(1)} %get-tuple-element.32), channel_id=1, source_target_pairs={{0,18},{1,27},{2,20},{3,13},{4,22},{5,31},{6,8},{7,17},{8,26},{9,3... | collective-permute-start | bytes 393224 | tf_op jit(solution)/shard_map/ppermute | solution.py:25
  35.8 1.8 %collective-permute-done.13 = bf16[128,256]{1,0:T(8,128)(2,1)S(1)} collective-permute-done((bf16[128,256]{1,0:T(8,128)(2,1)S(1)}, bf16[128,256]{1,0:T(8,128)(2,1)S(1)}, u32[]{:S(2)}, u32[]{:S(2)}) %collective-permute-start.13) | collective-permute-done | bytes 65568 | tf_op jit(solution)/shard_map/ppermute | solution.py:25
  37.6 0.2 collective-permute-start.14
  37.8 2.9 %collective-permute-start.9 = (bf16[256,256]{1,0:T(8,128)(2,1)S(1)}, bf16[256,256]{1,0:T(8,128)(2,1)S(1)}, u32[]{:S(2)}, u32[]{:S(2)}) collective-permute-start(bf16[256,256]{1,0:T(8,128)(2,1)S(1)} %get-tuple-element.33), channel_id=1, source_target_pairs={{0,16},{1,25},{2,22},{3,15},{4,20},{5,29},{6,10},{7,19},{8,24},{9,... | collective-permute-start | bytes 393224 | tf_op jit(solution)/shard_map/ppermute | solution.py:25
  40.7 0.7 %collective-permute-start.10 = (bf16[256,256]{1,0:T(8,128)(2,1)S(1)}, bf16[256,256]{1,0:T(8,128)(2,1)S(1)}, u32[]{:S(2)}, u32[]{:S(2)}) collective-permute-start(bf16[256,256]{1,0:T(8,128)(2,1)S(1)} %get-tuple-element.34), channel_id=1, source_target_pairs={{0,0},{1,31},{2,4},{3,9},{4,26},{5,3},{6,6},{7,13},{8,8},{9,7},{10... | collective-permute-start | bytes 393224 | tf_op jit(solution)/shard_map/ppermute | solution.py:25
  41.4 3.3 %collective-permute-start.11 = (bf16[256,256]{1,0:T(8,128)(2,1)S(1)}, bf16[256,256]{1,0:T(8,128)(2,1)S(1)}, u32[]{:S(2)}, u32[]{:S(2)}) collective-permute-start(bf16[256,256]{1,0:T(8,128)(2,1)S(1)} %get-tuple-element.35), channel_id=1, source_target_pairs={{0,2},{1,29},{2,6},{3,11},{4,24},{5,1},{6,4},{7,15},{8,10},{9,5},{... | collective-permute-start | bytes 393224 | tf_op jit(solution)/shard_map/ppermute | solution.py:25
  44.7 0.0 collective-permute-done.8
  44.7 0.0 collective-permute-done.14
  44.7 2.4 %collective-permute-start.15 = (bf16[128,256]{1,0:T(8,128)(2,1)S(1)}, bf16[128,256]{1,0:T(8,128)(2,1)S(1)}, u32[]{:S(2)}, u32[]{:S(2)}) collective-permute-start(bf16[128,256]{1,0:T(8,128)(2,1)S(1)} %add_convert_fusion.1), channel_id=1, source_target_pairs={{0,4},{1,5},{2,6},{3,7},{4,0},{5,1},{6,2},{7,3},{8,12},{9,13},{10,... | collective-permute-start | bytes 196616 | tf_op jit(solution)/shard_map/ppermute | solution.py:25
  47.1 1.2 %collective-permute-done.9 = bf16[256,256]{1,0:T(8,128)(2,1)S(1)} collective-permute-done((bf16[256,256]{1,0:T(8,128)(2,1)S(1)}, bf16[256,256]{1,0:T(8,128)(2,1)S(1)}, u32[]{:S(2)}, u32[]{:S(2)}) %collective-permute-start.9) | collective-permute-done | bytes 131104 | tf_op jit(solution)/shard_map/ppermute | solution.py:25
  48.3 0.0 collective-permute-done.10
  48.3 3.0 %collective-permute-done.11 = bf16[256,256]{1,0:T(8,128)(2,1)S(1)} collective-permute-done((bf16[256,256]{1,0:T(8,128)(2,1)S(1)}, bf16[256,256]{1,0:T(8,128)(2,1)S(1)}, u32[]{:S(2)}, u32[]{:S(2)}) %collective-permute-start.11) | collective-permute-done | bytes 131104 | tf_op jit(solution)/shard_map/ppermute | solution.py:25
  51.3 0.1 convert_add_fusion
  51.4 0.0 collective-permute-done.15
  51.4 1.0 %collective-permute-start.16 = (bf16[128,256]{1,0:T(8,128)(2,1)S(1)}, bf16[128,256]{1,0:T(8,128)(2,1)S(1)}, u32[]{:S(2)}, u32[]{:S(2)}) collective-permute-start(bf16[128,256]{1,0:T(8,128)(2,1)S(1)} %add_convert_fusion), channel_id=1, source_target_pairs={{0,2},{1,3},{2,0},{3,1},{4,6},{5,7},{6,4},{7,5},{8,10},{9,11},{10,... | collective-permute-start | bytes 196616 | tf_op jit(solution)/shard_map/ppermute | solution.py:25
  52.4 0.1 collective-permute-start.12
  52.5 3.3 %collective-permute-done.16 = bf16[128,256]{1,0:T(8,128)(2,1)S(1)} collective-permute-done((bf16[128,256]{1,0:T(8,128)(2,1)S(1)}, bf16[128,256]{1,0:T(8,128)(2,1)S(1)}, u32[]{:S(2)}, u32[]{:S(2)}) %collective-permute-start.16) | collective-permute-done | bytes 65568 | tf_op jit(solution)/shard_map/ppermute | solution.py:25
  55.8 0.1 collective-permute-start.17
  55.9 0.0 collective-permute-done.12
  55.9 0.7 %fusion.1 = bf16[128,256]{1,0:T(8,128)(2,1)} fusion(f32[128,256]{1,0:T(8,128)S(1)} %get-tuple-element.30, bf16[128,256]{1,0:T(8,128)(2,1)S(1)} %collective-permute-done.12, f32[2,128,256]{2,1,0:T(8,128)S(1)} %bitcast.27, s32[]{:T(128)S(6)} %select_n.59), kind=kLoop, calls=%fused_computation.8 | loop fusion | flops 131072 | bytes 393220 | tf_op jit(solution)/shard_map/convert_element_type | solution.py:329
  56.6 0.6 %collective-permute-done.17 = bf16[2,128,256]{2,1,0:T(8,128)(2,1)S(1)} collective-permute-done((bf16[2,128,256]{2,1,0:T(8,128)(2,1)S(1)}, bf16[2,128,256]{2,1,0:T(8,128)(2,1)S(1)}, u32[]{:S(2)}, u32[]{:S(2)}) %collective-permute-start.17) | collective-permute-done | bytes 131104 | tf_op jit(solution)/shard_map/ppermute | solution.py:25
  57.2 0.1 convert_multiply_fusion
  57.3 0.8 %fusion.7 = (f32[1,2,128,256]{3,2,0,1:T(8,128)}, f32[1,2,128,256]{3,2,0,1:T(8,128)}) fusion(f32[2,2,128,256]{3,2,0,1:T(8,128)S(1)} %convert_multiply_fusion), kind=kLoop, calls=%fused_computation.25 | loop fusion | bytes 1048576 | tf_op jit(solution)/shard_map/slice | solution.py:330
  (11 shorter events, 0.2 us)
Async XLA Ops:
  0.6 6.1 %copy-start.4 = (bf16[512,256]{1,0:T(8,128)(2,1)S(1)}, bf16[512,256]{1,0:T(8,128)(2,1)}, u32[]{:S(2)}) copy-start(bf16[512,256]{1,0:T(8,128)(2,1)} %features.1) | copy-start | bytes 786436
  0.6 10.1 %copy-start.5 = (bf16[128,256]{1,0:T(8,128)(2,1)S(1)}, bf16[128,256]{1,0:T(8,128)(2,1)}, u32[]{:S(2)}) copy-start(bf16[128,256]{1,0:T(8,128)(2,1)} %cot_own.1) | copy-start | bytes 196612
  0.7 10.2 %copy-start.2 = (s32[1,2,20,2]{2,3,1,0:T(2,128)S(1)}, s32[1,2,20,2]{2,3,1,0:T(2,128)}, u32[]{:S(2)}) copy-start(s32[1,2,20,2]{2,3,1,0:T(2,128)} %param.9) | copy-start | bytes 964
  0.7 10.6 %copy-start.3 = (s32[1,2,20]{2,1,0:T(2,128)S(1)}, s32[1,2,20]{2,1,0:T(2,128)}, u32[]{:S(2)}) copy-start(s32[1,2,20]{2,1,0:T(2,128)} %live.3) | copy-start | bytes 484
  0.7 10.6 %copy-start.6 = (s32[128]{0:T(128)S(1)}, s32[128]{0:T(128)}, u32[]{:S(2)}) copy-start(s32[128]{0:T(128)} %param.12) | copy-start | bytes 1540
  1.9 14.9 %collective-permute-start.2 = (bf16[20,128,128]{2,1,0:T(8,128)(2,1)S(1)}, bf16[20,128,128]{2,1,0:T(8,128)(2,1)S(1)}, u32[]{:S(2)}, u32[]{:S(2)}) collective-permute-start(bf16[20,128,128]{2,1,0:T(8,128)(2,1)S(1)} %picked_slot.1), channel_id=1, source_target_pairs={{0,2},{2,0},{8,10},{10,8},{16,18},{18,16},{24,26},{26,24}} | collective-permute-start | bytes 1966088 | tf_op jit(solution)/shard_map/ppermute | solution.py:256
  6.8 12.9 %collective-permute-start.3 = (bf16[512,256]{1,0:T(8,128)(2,1)S(1)}, bf16[512,256]{1,0:T(8,128)(2,1)S(1)}, u32[]{:S(2)}, u32[]{:S(2)}) collective-permute-start(bf16[512,256]{1,0:T(8,128)(2,1)S(1)} %copy-done.4), channel_id=1, source_target_pairs={{16,0},{25,1},{22,2},{15,3},{20,4},{29,5},{10,6},{19,7},{24,8},{1,... | collective-permute-start | bytes 786440 | tf_op jit(solution)/shard_map/ppermute | solution.py:236
  9.4 10.3 %collective-permute-start.4 = (bf16[512,256]{1,0:T(8,128)(2,1)S(1)}, bf16[512,256]{1,0:T(8,128)(2,1)S(1)}, u32[]{:S(2)}, u32[]{:S(2)}) collective-permute-start(bf16[512,256]{1,0:T(8,128)(2,1)S(1)} %copy-done.4), channel_id=1, source_target_pairs={{29,1},{6,2},{11,3},{24,4},{1,5},{15,7},{5,9},{14,10},{19,11},{0,1... | collective-permute-start | bytes 786440 | tf_op jit(solution)/shard_map/ppermute | solution.py:236
  10.7 6.1 %collective-permute-start.1 = (bf16[128,256]{1,0:T(8,128)(2,1)S(1)}, bf16[128,256]{1,0:T(8,128)(2,1)S(1)}, u32[]{:S(2)}, u32[]{:S(2)}) collective-permute-start(bf16[128,256]{1,0:T(8,128)(2,1)S(1)} %copy-done.5), channel_id=1, source_target_pairs={{0,2},{1,3},{2,0},{3,1},{4,6},{5,7},{6,4},{7,5},{8,10},{9,11},{10,... | collective-permute-start | bytes 196616 | tf_op jit(solution)/shard_map/ppermute | solution.py:25
  11.3 5.4 %collective-permute-start = (s32[256]{0:T(256)S(1)}, s32[256]{0:T(256)S(1)}, u32[]{:S(2)}, u32[]{:S(2)}) collective-permute-start(s32[256]{0:T(256)S(1)} %fusion.5), channel_id=1, source_target_pairs={{0,2},{1,3},{2,0},{3,1},{4,6},{5,7},{6,4},{7,5},{8,10},{9,11},{10,... | collective-permute-start | bytes 3080 | tf_op jit(solution)/shard_map/ppermute | solution.py:25
  19.7 8.8 %copy-start = (bf16[256,256]{1,0:T(8,128)(2,1)S(1)}, bf16[256,256]{1,0:T(8,128)(2,1)}, u32[]{:S(2)}) copy-start(bf16[256,256]{1,0:T(8,128)(2,1)} %w_self.3) | copy-start | bytes 393220
  19.7 8.8 %copy-start.1 = (bf16[256,256]{1,0:T(8,128)(2,1)S(1)}, bf16[256,256]{1,0:T(8,128)(2,1)}, u32[]{:S(2)}) copy-start(bf16[256,256]{1,0:T(8,128)(2,1)} %w_neigh.1) | copy-start | bytes 393220
  21.4 1.4 %collective-permute-start.5 = (bf16[256,256]{1,0:T(8,128)(2,1)S(1)}, bf16[256,256]{1,0:T(8,128)(2,1)S(1)}, u32[]{:S(2)}, u32[]{:S(2)}) collective-permute-start(bf16[256,256]{1,0:T(8,128)(2,1)S(1)} %get-tuple-element.25), channel_id=1, source_target_pairs={{0,1},{1,0},{2,3},{3,2},{4,5},{5,4},{6,7},{7,6},{8,9},{9,8},{10,11... | collective-permute-start | bytes 393224 | tf_op jit(solution)/shard_map/ppermute | solution.py:25
  22.9 5.6 %collective-permute-start.6 = (bf16[256,256]{1,0:T(8,128)(2,1)S(1)}, bf16[256,256]{1,0:T(8,128)(2,1)S(1)}, u32[]{:S(2)}, u32[]{:S(2)}) collective-permute-start(bf16[256,256]{1,0:T(8,128)(2,1)S(1)} %get-tuple-element.40), channel_id=1, source_target_pairs={{0,2},{1,3},{2,0},{3,1},{4,6},{5,7},{6,4},{7,5},{8,10},{9,11},{10,... | collective-permute-start | bytes 393224 | tf_op jit(solution)/shard_map/ppermute | solution.py:25
  29.6 1.4 %collective-permute-start.7 = (bf16[384,256]{1,0:T(8,128)(2,1)S(1)}, bf16[384,256]{1,0:T(8,128)(2,1)S(1)}, u32[]{:S(2)}, u32[]{:S(2)}) collective-permute-start(bf16[384,256]{1,0:T(8,128)(2,1)S(1)} %get-tuple-element.31.own), channel_id=1, source_target_pairs={{0,1},{1,0},{2,3},{3,2},{4,5},{5,4},{6,7},{7,6},{8,9},{9,8},{10,11... | collective-permute-start | bytes 589832 | tf_op jit(solution)/shard_map/ppermute | solution.py:25
  31.1 6.5 %collective-permute-start.13 = (bf16[128,256]{1,0:T(8,128)(2,1)S(1)}, bf16[128,256]{1,0:T(8,128)(2,1)S(1)}, u32[]{:S(2)}, u32[]{:S(2)}) collective-permute-start(bf16[128,256]{1,0:T(8,128)(2,1)S(1)} %add_convert_fusion.3), channel_id=1, source_target_pairs={{0,16},{1,17},{2,18},{3,19},{4,20},{5,21},{6,22},{7,23},{8,24},{9,... | collective-permute-start | bytes 196616 | tf_op jit(solution)/shard_map/ppermute | solution.py:25
  34.4 10.3 %collective-permute-start.8 = (bf16[256,256]{1,0:T(8,128)(2,1)S(1)}, bf16[256,256]{1,0:T(8,128)(2,1)S(1)}, u32[]{:S(2)}, u32[]{:S(2)}) collective-permute-start(bf16[256,256]{1,0:T(8,128)(2,1)S(1)} %get-tuple-element.32), channel_id=1, source_target_pairs={{0,18},{1,27},{2,20},{3,13},{4,22},{5,31},{6,8},{7,17},{8,26},{9,3... | collective-permute-start | bytes 393224 | tf_op jit(solution)/shard_map/ppermute | solution.py:25
  37.6 7.1 %collective-permute-start.14 = (bf16[128,256]{1,0:T(8,128)(2,1)S(1)}, bf16[128,256]{1,0:T(8,128)(2,1)S(1)}, u32[]{:S(2)}, u32[]{:S(2)}) collective-permute-start(bf16[128,256]{1,0:T(8,128)(2,1)S(1)} %add_convert_fusion.2), channel_id=1, source_target_pairs={{0,8},{1,9},{2,10},{3,11},{4,12},{5,13},{6,14},{7,15},{8,0},{9,1},... | collective-permute-start | bytes 196616 | tf_op jit(solution)/shard_map/ppermute | solution.py:25
  37.8 10.5 %collective-permute-start.9 = (bf16[256,256]{1,0:T(8,128)(2,1)S(1)}, bf16[256,256]{1,0:T(8,128)(2,1)S(1)}, u32[]{:S(2)}, u32[]{:S(2)}) collective-permute-start(bf16[256,256]{1,0:T(8,128)(2,1)S(1)} %get-tuple-element.33), channel_id=1, source_target_pairs={{0,16},{1,25},{2,22},{3,15},{4,20},{5,29},{6,10},{7,19},{8,24},{9,... | collective-permute-start | bytes 393224 | tf_op jit(solution)/shard_map/ppermute | solution.py:25
  40.7 7.6 %collective-permute-start.10 = (bf16[256,256]{1,0:T(8,128)(2,1)S(1)}, bf16[256,256]{1,0:T(8,128)(2,1)S(1)}, u32[]{:S(2)}, u32[]{:S(2)}) collective-permute-start(bf16[256,256]{1,0:T(8,128)(2,1)S(1)} %get-tuple-element.34), channel_id=1, source_target_pairs={{0,0},{1,31},{2,4},{3,9},{4,26},{5,3},{6,6},{7,13},{8,8},{9,7},{10... | collective-permute-start | bytes 393224 | tf_op jit(solution)/shard_map/ppermute | solution.py:25
  41.4 9.9 %collective-permute-start.11 = (bf16[256,256]{1,0:T(8,128)(2,1)S(1)}, bf16[256,256]{1,0:T(8,128)(2,1)S(1)}, u32[]{:S(2)}, u32[]{:S(2)}) collective-permute-start(bf16[256,256]{1,0:T(8,128)(2,1)S(1)} %get-tuple-element.35), channel_id=1, source_target_pairs={{0,2},{1,29},{2,6},{3,11},{4,24},{5,1},{6,4},{7,15},{8,10},{9,5},{... | collective-permute-start | bytes 393224 | tf_op jit(solution)/shard_map/ppermute | solution.py:25
  44.7 6.7 %collective-permute-start.15 = (bf16[128,256]{1,0:T(8,128)(2,1)S(1)}, bf16[128,256]{1,0:T(8,128)(2,1)S(1)}, u32[]{:S(2)}, u32[]{:S(2)}) collective-permute-start(bf16[128,256]{1,0:T(8,128)(2,1)S(1)} %add_convert_fusion.1), channel_id=1, source_target_pairs={{0,4},{1,5},{2,6},{3,7},{4,0},{5,1},{6,2},{7,3},{8,12},{9,13},{10,... | collective-permute-start | bytes 196616 | tf_op jit(solution)/shard_map/ppermute | solution.py:25
  51.4 4.3 %collective-permute-start.16 = (bf16[128,256]{1,0:T(8,128)(2,1)S(1)}, bf16[128,256]{1,0:T(8,128)(2,1)S(1)}, u32[]{:S(2)}, u32[]{:S(2)}) collective-permute-start(bf16[128,256]{1,0:T(8,128)(2,1)S(1)} %add_convert_fusion), channel_id=1, source_target_pairs={{0,2},{1,3},{2,0},{3,1},{4,6},{5,7},{6,4},{7,5},{8,10},{9,11},{10,... | collective-permute-start | bytes 196616 | tf_op jit(solution)/shard_map/ppermute | solution.py:25
  52.4 3.4 %collective-permute-start.12 = (bf16[128,256]{1,0:T(8,128)(2,1)S(1)}, bf16[128,256]{1,0:T(8,128)(2,1)S(1)}, u32[]{:S(2)}, u32[]{:S(2)}) collective-permute-start(bf16[128,256]{1,0:T(8,128)(2,1)S(1)} %fusion.2), channel_id=1, source_target_pairs={{0,1},{1,0},{2,3},{3,2},{4,5},{5,4},{6,7},{7,6},{8,9},{9,8},{10,11... | collective-permute-start | bytes 196616 | tf_op jit(solution)/shard_map/ppermute | solution.py:25
  55.8 1.4 %collective-permute-start.17 = (bf16[2,128,256]{2,1,0:T(8,128)(2,1)S(1)}, bf16[2,128,256]{2,1,0:T(8,128)(2,1)S(1)}, u32[]{:S(2)}, u32[]{:S(2)}) collective-permute-start(bf16[2,128,256]{2,1,0:T(8,128)(2,1)S(1)} %maximum_select_fusion.2), channel_id=1, source_target_pairs={{0,1},{1,0},{2,3},{3,2},{4,5},{5,4},{6,7},{7,6},{8,9},{9,8},{10,11... | collective-permute-start | bytes 393224 | tf_op jit(solution)/shard_map/ppermute | solution.py:25

commit v7 on v6

--- a/solution.py
+++ b/solution.py
@@ -87,17 +87,12 @@
 
 
 def prepare(
-    swap, tiles, features, cot_own, deg_own, w_self, cot_far, deg_far, *rest,
+    swap, tiles, features, *rest,
 ):
-    moved = rest[:-8]
-    kept_tiles, panel, self_term, cot, inv_root, deg_near, weights, sems = rest[-8:]
-    rep = lax.axis_index("rep")
-    core, plane = lax.rem(rep, 2), lax.div(rep, 2)
-    share = cot_own.shape[0]
-    near = pl.ds(pl.multiple_of(plane * share, share), share)
-    away = pl.ds(pl.multiple_of((1 - plane) * share, share), share)
-    pairs = [(cot_own, cot.at[near]), (deg_own, deg_near), (w_self, weights), (features, panel)]
-    copies = [pltpu.make_async_copy(*pair, sems.at[i]) for i, pair in enumerate(pairs)]
+    moved = rest[:-3]
+    kept_tiles, panel, sems = rest[-3:]
+    rep = lax.axis_index("rep")
+    copies = [pltpu.make_async_copy(features, panel, sems.at[4])]
     for copy in copies:
         copy.start()
 
@@ -105,24 +100,33 @@
     for order in range(2):
         is_moved, slot = slot_of(swap, order, rep, lax.axis_index("blk"))
         place = kept_tiles.at[order]
-        here = pltpu.make_async_copy(tiles.at[0, slot], place, sems.at[len(tile_copies) + 5])
+        here = pltpu.make_async_copy(tiles.at[0, slot], place, sems.at[len(tile_copies)])
         tile_copies.append((jnp.logical_not(is_moved), here))
         if moved:
-            come = pltpu.make_async_copy(moved[0], place, sems.at[len(tile_copies) + 5])
+            come = pltpu.make_async_copy(moved[0], place, sems.at[len(tile_copies)])
             tile_copies.append((is_moved, come))
     for is_needed, copy in tile_copies:
         pl.when(is_needed)(copy.start)
     for copy in copies:
         copy.wait()
+    for is_needed, copy in tile_copies:
+        pl.when(is_needed)(copy.wait)
+
+
+def row_terms(panel, cot_own, deg_own, w_self, cot_far, deg_far, self_term, cot, inv_root):
+    rep = lax.axis_index("rep")
+    core, plane = lax.rem(rep, 2), lax.div(rep, 2)
+    share = cot_own.shape[0]
+    near = pl.ds(pl.multiple_of(plane * share, share), share)
+    away = pl.ds(pl.multiple_of((1 - plane) * share, share), share)
+    cot[near, :] = cot_own[...]
     cot[away, :] = cot_far[...]
     width = inv_root.shape[1]
-    for where, deg in ((near, deg_near[...]), (away, deg_far[:1, :])):
+    for where, deg in ((near, deg_own[...]), (away, deg_far[:1, :])):
         inv_root[where, :] = jnp.transpose(jnp.broadcast_to(1.0 / jnp.sqrt(deg.astype(F32)), (width, share)))
     for h in range(2):
         rows = panel[pl.ds(pl.multiple_of((2 * h + core) * share, share), share), :]
-        self_term[h * share : (h + 1) * share, :] = dot(rows, weights[...], ((1,), (0,)))
-    for is_needed, copy in tile_copies:
-        pl.when(is_needed)(copy.wait)
+        self_term[h * share : (h + 1) * share, :] = dot(rows, w_self[...], ((1,), (0,)))
 
 
 def middle(chip_sum, far_sum, inv_root, self_term, cot, panel, w_self, w_neigh, hidden, own_term, message, kept_grad, grads):
@@ -255,15 +259,16 @@
         )[0]
         moved.append(lax.ppermute(picked, BOTH, pairs))
     wide = (half, dim)
-    raw = [tile_vals, features, cotangent, degree.reshape(1, share), w_self]
-    raw = [pltpu.with_memory_space_constraint(a, pltpu.HBM) for a in raw]
-    tiles, panel, self_term, cot, inv_root = kernel_call(
-        functools.partial(prepare, swap),
-        "prepare",
-        [(tile_vals.shape[1:], BF16), ((rows, dim), BF16), (wide, F32), (wide, BF16), (wide, F32)],
-        raw + [cot_far, far_note.reshape(2, share)] + moved,
-        [pltpu.VMEM((1, share), jnp.int32), pltpu.VMEM(w_self.shape, BF16), pltpu.SemaphoreType.DMA((7 + 2 * len(moved),))],
-        [pl.BlockSpec(memory_space=pltpu.HBM)] * 5 + [VMEM] * 2 + [pl.BlockSpec(memory_space=pl.ANY)] * len(moved),
+    raw = [pltpu.with_memory_space_constraint(a, pltpu.HBM) for a in (tile_vals, features)]
+    tiles, panel = kernel_call(
+        functools.partial(prepare, swap), "prepare", [(tile_vals.shape[1:], BF16), ((rows, dim), BF16)], raw + moved,
+        [pltpu.SemaphoreType.DMA((5,))],
+        [pl.BlockSpec(memory_space=pltpu.HBM)] * 2 + [pl.BlockSpec(memory_space=pl.ANY)] * len(moved),
+    )
+    far_note, cot_far, panel = lax.optimization_barrier((far_note, cot_far, panel))
+    self_term, cot, inv_root = kernel_call(
+        row_terms, "row_terms", [(wide, F32), (wide, BF16), (wide, F32)],
+        [panel, cotangent, degree.reshape(1, share), w_self, cot_far, far_note.reshape(2, share)],
     )
 
     source, total = pltpu.VMEM((rows, dim), BF16), pltpu.VMEM((rows + tile_size, dim), F32)
@@ -315,7 +320,7 @@
     for i in range(top - 1, 1, -1):
         rounded = added(rounded, others(rounded, 1 << i))
     rounded = added(rounded, tied(others(rounded, 2), arrived[0]))
-    rounded = added(rounded, tied(others(rounded, 1), arrived[1]))
+    rounded = added(rounded, tied(others(rounded, 1), arrived[1], arrived[2]))
     twin = flip_plane(rounded)
     by_plane = jnp.where(plane == 0, jnp.stack([rounded, twin]), jnp.stack([twin, rounded]))
     twin = flip_core(by_plane)

time: 58.3 us -> 58 us (level)
  waiting for transfers between devices: 22.7 us -> 21.9 us
    ppermute x15, waiting for transfers between devices: 21.1 us -> 16.8 us  [exchange(): return lax.ppermute(value, BOTH, pairs)]
    ppermute x1, waiting for transfers between devices: 0.01 us -> 2.68 us  [on_device(): moved.append(lax.ppermute(picked, BOTH, pairs))]
    ppermute x2, waiting for transfers between devices: 1.56 us -> 2.45 us  [fetch(): return lax.ppermute(features, BOTH, pairs)]
    pallas_call x5 -> x6, Pallas kernels: 7.05 us -> 7.04 us  [kernel_call(): pl.pallas_call(kernel, out_shape=[jax.ShapeDtypeStruct(*out) for out in o...]
  transfers between devices with their start and end apart: 18 -> 18, of which waited for: 10 -> 11; matrix products, arithmetic and copies ran while one was open for 2% -> 2% of each run, Pallas kernels for 5% -> 5%
where the time goes in v7:
time: 58 us; the launch traced here: 57.6 us
  starting transfers between devices  25.4 us (44%)
  waiting for transfers between devices  21.9 us (38%)
  Pallas kernels  7.04 us (12%)
  local copies, waits for them, and re-layouts  1.26 us (2%)
  other arithmetic  1.01 us (2%)
  between operations  0.91 us (2%)
    ppermute x15, waiting for transfers between devices, exchange(): return lax.ppermute(value, BOTH, pairs)  16.8 us
    ppermute x15, starting transfers between devices, exchange(): return lax.ppermute(value, BOTH, pairs)  16.6 us
    pallas_call x6, Pallas kernels, kernel_call(): pl.pallas_call(kernel, out_shape=[jax.ShapeDtypeStruct(*out) for out in o...  7.04 us
    ppermute x1, starting transfers between devices, on_device(): moved.append(lax.ppermute(picked, BOTH, pairs))  4.85 us
    ppermute x2, starting transfers between devices, fetch(): return lax.ppermute(features, BOTH, pairs)  3.93 us
    ppermute x1, waiting for transfers between devices, on_device(): moved.append(lax.ppermute(picked, BOTH, pairs))  2.68 us
    ppermute x2, waiting for transfers between devices, fetch(): return lax.ppermute(features, BOTH, pairs)  2.45 us
  transfers between devices with their start and end apart: 18, of which 11 were waited for; matrix products, arithmetic and copies ran while one was open for 2% of the time, Pallas kernels for 5%

profile of v7, /device:TPU:0, one launch (start us, length us, event | category | flops | bytes accessed | tf_op | source)
XLA Modules:
  0.0 57.6 jit_solution(11021796550958225490)
XLA Ops:
  0.6 0.0 copy-start.6
  0.6 0.0 copy-start.2
  0.7 0.0 copy-start.3
  0.7 0.0 copy-start.4
  0.7 0.0 copy-start.5
  0.7 1.2 %picked_slot.1 = bf16[20,128,128]{2,1,0:T(8,128)(2,1)S(1)} custom-call(bf16[1,2,20,128,128]{4,3,2,1,0:T(8,128)(2,1)} %tiles.3), custom_call_target="tpu_custom_call" | custom-call | tf_op jit(solution)/shard_map/picked_slot/pallas_call | solution.py:195
  1.8 4.8 %collective-permute-start.2 = (bf16[20,128,128]{2,1,0:T(8,128)(2,1)S(1)}, bf16[20,128,128]{2,1,0:T(8,128)(2,1)S(1)}, u32[]{:S(2)}, u32[]{:S(2)}) collective-permute-start(bf16[20,128,128]{2,1,0:T(8,128)(2,1)S(1)} %picked_slot.1), channel_id=1, source_target_pairs={{0,2},{2,0},{8,10},{10,8},{16,18},{18,16},{24,26},{26,24}} | collective-permute-start | bytes 1966088 | tf_op jit(solution)/shard_map/ppermute | solution.py:260
  6.7 0.0 copy-done.6
  6.7 2.6 %collective-permute-start.3 = (bf16[512,256]{1,0:T(8,128)(2,1)S(1)}, bf16[512,256]{1,0:T(8,128)(2,1)S(1)}, u32[]{:S(2)}, u32[]{:S(2)}) collective-permute-start(bf16[512,256]{1,0:T(8,128)(2,1)S(1)} %copy-done.6), channel_id=1, source_target_pairs={{16,0},{25,1},{22,2},{15,3},{20,4},{29,5},{10,6},{19,7},{24,8},{1,... | collective-permute-start | bytes 786440 | tf_op jit(solution)/shard_map/ppermute | solution.py:240
  9.4 1.3 %collective-permute-start.4 = (bf16[512,256]{1,0:T(8,128)(2,1)S(1)}, bf16[512,256]{1,0:T(8,128)(2,1)S(1)}, u32[]{:S(2)}, u32[]{:S(2)}) collective-permute-start(bf16[512,256]{1,0:T(8,128)(2,1)S(1)} %copy-done.6), channel_id=1, source_target_pairs={{29,1},{6,2},{11,3},{24,4},{1,5},{15,7},{5,9},{14,10},{19,11},{0,1... | collective-permute-start | bytes 786440 | tf_op jit(solution)/shard_map/ppermute | solution.py:240
  10.7 0.0 copy-done.2
  10.7 0.1 collective-permute-start.1
  10.8 0.0 copy-done.3
  10.8 0.1 copy.14
  10.9 0.1 reshape_squeeze.6
  11.0 0.1 copy.15
  11.1 0.1 reshape_squeeze.7
  11.2 0.0 copy-done.4
  11.2 0.0 copy-done.5
  11.2 0.1 fusion.5
  11.3 2.0 %collective-permute-start = (s32[256]{0:T(256)S(1)}, s32[256]{0:T(256)S(1)}, u32[]{:S(2)}, u32[]{:S(2)}) collective-permute-start(s32[256]{0:T(256)S(1)} %fusion.5), channel_id=1, source_target_pairs={{0,2},{1,3},{2,0},{3,1},{4,6},{5,7},{6,4},{7,5},{8,10},{9,11},{10,... | collective-permute-start | bytes 3080 | tf_op jit(solution)/shard_map/ppermute | solution.py:25
  13.3 2.7 %collective-permute-done.2.rest_0_ = bf16[20,128,128]{2,1,0:T(8,128)(2,1)S(1)} collective-permute-done((bf16[20,128,128]{2,1,0:T(8,128)(2,1)S(1)}, bf16[20,128,128]{2,1,0:T(8,128)(2,1)S(1)}, u32[]{:S(2)}, u32[]{:S(2)}) %collective-permute-start.2) | collective-permute-done | bytes 655392 | tf_op jit(solution)/shard_map/ppermute | solution.py:260
  16.0 1.2 %prepare.1 = (bf16[2,20,128,128]{3,2,1,0:T(8,128)(2,1)S(1)}, bf16[512,256]{1,0:T(8,128)(2,1)S(1)}) custom-call(bf16[1,2,20,128,128]{4,3,2,1,0:T(8,128)(2,1)} %tiles.3, bf16[512,256]{1,0:T(8,128)(2,1)} %features.1, bf16[20,128,128]{2,1,0:T(8,128)(2,1)S(1)} %collective-permute-done.2.rest_0_), custom_call_target="tpu_custom_call" | custom-call | tf_op jit(solution)/shard_map/prepare/pallas_call | solution.py:195
  17.2 0.0 collective-permute-done.note
  17.2 0.0 collective-permute-done.1.cot_far
  17.2 2.4 %collective-permute-done.3.far = bf16[512,256]{1,0:T(8,128)(2,1)S(1)} collective-permute-done((bf16[512,256]{1,0:T(8,128)(2,1)S(1)}, bf16[512,256]{1,0:T(8,128)(2,1)S(1)}, u32[]{:S(2)}, u32[]{:S(2)}) %collective-permute-start.3) | collective-permute-done | bytes 262176 | tf_op jit(solution)/shard_map/ppermute | solution.py:240
  19.7 0.0 collective-permute-done.4.near
  19.7 0.0 copy-start
  19.7 1.7 %forward.1 = (f32[256,256]{1,0:T(8,128)S(1)}, bf16[256,256]{1,0:T(8,128)(2,1)S(1)}) custom-call(s32[1,2,2,20]{3,2,1,0:T(2,128)S(1)} %bitcast.23, s32[1,2,20]{2,1,0:T(2,128)S(1)} %copy-done.4, s32[256]{0:T(256)S(1)} %collective-permute-done.note, bf16[2,20,128,128]{3,2,1,0:T(8,128)(2,1)S(1)} %get-tuple-element.27.tiles, ...), custom_call_target="tpu_custom_call" | custom-call | tf_op jit(solution)/shard_map/forward/pallas_call | solution.py:195
  21.4 0.1 collective-permute-start.5
  21.5 1.3 %collective-permute-done.5 = bf16[256,256]{1,0:T(8,128)(2,1)S(1)} collective-permute-done((bf16[256,256]{1,0:T(8,128)(2,1)S(1)}, bf16[256,256]{1,0:T(8,128)(2,1)S(1)}, u32[]{:S(2)}, u32[]{:S(2)}) %collective-permute-start.5) | collective-permute-done | bytes 131104 | tf_op jit(solution)/shard_map/ppermute | solution.py:25
  22.8 0.5 collective-permute-start.6
  23.4 0.0 copy-done
  23.4 0.2 row_terms.1
  23.6 4.9 %collective-permute-done.6.far_sum = bf16[256,256]{1,0:T(8,128)(2,1)S(1)} collective-permute-done((bf16[256,256]{1,0:T(8,128)(2,1)S(1)}, bf16[256,256]{1,0:T(8,128)(2,1)S(1)}, u32[]{:S(2)}, u32[]{:S(2)}) %collective-permute-start.6) | collective-permute-done | bytes 131104 | tf_op jit(solution)/shard_map/ppermute | solution.py:25
  28.4 0.0 copy-done.1
  28.4 1.1 %middle.1 = (bf16[128,256]{1,0:T(8,128)(2,1)}, f32[128,256]{1,0:T(8,128)S(1)}, bf16[384,256]{1,0:T(8,128)(2,1)S(1)}, f32[128,256]{1,0:T(8,128)S(1)}) custom-call(f32[256,256]{1,0:T(8,128)S(1)} %get-tuple-element.47.chip_sum, bf16[256,256]{1,0:T(8,128)(2,1)S(1)} %collective-permute-done.6.far_sum, f32[256,256]{1,0:T(8,128)S(1)} %get-tuple-element.32.inv_root, ...), custom_call_target="tpu_custom_call" | custom-call | tf_op jit(solution)/shard_map/middle/pallas_call | solution.py:195
  29.6 0.0 collective-permute-start.7
  29.6 1.4 %collective-permute-done.7.other = bf16[384,256]{1,0:T(8,128)(2,1)S(1)} collective-permute-done((bf16[384,256]{1,0:T(8,128)(2,1)S(1)}, bf16[384,256]{1,0:T(8,128)(2,1)S(1)}, u32[]{:S(2)}, u32[]{:S(2)}) %collective-permute-start.7) | collective-permute-done | bytes 196640 | tf_op jit(solution)/shard_map/ppermute | solution.py:25
  31.0 0.8 %collective-permute-start.13 = (bf16[128,256]{1,0:T(8,128)(2,1)S(1)}, bf16[128,256]{1,0:T(8,128)(2,1)S(1)}, u32[]{:S(2)}, u32[]{:S(2)}) collective-permute-start(bf16[128,256]{1,0:T(8,128)(2,1)S(1)} %add_convert_fusion.3), channel_id=1, source_target_pairs={{0,16},{1,17},{2,18},{3,19},{4,20},{5,21},{6,22},{7,23},{8,24},{9,... | collective-permute-start | bytes 196616 | tf_op jit(solution)/shard_map/ppermute | solution.py:25
  31.8 1.6 %backward.1 = (bf16[256,256]{1,0:T(8,128)(2,1)S(1)}, bf16[256,256]{1,0:T(8,128)(2,1)S(1)}, bf16[256,256]{1,0:T(8,128)(2,1)S(1)}, bf16[256,256]{1,0:T(8,128)(2,1)S(1)}) custom-call(s32[1,2,2,20]{3,2,1,0:T(2,128)S(1)} %bitcast.24, s32[1,2,20]{2,1,0:T(2,128)S(1)} %copy-done.4, s32[256]{0:T(256)S(1)} %collective-permute-done.note, ...), custom_call_target="tpu_custom_call" | custom-call | tf_op jit(solution)/shard_map/backward/pallas_call | solution.py:195
  33.5 2.2 %collective-permute-start.8 = (bf16[256,256]{1,0:T(8,128)(2,1)S(1)}, bf16[256,256]{1,0:T(8,128)(2,1)S(1)}, u32[]{:S(2)}, u32[]{:S(2)}) collective-permute-start(bf16[256,256]{1,0:T(8,128)(2,1)S(1)} %get-tuple-element.38), channel_id=1, source_target_pairs={{0,18},{1,27},{2,20},{3,13},{4,22},{5,31},{6,8},{7,17},{8,26},{9,3... | collective-permute-start | bytes 393224 | tf_op jit(solution)/shard_map/ppermute | solution.py:25
  35.7 1.9 %collective-permute-done.13 = bf16[128,256]{1,0:T(8,128)(2,1)S(1)} collective-permute-done((bf16[128,256]{1,0:T(8,128)(2,1)S(1)}, bf16[128,256]{1,0:T(8,128)(2,1)S(1)}, u32[]{:S(2)}, u32[]{:S(2)}) %collective-permute-start.13) | collective-permute-done | bytes 65568 | tf_op jit(solution)/shard_map/ppermute | solution.py:25
  37.6 0.2 collective-permute-start.14
  37.8 0.7 %collective-permute-start.10 = (bf16[256,256]{1,0:T(8,128)(2,1)S(1)}, bf16[256,256]{1,0:T(8,128)(2,1)S(1)}, u32[]{:S(2)}, u32[]{:S(2)}) collective-permute-start(bf16[256,256]{1,0:T(8,128)(2,1)S(1)} %get-tuple-element.40), channel_id=1, source_target_pairs={{0,0},{1,31},{2,4},{3,9},{4,26},{5,3},{6,6},{7,13},{8,8},{9,7},{10... | collective-permute-start | bytes 393224 | tf_op jit(solution)/shard_map/ppermute | solution.py:25
  38.5 2.9 %collective-permute-start.9 = (bf16[256,256]{1,0:T(8,128)(2,1)S(1)}, bf16[256,256]{1,0:T(8,128)(2,1)S(1)}, u32[]{:S(2)}, u32[]{:S(2)}) collective-permute-start(bf16[256,256]{1,0:T(8,128)(2,1)S(1)} %get-tuple-element.39), channel_id=1, source_target_pairs={{0,16},{1,25},{2,22},{3,15},{4,20},{5,29},{6,10},{7,19},{8,24},{9,... | collective-permute-start | bytes 393224 | tf_op jit(solution)/shard_map/ppermute | solution.py:25
  41.4 2.0 %collective-permute-start.11 = (bf16[256,256]{1,0:T(8,128)(2,1)S(1)}, bf16[256,256]{1,0:T(8,128)(2,1)S(1)}, u32[]{:S(2)}, u32[]{:S(2)}) collective-permute-start(bf16[256,256]{1,0:T(8,128)(2,1)S(1)} %get-tuple-element.41), channel_id=1, source_target_pairs={{0,2},{1,29},{2,6},{3,11},{4,24},{5,1},{6,4},{7,15},{8,10},{9,5},{... | collective-permute-start | bytes 393224 | tf_op jit(solution)/shard_map/ppermute | solution.py:25
  43.4 0.0 collective-permute-done.8
  43.4 0.0 collective-permute-done.14
  43.5 3.3 %collective-permute-start.15 = (bf16[128,256]{1,0:T(8,128)(2,1)S(1)}, bf16[128,256]{1,0:T(8,128)(2,1)S(1)}, u32[]{:S(2)}, u32[]{:S(2)}) collective-permute-start(bf16[128,256]{1,0:T(8,128)(2,1)S(1)} %add_convert_fusion.1), channel_id=1, source_target_pairs={{0,4},{1,5},{2,6},{3,7},{4,0},{5,1},{6,2},{7,3},{8,12},{9,13},{10,... | collective-permute-start | bytes 196616 | tf_op jit(solution)/shard_map/ppermute | solution.py:25
  46.8 0.0 collective-permute-done.10
  46.8 0.5 collective-permute-done.9
  47.3 1.9 %collective-permute-done.11 = bf16[256,256]{1,0:T(8,128)(2,1)S(1)} collective-permute-done((bf16[256,256]{1,0:T(8,128)(2,1)S(1)}, bf16[256,256]{1,0:T(8,128)(2,1)S(1)}, u32[]{:S(2)}, u32[]{:S(2)}) %collective-permute-start.11) | collective-permute-done | bytes 131104 | tf_op jit(solution)/shard_map/ppermute | solution.py:25
  49.2 0.1 convert_add_fusion
  49.2 1.3 %collective-permute-done.15 = bf16[128,256]{1,0:T(8,128)(2,1)S(1)} collective-permute-done((bf16[128,256]{1,0:T(8,128)(2,1)S(1)}, bf16[128,256]{1,0:T(8,128)(2,1)S(1)}, u32[]{:S(2)}, u32[]{:S(2)}) %collective-permute-start.15) | collective-permute-done | bytes 65568 | tf_op jit(solution)/shard_map/ppermute | solution.py:25
  50.6 0.6 collective-permute-start.16
  51.2 1.2 %collective-permute-start.12 = (bf16[128,256]{1,0:T(8,128)(2,1)S(1)}, bf16[128,256]{1,0:T(8,128)(2,1)S(1)}, u32[]{:S(2)}, u32[]{:S(2)}) collective-permute-start(bf16[128,256]{1,0:T(8,128)(2,1)S(1)} %fusion.2), channel_id=1, source_target_pairs={{0,1},{1,0},{2,3},{3,2},{4,5},{5,4},{6,7},{7,6},{8,9},{9,8},{10,11... | collective-permute-start | bytes 196616 | tf_op jit(solution)/shard_map/ppermute | solution.py:25
  52.4 2.9 %collective-permute-done.16 = bf16[128,256]{1,0:T(8,128)(2,1)S(1)} collective-permute-done((bf16[128,256]{1,0:T(8,128)(2,1)S(1)}, bf16[128,256]{1,0:T(8,128)(2,1)S(1)}, u32[]{:S(2)}, u32[]{:S(2)}) %collective-permute-start.16) | collective-permute-done | bytes 65568 | tf_op jit(solution)/shard_map/ppermute | solution.py:25
  55.3 0.1 collective-permute-start.17
  55.3 0.0 collective-permute-done.12
  55.4 0.7 %fusion.1 = bf16[128,256]{1,0:T(8,128)(2,1)} fusion(f32[128,256]{1,0:T(8,128)S(1)} %get-tuple-element.36, bf16[128,256]{1,0:T(8,128)(2,1)S(1)} %collective-permute-done.12, f32[2,128,256]{2,1,0:T(8,128)S(1)} %bitcast.28, s32[]{:T(128)S(6)} %select_n.59), kind=kLoop, calls=%fused_computation.8 | loop fusion | flops 131072 | bytes 393220 | tf_op jit(solution)/shard_map/convert_element_type | solution.py:334
  56.0 0.6 %collective-permute-done.17 = bf16[2,128,256]{2,1,0:T(8,128)(2,1)S(1)} collective-permute-done((bf16[2,128,256]{2,1,0:T(8,128)(2,1)S(1)}, bf16[2,128,256]{2,1,0:T(8,128)(2,1)S(1)}, u32[]{:S(2)}, u32[]{:S(2)}) %collective-permute-start.17) | collective-permute-done | bytes 131104 | tf_op jit(solution)/shard_map/ppermute | solution.py:25
  56.7 0.1 convert_multiply_fusion
  56.7 0.8 %fusion.7 = (f32[1,2,128,256]{3,2,0,1:T(8,128)}, f32[1,2,128,256]{3,2,0,1:T(8,128)}) fusion(f32[2,2,128,256]{3,2,0,1:T(8,128)S(1)} %convert_multiply_fusion), kind=kLoop, calls=%fused_computation.25 | loop fusion | bytes 1048576 | tf_op jit(solution)/shard_map/slice | solution.py:335
  (12 shorter events, 0.2 us)
Async XLA Ops:
  0.6 6.1 %copy-start.6 = (bf16[512,256]{1,0:T(8,128)(2,1)S(1)}, bf16[512,256]{1,0:T(8,128)(2,1)}, u32[]{:S(2)}) copy-start(bf16[512,256]{1,0:T(8,128)(2,1)} %features.1) | copy-start | bytes 786436
  0.6 10.0 %copy-start.2 = (bf16[128,256]{1,0:T(8,128)(2,1)S(1)}, bf16[128,256]{1,0:T(8,128)(2,1)}, u32[]{:S(2)}) copy-start(bf16[128,256]{1,0:T(8,128)(2,1)} %cot_own.1) | copy-start | bytes 196612
  0.7 10.1 %copy-start.3 = (s32[1,2,20,2]{2,3,1,0:T(2,128)S(1)}, s32[1,2,20,2]{2,3,1,0:T(2,128)}, u32[]{:S(2)}) copy-start(s32[1,2,20,2]{2,3,1,0:T(2,128)} %param.9) | copy-start | bytes 964
  0.7 10.5 %copy-start.4 = (s32[1,2,20]{2,1,0:T(2,128)S(1)}, s32[1,2,20]{2,1,0:T(2,128)}, u32[]{:S(2)}) copy-start(s32[1,2,20]{2,1,0:T(2,128)} %live.3) | copy-start | bytes 484
  0.7 10.5 %copy-start.5 = (s32[128]{0:T(128)S(1)}, s32[128]{0:T(128)}, u32[]{:S(2)}) copy-start(s32[128]{0:T(128)} %param.12) | copy-start | bytes 1540
  1.8 14.1 %collective-permute-start.2 = (bf16[20,128,128]{2,1,0:T(8,128)(2,1)S(1)}, bf16[20,128,128]{2,1,0:T(8,128)(2,1)S(1)}, u32[]{:S(2)}, u32[]{:S(2)}) collective-permute-start(bf16[20,128,128]{2,1,0:T(8,128)(2,1)S(1)} %picked_slot.1), channel_id=1, source_target_pairs={{0,2},{2,0},{8,10},{10,8},{16,18},{18,16},{24,26},{26,24}} | collective-permute-start | bytes 1966088 | tf_op jit(solution)/shard_map/ppermute | solution.py:260
  6.7 12.9 %collective-permute-start.3 = (bf16[512,256]{1,0:T(8,128)(2,1)S(1)}, bf16[512,256]{1,0:T(8,128)(2,1)S(1)}, u32[]{:S(2)}, u32[]{:S(2)}) collective-permute-start(bf16[512,256]{1,0:T(8,128)(2,1)S(1)} %copy-done.6), channel_id=1, source_target_pairs={{16,0},{25,1},{22,2},{15,3},{20,4},{29,5},{10,6},{19,7},{24,8},{1,... | collective-permute-start | bytes 786440 | tf_op jit(solution)/shard_map/ppermute | solution.py:240
  9.4 10.3 %collective-permute-start.4 = (bf16[512,256]{1,0:T(8,128)(2,1)S(1)}, bf16[512,256]{1,0:T(8,128)(2,1)S(1)}, u32[]{:S(2)}, u32[]{:S(2)}) collective-permute-start(bf16[512,256]{1,0:T(8,128)(2,1)S(1)} %copy-done.6), channel_id=1, source_target_pairs={{29,1},{6,2},{11,3},{24,4},{1,5},{15,7},{5,9},{14,10},{19,11},{0,1... | collective-permute-start | bytes 786440 | tf_op jit(solution)/shard_map/ppermute | solution.py:240
  10.7 6.5 %collective-permute-start.1 = (bf16[128,256]{1,0:T(8,128)(2,1)S(1)}, bf16[128,256]{1,0:T(8,128)(2,1)S(1)}, u32[]{:S(2)}, u32[]{:S(2)}) collective-permute-start(bf16[128,256]{1,0:T(8,128)(2,1)S(1)} %copy-done.2), channel_id=1, source_target_pairs={{0,2},{1,3},{2,0},{3,1},{4,6},{5,7},{6,4},{7,5},{8,10},{9,11},{10,... | collective-permute-start | bytes 196616 | tf_op jit(solution)/shard_map/ppermute | solution.py:25
  11.3 5.9 %collective-permute-start = (s32[256]{0:T(256)S(1)}, s32[256]{0:T(256)S(1)}, u32[]{:S(2)}, u32[]{:S(2)}) collective-permute-start(s32[256]{0:T(256)S(1)} %fusion.5), channel_id=1, source_target_pairs={{0,2},{1,3},{2,0},{3,1},{4,6},{5,7},{6,4},{7,5},{8,10},{9,11},{10,... | collective-permute-start | bytes 3080 | tf_op jit(solution)/shard_map/ppermute | solution.py:25
  19.7 3.7 %copy-start = (bf16[256,256]{1,0:T(8,128)(2,1)S(1)}, bf16[256,256]{1,0:T(8,128)(2,1)}, u32[]{:S(2)}) copy-start(bf16[256,256]{1,0:T(8,128)(2,1)} %w_self.3) | copy-start | bytes 393220
  19.7 8.8 %copy-start.1 = (bf16[256,256]{1,0:T(8,128)(2,1)S(1)}, bf16[256,256]{1,0:T(8,128)(2,1)}, u32[]{:S(2)}) copy-start(bf16[256,256]{1,0:T(8,128)(2,1)} %w_neigh.1) | copy-start | bytes 393220
  21.4 1.4 %collective-permute-start.5 = (bf16[256,256]{1,0:T(8,128)(2,1)S(1)}, bf16[256,256]{1,0:T(8,128)(2,1)S(1)}, u32[]{:S(2)}, u32[]{:S(2)}) collective-permute-start(bf16[256,256]{1,0:T(8,128)(2,1)S(1)} %get-tuple-element.30), channel_id=1, source_target_pairs={{0,1},{1,0},{2,3},{3,2},{4,5},{5,4},{6,7},{7,6},{8,9},{9,8},{10,11... | collective-permute-start | bytes 393224 | tf_op jit(solution)/shard_map/ppermute | solution.py:25
  22.8 5.6 %collective-permute-start.6 = (bf16[256,256]{1,0:T(8,128)(2,1)S(1)}, bf16[256,256]{1,0:T(8,128)(2,1)S(1)}, u32[]{:S(2)}, u32[]{:S(2)}) collective-permute-start(bf16[256,256]{1,0:T(8,128)(2,1)S(1)} %get-tuple-element.46), channel_id=1, source_target_pairs={{0,2},{1,3},{2,0},{3,1},{4,6},{5,7},{6,4},{7,5},{8,10},{9,11},{10,... | collective-permute-start | bytes 393224 | tf_op jit(solution)/shard_map/ppermute | solution.py:25
  29.6 1.4 %collective-permute-start.7 = (bf16[384,256]{1,0:T(8,128)(2,1)S(1)}, bf16[384,256]{1,0:T(8,128)(2,1)S(1)}, u32[]{:S(2)}, u32[]{:S(2)}) collective-permute-start(bf16[384,256]{1,0:T(8,128)(2,1)S(1)} %get-tuple-element.37.own), channel_id=1, source_target_pairs={{0,1},{1,0},{2,3},{3,2},{4,5},{5,4},{6,7},{7,6},{8,9},{9,8},{10,11... | collective-permute-start | bytes 589832 | tf_op jit(solution)/shard_map/ppermute | solution.py:25
  31.0 6.5 %collective-permute-start.13 = (bf16[128,256]{1,0:T(8,128)(2,1)S(1)}, bf16[128,256]{1,0:T(8,128)(2,1)S(1)}, u32[]{:S(2)}, u32[]{:S(2)}) collective-permute-start(bf16[128,256]{1,0:T(8,128)(2,1)S(1)} %add_convert_fusion.3), channel_id=1, source_target_pairs={{0,16},{1,17},{2,18},{3,19},{4,20},{5,21},{6,22},{7,23},{8,24},{9,... | collective-permute-start | bytes 196616 | tf_op jit(solution)/shard_map/ppermute | solution.py:25
  33.5 10.0 %collective-permute-start.8 = (bf16[256,256]{1,0:T(8,128)(2,1)S(1)}, bf16[256,256]{1,0:T(8,128)(2,1)S(1)}, u32[]{:S(2)}, u32[]{:S(2)}) collective-permute-start(bf16[256,256]{1,0:T(8,128)(2,1)S(1)} %get-tuple-element.38), channel_id=1, source_target_pairs={{0,18},{1,27},{2,20},{3,13},{4,22},{5,31},{6,8},{7,17},{8,26},{9,3... | collective-permute-start | bytes 393224 | tf_op jit(solution)/shard_map/ppermute | solution.py:25
  37.6 5.8 %collective-permute-start.14 = (bf16[128,256]{1,0:T(8,128)(2,1)S(1)}, bf16[128,256]{1,0:T(8,128)(2,1)S(1)}, u32[]{:S(2)}, u32[]{:S(2)}) collective-permute-start(bf16[128,256]{1,0:T(8,128)(2,1)S(1)} %add_convert_fusion.2), channel_id=1, source_target_pairs={{0,8},{1,9},{2,10},{3,11},{4,12},{5,13},{6,14},{7,15},{8,0},{9,1},... | collective-permute-start | bytes 196616 | tf_op jit(solution)/shard_map/ppermute | solution.py:25
  37.8 9.0 %collective-permute-start.10 = (bf16[256,256]{1,0:T(8,128)(2,1)S(1)}, bf16[256,256]{1,0:T(8,128)(2,1)S(1)}, u32[]{:S(2)}, u32[]{:S(2)}) collective-permute-start(bf16[256,256]{1,0:T(8,128)(2,1)S(1)} %get-tuple-element.40), channel_id=1, source_target_pairs={{0,0},{1,31},{2,4},{3,9},{4,26},{5,3},{6,6},{7,13},{8,8},{9,7},{10... | collective-permute-start | bytes 393224 | tf_op jit(solution)/shard_map/ppermute | solution.py:25
  38.5 8.8 %collective-permute-start.9 = (bf16[256,256]{1,0:T(8,128)(2,1)S(1)}, bf16[256,256]{1,0:T(8,128)(2,1)S(1)}, u32[]{:S(2)}, u32[]{:S(2)}) collective-permute-start(bf16[256,256]{1,0:T(8,128)(2,1)S(1)} %get-tuple-element.39), channel_id=1, source_target_pairs={{0,16},{1,25},{2,22},{3,15},{4,20},{5,29},{6,10},{7,19},{8,24},{9,... | collective-permute-start | bytes 393224 | tf_op jit(solution)/shard_map/ppermute | solution.py:25
  41.4 7.7 %collective-permute-start.11 = (bf16[256,256]{1,0:T(8,128)(2,1)S(1)}, bf16[256,256]{1,0:T(8,128)(2,1)S(1)}, u32[]{:S(2)}, u32[]{:S(2)}) collective-permute-start(bf16[256,256]{1,0:T(8,128)(2,1)S(1)} %get-tuple-element.41), channel_id=1, source_target_pairs={{0,2},{1,29},{2,6},{3,11},{4,24},{5,1},{6,4},{7,15},{8,10},{9,5},{... | collective-permute-start | bytes 393224 | tf_op jit(solution)/shard_map/ppermute | solution.py:25
  43.5 7.1 %collective-permute-start.15 = (bf16[128,256]{1,0:T(8,128)(2,1)S(1)}, bf16[128,256]{1,0:T(8,128)(2,1)S(1)}, u32[]{:S(2)}, u32[]{:S(2)}) collective-permute-start(bf16[128,256]{1,0:T(8,128)(2,1)S(1)} %add_convert_fusion.1), channel_id=1, source_target_pairs={{0,4},{1,5},{2,6},{3,7},{4,0},{5,1},{6,2},{7,3},{8,12},{9,13},{10,... | collective-permute-start | bytes 196616 | tf_op jit(solution)/shard_map/ppermute | solution.py:25
  50.6 4.6 %collective-permute-start.16 = (bf16[128,256]{1,0:T(8,128)(2,1)S(1)}, bf16[128,256]{1,0:T(8,128)(2,1)S(1)}, u32[]{:S(2)}, u32[]{:S(2)}) collective-permute-start(bf16[128,256]{1,0:T(8,128)(2,1)S(1)} %add_convert_fusion), channel_id=1, source_target_pairs={{0,2},{1,3},{2,0},{3,1},{4,6},{5,7},{6,4},{7,5},{8,10},{9,11},{10,... | collective-permute-start | bytes 196616 | tf_op jit(solution)/shard_map/ppermute | solution.py:25
  51.2 4.2 %collective-permute-start.12 = (bf16[128,256]{1,0:T(8,128)(2,1)S(1)}, bf16[128,256]{1,0:T(8,128)(2,1)S(1)}, u32[]{:S(2)}, u32[]{:S(2)}) collective-permute-start(bf16[128,256]{1,0:T(8,128)(2,1)S(1)} %fusion.2), channel_id=1, source_target_pairs={{0,1},{1,0},{2,3},{3,2},{4,5},{5,4},{6,7},{7,6},{8,9},{9,8},{10,11... | collective-permute-start | bytes 196616 | tf_op jit(solution)/shard_map/ppermute | solution.py:25
  55.3 1.4 %collective-permute-start.17 = (bf16[2,128,256]{2,1,0:T(8,128)(2,1)S(1)}, bf16[2,128,256]{2,1,0:T(8,128)(2,1)S(1)}, u32[]{:S(2)}, u32[]{:S(2)}) collective-permute-start(bf16[2,128,256]{2,1,0:T(8,128)(2,1)S(1)} %maximum_select_fusion.2), channel_id=1, source_target_pairs={{0,1},{1,0},{2,3},{3,2},{4,5},{5,4},{6,7},{7,6},{8,9},{9,8},{10,11... | collective-permute-start | bytes 393224 | tf_op jit(solution)/shard_map/ppermute | solution.py:25
